TPU v7x, 1024 devices: a whole 4x4x32 slice. The times are simulated.
1024 devices in a mesh: blk: 256 (over y_hi, z, x), grp: 4 (over y_lo, core).
Axes of the slice: x: 4, y: 4 (y_hi: 2, y_lo: 2; y = y_hi * 2 + y_lo), z: 32, core: 2. Of those that a mesh axis runs over, the one named last changes fastest.
Arguments:
- images: bfloat16 [131072, 1152], P(('blk', 'grp')), as said below
- texts: bfloat16 [131072, 1152], P(('blk', 'grp')), as said below
- log_scale: float32 [1], replicated, may hold values from 1.6 to 2.6
- bias: float32 [1], replicated, may hold values from -3 to -1
Outputs:
- row_loss: float32 [131072], P(('blk', 'grp'))
- image_grad: float32 [131072, 1152], P(('blk', 'grp'))
- text_grad: float32 [131072, 1152], P(('blk', 'grp'))
Inputs may be any that keep to these rules, and one draw needn't show every extreme that they name: `images`: rows of image embeddings come with different norms. `texts`: rows of text embeddings come with different norms.
All inputs are finite; a program needn't handle non-finite values.
Results may differ from a plain program's by a relative error of at most 0.0054.
Values may be sent and summed in bfloat16 or wider, within the bound.
No kernel may reach another device: no remote copies, remote signals or barrier semaphores. Data moves between devices by JAX's collectives and lax.ppermute only.
A program may use at most 32 MiB of HBM per device.

v0:
```python
import jax
import jax.numpy as jnp
from jax import lax
from jax.sharding import PartitionSpec as P

STEPS = 3


def passed_along(block, axis, distance):
    devices = range(lax.axis_size(axis))
    route = [((i - distance) % len(devices), i) for i in devices]
    return lax.ppermute(block, axis, route)


def unit_rows(values):
    wide = values.astype(jnp.float32)
    inverse = lax.rsqrt(jnp.sum(wide * wide, axis=-1, keepdims=True) + 1e-06)
    return ((wide * inverse).astype(jnp.bfloat16), inverse)


def pair_tile(image_unit, text_unit, scale, offset, positive):
    logit = (
        scale
        * lax.dot_general(
            image_unit, text_unit, (((1,), (1,)), ((), ())), preferred_element_type=jnp.float32
        )
        + offset
    )
    signs = 2.0 * positive - 1.0
    term = jax.nn.softplus(-signs * logit)
    coef = (-signs * jax.nn.sigmoid(-signs * logit) * scale / STEPS).astype(jnp.bfloat16)
    return (jnp.sum(term, axis=1), coef)


def text_terms(coef, image_unit):
    return lax.dot_general(
        coef, image_unit, (((0,), (0,)), ((), ())), preferred_element_type=jnp.float32
    )


def shards(images, texts, log_scale, bias):
    scale = jnp.exp(log_scale[0])
    offset = bias[0]
    image_unit, image_inv = unit_rows(images)
    text_unit, unused = unit_rows(texts)
    rows = images.shape[0]
    width = images.shape[1]
    members = lax.axis_size("grp")
    span = rows * members
    member = lax.axis_index("grp")
    columns = lax.iota(jnp.int32, span)
    row_ids = lax.iota(jnp.int32, rows)
    diagonal = (columns[None, :] == row_ids[:, None] + member * rows).astype(jnp.float32)
    nothing = jnp.zeros((rows, span), jnp.float32)
    loss = jnp.zeros((rows,), jnp.float32)
    grad = jnp.zeros((rows, width), jnp.float32)
    block_unit = lax.all_gather(text_unit, "grp", axis=0, tiled=True)
    totals = jnp.zeros((span, width), jnp.float32)
    for step in range(STEPS):
        positive = diagonal if step == 0 else nothing
        row_terms, coef = pair_tile(image_unit, block_unit, scale, offset, positive)
        loss = loss + row_terms
        grad = grad + jnp.dot(coef, block_unit, preferred_element_type=jnp.float32)
        totals = totals + text_terms(coef, image_unit)
        if step < STEPS - 1:
            block_unit = passed_along(block_unit, "blk", 1)
            totals = passed_along(totals, "blk", 1)
    text_grad = lax.psum_scatter(totals, "grp", scatter_dimension=0, tiled=True)
    unit_wide = image_unit.astype(jnp.float32)
    along = jnp.sum(unit_wide * grad, axis=1, keepdims=True)
    image_grad = image_inv * (grad - unit_wide * along)
    row_loss = loss / (STEPS * span)
    return (row_loss, image_grad, text_grad)


def solution(mesh):
    return jax.shard_map(
        shards,
        mesh=mesh,
        in_specs=(P(("blk", "grp"), None), P(("blk", "grp"), None), P(), P()),
        out_specs=(P(("blk", "grp")), P(("blk", "grp"), None), P(("blk", "grp"), None)),
        check_vma=False,
    )
```

profile of v0, /device:TPU:1, one launch (start us, length us, event | category | flops | bytes accessed | tf_op | source)
XLA Modules:
  0.0 287.2 jit_solution(2669618484527888835)
XLA Ops:
  7.2 0.0 copy-start
  7.2 0.0 all-gather.2.cloned.1.call-start
  7.2 1.1 fusion.6
  8.4 1.8 fusion.7
  10.2 0.0 all-gather.2.cloned.1.call-update
  10.2 0.0 reduce-scatter.2.cloned.1.call-start
  11.6 0.0 copy-done
  11.6 0.1 fusion.4
  11.7 48.6 %all-gather.2.cloned.1.call-done = bf16[512,1152]{1,0:T(8,128)(2,1)} async-done(((bf16[128,1152]{1,0:T(8,128)(2,1)}), bf16[512,1152]{1,0:T(8,128)(2,1)}) %all-gather.2.cloned.1.call-update) | async-done | bytes 1179664 | tf_op jit(solution)/shard_map/all_gather | solution.py:57
  60.3 2.0 fusion.11
  62.3 0.6 fusion.15
  63.0 2.3 collective-permute-start.2
  65.3 0.0 copy-done.1
  65.3 3.1 %collective-permute-start = (bf16[512,1152]{1,0:T(8,128)(2,1)S(1)}, bf16[512,1152]{1,0:T(8,128)(2,1)S(1)}, u32[]{:S(2)}, u32[]{:S(2)}) collective-permute-start(bf16[512,1152]{1,0:T(8,128)(2,1)S(1)} %copy-done.1), channel_id=1, source_target_pairs={{1020,0},{0,4},{4,8},{8,12},{12,16},{16,20},{20,24},{24,28},{28,32... | collective-permute-start | bytes 3538952 | tf_op jit(solution)/shard_map/ppermute | solution.py:12
  68.4 81.9 %collective-permute-done = bf16[512,1152]{1,0:T(8,128)(2,1)S(1)} collective-permute-done((bf16[512,1152]{1,0:T(8,128)(2,1)S(1)}, bf16[512,1152]{1,0:T(8,128)(2,1)S(1)}, u32[]{:S(2)}, u32[]{:S(2)}) %collective-permute-start) | collective-permute-done | bytes 1179680 | tf_op jit(solution)/shard_map/ppermute | solution.py:12
  150.3 0.7 fusion.12
  151.0 0.0 collective-permute-done.2
  151.0 0.5 convolution_add_fusion
  151.6 1.9 collective-permute-start.3
  153.5 1.9 collective-permute-start.1
  155.4 81.1 %collective-permute-done.1 = bf16[512,1152]{1,0:T(8,128)(2,1)S(1)} collective-permute-done((bf16[512,1152]{1,0:T(8,128)(2,1)S(1)}, bf16[512,1152]{1,0:T(8,128)(2,1)S(1)}, u32[]{:S(2)}, u32[]{:S(2)}) %collective-permute-start.1) | collective-permute-done | bytes 1179680 | tf_op jit(solution)/shard_map/ppermute | solution.py:12
  236.5 0.7 fusion.13
  237.3 0.5 fusion.14
  237.8 0.0 collective-permute-done.3
  237.8 1.7 add.100
  239.5 0.0 reduce-scatter.2.cloned.1.call-update
  239.5 1.7 fusion.16
  241.2 0.4 convolution_add_fusion.2
  241.6 0.5 add_multiply_fusion
  242.1 0.5 fusion.8
  242.6 1.0 fusion.10
  243.6 36.8 %reduce-scatter.2.cloned.1.call-done = f32[128,1152]{1,0:T(8,128)} async-done(((f32[512,1152]{1,0:T(8,128)}), f32[128,1152]{1,0:T(8,128)}) %reduce-scatter.2.cloned.1.call-update) | async-done | bytes 589840 | tf_op jit(solution)/shard_map/reduce_scatter | solution.py:68
  (4 shorter events, 0.0 us)
Async XLA Ops:
  7.2 4.4 %copy-start = (bf16[128,1152]{1,0:T(8,128)(2,1)S(1)}, bf16[128,1152]{1,0:T(8,128)(2,1)}, u32[]{:S(2)}) copy-start(bf16[128,1152]{1,0:T(8,128)(2,1)} %param.4) | copy-start | bytes 884740
  7.2 53.1 %all-gather.2.cloned.1.call-start = ((), (), s32[]{:S(2)}) async-start(), calls=%async_computation.1 | async-start | bytes 1474560 | tf_op jit(solution)/shard_map/all_gather | solution.py:57
  10.2 270.2 %reduce-scatter.2.cloned.1.call-start = ((), (), s32[]{:S(2)}) async-start(), calls=%async_computation.2 | async-start | bytes 2949120 | tf_op jit(solution)/shard_map/reduce_scatter | solution.py:68
  62.3 2.9 %copy-start.1 = (bf16[512,1152]{1,0:T(8,128)(2,1)S(1)}, bf16[512,1152]{1,0:T(8,128)(2,1)}, u32[]{:S(2)}) copy-start(bf16[512,1152]{1,0:T(8,128)(2,1)} %all-gather.2.cloned.1.call-done) | copy-start | bytes 3538948
  63.0 88.1 %collective-permute-start.2 = (f32[512,1152]{1,0:T(8,128)S(1)}, f32[512,1152]{1,0:T(8,128)S(1)}, u32[]{:S(2)}, u32[]{:S(2)}) collective-permute-start(f32[512,1152]{1,0:T(8,128)S(1)} %fusion.15), channel_id=1, source_target_pairs={{1020,0},{0,4},{4,8},{8,12},{12,16},{16,20},{20,24},{24,28},{28,32... | collective-permute-start | bytes 7077896 | tf_op jit(solution)/shard_map/ppermute | solution.py:12
  65.3 85.0 %collective-permute-start = (bf16[512,1152]{1,0:T(8,128)(2,1)S(1)}, bf16[512,1152]{1,0:T(8,128)(2,1)S(1)}, u32[]{:S(2)}, u32[]{:S(2)}) collective-permute-start(bf16[512,1152]{1,0:T(8,128)(2,1)S(1)} %copy-done.1), channel_id=1, source_target_pairs={{1020,0},{0,4},{4,8},{8,12},{12,16},{16,20},{20,24},{24,28},{28,32... | collective-permute-start | bytes 3538952 | tf_op jit(solution)/shard_map/ppermute | solution.py:12
  151.6 86.2 %collective-permute-start.3 = (f32[512,1152]{1,0:T(8,128)S(1)}, f32[512,1152]{1,0:T(8,128)S(1)}, u32[]{:S(2)}, u32[]{:S(2)}) collective-permute-start(f32[512,1152]{1,0:T(8,128)S(1)} %convolution_add_fusion), channel_id=1, source_target_pairs={{1020,0},{0,4},{4,8},{8,12},{12,16},{16,20},{20,24},{24,28},{28,32... | collective-permute-start | bytes 7077896 | tf_op jit(solution)/shard_map/ppermute | solution.py:12
  153.5 83.0 %collective-permute-start.1 = (bf16[512,1152]{1,0:T(8,128)(2,1)S(1)}, bf16[512,1152]{1,0:T(8,128)(2,1)S(1)}, u32[]{:S(2)}, u32[]{:S(2)}) collective-permute-start(bf16[512,1152]{1,0:T(8,128)(2,1)S(1)} %collective-permute-done), channel_id=1, source_target_pairs={{1020,0},{0,4},{4,8},{8,12},{12,16},{16,20},{20,24},{24,28},{28,32... | collective-permute-start | bytes 3538952 | tf_op jit(solution)/shard_map/ppermute | solution.py:12
Sparse Core Ops, SparseCore 0:
  11.3 49.0 all-gather.1
  239.6 40.7 reduce-scatter.1
where the time goes:
time: 288 us; the launch traced here: 287 us
  waiting for transfers between devices  248 us (86%)
  between operations  15.5 us (5%)
  starting transfers between devices  9.31 us (3%)
  matrix products  7.72 us (3%)
  other arithmetic  6.3 us (2%)
    ppermute x4, waiting for transfers between devices, passed_along(): return lax.ppermute(block, axis, route)  163 us
    all_gather x1, waiting for transfers between devices, shards(): block_unit = lax.all_gather(text_unit, 'grp', axis=0, tiled=True)  48.6 us
    reduce_scatter x1, waiting for transfers between devices, shards(): text_grad = lax.psum_scatter(totals, 'grp', scatter_dimension=0, tiled=True)  36.8 us
    ppermute x4, starting transfers between devices, passed_along(): return lax.ppermute(block, axis, route)  9.23 us
  transfers between devices with their start and end apart: 6, of which 4 were waited for; matrix products, arithmetic and copies ran while one was open for 2% of the time, Pallas kernels for 0%

commit v1 on v0

v1 whole, which is shorter than its diff:
```python
import jax
import jax.numpy as jnp
from jax import lax
from jax.experimental import pallas as pl
from jax.experimental.pallas import tpu as pltpu
from jax.sharding import PartitionSpec as P

STEPS = 3
LOSS_ROWS = 16
F32 = jnp.float32
BF16 = jnp.bfloat16


def passed_along(block, distance):
    count = lax.axis_size("blk")
    return lax.ppermute(block, "blk", [(i, (i + distance) % count) for i in range(count)])


def swapped(block, flip):
    return lax.ppermute(block, "grp", [(i, i ^ flip) for i in range(lax.axis_size("grp"))])


def unit_rows(values):
    wide = values.astype(F32)
    inverse = lax.rsqrt(jnp.sum(wide * wide, axis=-1, keepdims=True) + 1e-06)
    return ((wide * inverse).astype(BF16), inverse)


def pair_terms(text_unit, image_units, log_scale, bias, positive=None):
    dots = lax.dot_general(
        text_unit, image_units, (((1,), (1,)), ((), ())), preferred_element_type=F32
    )
    scale = jnp.exp(jnp.full((1, dots.shape[1]), log_scale, F32))
    logit = scale * dots + bias
    value = logit if positive is None else jnp.where(positive, -logit, logit)
    small = jnp.exp(-jnp.abs(value))
    term = jnp.maximum(value, 0.0) + jnp.log1p(small)
    share = jnp.where(value >= 0.0, 1.0, small) / (1.0 + small)
    coef = share * (scale / STEPS)
    if positive is not None:
        coef = jnp.where(positive, -coef, coef)
    return (jnp.sum(term, axis=0, keepdims=True), coef.astype(BF16))


def by_image(coef, text_unit):
    return lax.dot_general(
        coef, text_unit, (((0,), (0,)), ((), ())), preferred_element_type=F32
    )


def coded_loss(loss, width):
    high = loss.astype(BF16)
    low = (loss - high.astype(F32)).astype(BF16)
    rows = loss.shape[1]
    half = LOSS_ROWS // 2
    parts = [jnp.broadcast_to(part.astype(F32), (half, rows)) for part in (high, low)]
    filled = jnp.concatenate([jnp.concatenate(parts, axis=0), jnp.zeros((LOSS_ROWS, width - rows), F32)], axis=1)
    return filled.astype(BF16)


def decoded_loss(tail, rows):
    wide = tail.astype(F32)
    half = LOSS_ROWS // 2
    return wide[0:1, :rows] + wide[half : half + 1, :rows]


def own_kernel(log_scale, bias, own, core, across, diagonal, texts, units, unit_out, coef_out, loss_out, text_part):
    rows = own.shape[0]
    for place, block in enumerate((own, core, across, diagonal)):
        units[place * rows : (place + 1) * rows, :] = unit_rows(block[...])[0]
    text_unit = unit_rows(texts[...])[0]
    unit_out[...] = text_unit
    everything = units[...]
    shape = (rows, everything.shape[0])
    positive = lax.broadcasted_iota(jnp.int32, shape, 0) == lax.broadcasted_iota(jnp.int32, shape, 1)
    loss, coef = pair_terms(text_unit, everything, log_scale[0], bias[0], positive)
    coef_out[...] = coef
    loss_out[...] = loss
    text_part[...] = jnp.dot(coef, everything, preferred_element_type=F32).astype(BF16)


def band_kernel(log_scale, bias, units, text_unit, coef_own, loss_own, texts_one, texts_two, to_core, kept, kept_loss, part_one, part_two):
    rows = texts_one.shape[0]
    width = texts_one.shape[1]
    everything = units[...]
    one = unit_rows(texts_one[...])[0]
    two = unit_rows(texts_two[...])[0]
    loss_one, coef_one = pair_terms(one, everything, log_scale[0], bias[0])
    loss_two, coef_two = pair_terms(two, everything, log_scale[0], bias[0])
    part_one[...] = jnp.dot(coef_one, everything, preferred_element_type=F32).astype(BF16)
    part_two[...] = jnp.dot(coef_two, everything, preferred_element_type=F32)
    loss = loss_own[...] + loss_one + loss_two
    coef_zero = coef_own[...]
    unit_zero = text_unit[...]
    for place, (home, slot) in enumerate(((kept, 0), (to_core, 0), (kept, 1), (to_core, 1))):
        part = slice(place * rows, (place + 1) * rows)
        total = by_image(coef_zero[:, part], unit_zero) + by_image(coef_one[:, part], one) + by_image(coef_two[:, part], two)
        if home is kept:
            kept[slot] = total
            kept_loss[slot : slot + 1, :] = loss[:, part]
        else:
            to_core[slot, :rows, :] = total.astype(BF16)
            to_core[slot, rows:, :] = coded_loss(loss[:, part], width)


def pair_kernel(kept, kept_loss, from_core, to_across):
    rows = kept.shape[1]
    to_across[:rows, :] = (kept[1] + from_core[1, :rows, :].astype(F32)).astype(BF16)
    loss = kept_loss[1:2, :] + decoded_loss(from_core[1, rows:, :], rows)
    to_across[rows:, :] = coded_loss(loss, kept.shape[2])


def last_kernel(images, kept, kept_loss, from_core, from_across, image_grad, row_loss):
    rows = images.shape[0]
    unit, inverse = unit_rows(images[...])
    grad = kept[0] + from_core[0, :rows, :].astype(F32) + from_across[:rows, :].astype(F32)
    wide = unit.astype(F32)
    along = jnp.sum(wide * grad, axis=1, keepdims=True)
    image_grad[...] = inverse * (grad - wide * along)
    loss = kept_loss[0:1, :] + decoded_loss(from_core[0, rows:, :], rows) + decoded_loss(from_across[rows:, :], rows)
    row_loss[...] = loss / (STEPS * 4 * rows)


def call(kernel, name, outs, arguments, scalars=0, flops=0):
    in_specs = [pl.BlockSpec(memory_space=pltpu.SMEM)] * scalars
    in_specs += [pl.BlockSpec(memory_space=pltpu.VMEM)] * (len(arguments) - scalars)
    moved = sum(a.size * a.dtype.itemsize for a in (*arguments, *outs))
    return pl.pallas_call(
        kernel,
        name=name,
        out_shape=outs,
        in_specs=in_specs,
        out_specs=tuple(pl.BlockSpec(memory_space=pltpu.VMEM) for _ in outs),
        cost_estimate=pl.CostEstimate(flops=flops, bytes_accessed=moved, transcendentals=0),
        compiler_params=pltpu.CompilerParams(vmem_limit_bytes=24 * 1024 * 1024),
    )(*arguments)


def shards(images, texts, log_scale, bias):
    rows, width = images.shape
    span = rows * lax.axis_size("grp")
    tall = rows + LOSS_ROWS
    made = jax.ShapeDtypeStruct
    across = swapped(images, 2)
    texts_one = passed_along(texts, 1)
    texts_two = passed_along(texts, 2)
    core = swapped(images, 1)
    diagonal = swapped(across, 1)
    matmul = 2 * rows * span * width
    units, text_unit, coef, loss, part_zero = call(
        own_kernel,
        "own_texts",
        (
            made((span, width), BF16),
            made((rows, width), BF16),
            made((rows, span), BF16),
            made((1, span), F32),
            made((rows, width), BF16),
        ),
        (log_scale, bias, images, core, across, diagonal, texts),
        2,
        2 * matmul,
    )
    part_zero = passed_along(part_zero, 2)
    to_core, kept, kept_loss, part_one, part_two = call(
        band_kernel,
        "band_texts",
        (
            made((2, tall, width), BF16),
            made((2, rows, width), F32),
            made((2, rows), F32),
            made((rows, width), BF16),
            made((rows, width), F32),
        ),
        (log_scale, bias, units, text_unit, coef, loss, texts_one, texts_two),
        2,
        7 * matmul,
    )
    from_core = swapped(to_core, 1)
    part_one = passed_along(part_one, 1)
    (to_across,) = call(pair_kernel, "chip_sum", (made((tall, width), BF16),), (kept, kept_loss, from_core))
    from_across = swapped(to_across, 2)
    text_grad = part_two + part_one.astype(F32) + part_zero.astype(F32)
    image_grad, row_loss = call(
        last_kernel,
        "image_grad",
        (made((rows, width), F32), made((1, rows), F32)),
        (images, kept, kept_loss, from_core, from_across),
    )
    return (row_loss.reshape(rows), image_grad, text_grad)


def solution(mesh):
    return jax.shard_map(
        shards,
        mesh=mesh,
        in_specs=(P(("blk", "grp"), None), P(("blk", "grp"), None), P(), P()),
        out_specs=(P(("blk", "grp")), P(("blk", "grp"), None), P(("blk", "grp"), None)),
        check_vma=False,
    )
```

time: 288 us -> 86.9 us (0.30)
  waiting for transfers between devices: 248 us -> 39.1 us
  starting transfers between devices: 9.31 us -> 37.5 us
  between operations: 15.5 us -> 2.06 us
  matrix products: 7.72 us -> 0 us
  other arithmetic: 6.3 us -> 0.92 us
  Pallas kernels: 0 us -> 4.86 us
    ppermute x4 -> x9, waiting for transfers between devices: 163 us -> 39.1 us  [the longest x4 34.6 us: passed_along(): lax.ppermute(block, 'blk', [(i, (i + distance) % count) for i in range(co...]
    all_gather x1 -> x0, waiting for transfers between devices: 48.6 us -> none  [shards(): block_unit = lax.all_gather(text_unit, 'grp', axis=0, tiled=True)]
    reduce_scatter x1 -> x0, waiting for transfers between devices: 36.8 us -> none  [shards(): text_grad = lax.psum_scatter(totals, 'grp', scatter_dimension=0, tiled=True)]
    ppermute x4 -> x9, starting transfers between devices: 9.23 us -> 37.5 us  [the longest x5 29.8 us: swapped(): lax.ppermute(block, 'grp', [(i, i ^ flip) for i in range(lax.axis_size('g...]
    dot_general x9 -> x0, matrix products: 7.72 us -> none  [the longest x3 3.48 us: pair_tile(): lax.dot_general(image_unit, text_unit, (((1,), (1,)), ((), ())), preferre...]
    pallas_call x0 -> x4, Pallas kernels: none -> 4.86 us  [call(): pl.pallas_call(kernel, name=name, out_shape=outs, in_specs=in_specs, out_...]
  transfers between devices with their start and end apart: 6 -> 9, of which waited for: 4 -> 5; matrix products, arithmetic and copies ran while one was open for 2% -> 1% of each run, Pallas kernels for 0% -> 2%
where the time goes in v1:
time: 86.9 us; the launch traced here: 86.4 us
  waiting for transfers between devices  39.1 us (45%)
  starting transfers between devices  37.5 us (43%)
  Pallas kernels  4.86 us (6%)
  between operations  2.06 us (2%)
  local copies, waits for them, and re-layouts  1.92 us (2%)
  other arithmetic  0.92 us (1%)
    ppermute x4, waiting for transfers between devices, passed_along(): lax.ppermute(block, 'blk', [(i, (i + distance) % count) for i in range(co...  34.6 us
    ppermute x5, starting transfers between devices, swapped(): lax.ppermute(block, 'grp', [(i, i ^ flip) for i in range(lax.axis_size('g...  29.8 us
    ppermute x4, starting transfers between devices, passed_along(): lax.ppermute(block, 'blk', [(i, (i + distance) % count) for i in range(co...  7.68 us
    pallas_call x4, Pallas kernels, call(): pl.pallas_call(kernel, name=name, out_shape=outs, in_specs=in_specs, out_...  4.86 us
    ppermute x5, waiting for transfers between devices, swapped(): lax.ppermute(block, 'grp', [(i, i ^ flip) for i in range(lax.axis_size('g...  4.53 us
    unnamed x6, local copies, waits for them, and re-layouts  1.92 us
  transfers between devices with their start and end apart: 9, of which 5 were waited for; matrix products, arithmetic and copies ran while one was open for 1% of the time, Pallas kernels for 2%

profile of v1, /device:TPU:1, one launch (start us, length us, event | category | flops | bytes accessed | tf_op | source)
XLA Modules:
  0.0 86.4 jit_solution(9609426094392988583)
XLA Ops:
  0.6 4.0 %collective-permute-start.1 = (bf16[128,1152]{1,0:T(8,128)(2,1)}, bf16[128,1152]{1,0:T(8,128)(2,1)S(1)}, u32[]{:S(2)}, u32[]{:S(2)}) collective-permute-start(bf16[128,1152]{1,0:T(8,128)(2,1)} %images.1), channel_id=1, source_target_pairs={{0,2},{1,3},{2,0},{3,1},{4,6},{5,7},{6,4},{7,5},{8,10},{9,11},{10,... | collective-permute-start | bytes 884744 | tf_op jit(solution)/shard_map/ppermute | solution.py:20
  4.7 14.0 %collective-permute-start = (bf16[128,1152]{1,0:T(8,128)(2,1)}, bf16[128,1152]{1,0:T(8,128)(2,1)S(1)}, u32[]{:S(2)}, u32[]{:S(2)}) collective-permute-start(bf16[128,1152]{1,0:T(8,128)(2,1)} %images.1), channel_id=1, source_target_pairs={{0,1},{1,0},{2,3},{3,2},{4,5},{5,4},{6,7},{7,6},{8,9},{9,8},{10,11... | collective-permute-start | bytes 884744 | tf_op jit(solution)/shard_map/ppermute | solution.py:20
  18.6 0.0 collective-permute-done.1.across
  18.6 6.9 %collective-permute-start.2 = (bf16[128,1152]{1,0:T(8,128)(2,1)S(1)}, bf16[128,1152]{1,0:T(8,128)(2,1)S(1)}, u32[]{:S(2)}, u32[]{:S(2)}) collective-permute-start(bf16[128,1152]{1,0:T(8,128)(2,1)S(1)} %collective-permute-done.1.across), channel_id=1, source_target_pairs={{0,1},{1,0},{2,3},{3,2},{4,5},{5,4},{6,7},{7,6},{8,9},{9,8},{10,11... | collective-permute-start | bytes 884744 | tf_op jit(solution)/shard_map/ppermute | solution.py:20
  25.5 1.9 %collective-permute-start.4 = (bf16[128,1152]{1,0:T(8,128)(2,1)}, bf16[128,1152]{1,0:T(8,128)(2,1)S(1)}, u32[]{:S(2)}, u32[]{:S(2)}) collective-permute-start(bf16[128,1152]{1,0:T(8,128)(2,1)} %texts.1), channel_id=1, source_target_pairs={{0,8},{4,12},{8,16},{12,20},{16,24},{20,28},{24,32},{28,36},{32,40... | collective-permute-start | bytes 884744 | tf_op jit(solution)/shard_map/ppermute | solution.py:16
  27.4 1.9 %collective-permute-start.3 = (bf16[128,1152]{1,0:T(8,128)(2,1)}, bf16[128,1152]{1,0:T(8,128)(2,1)S(1)}, u32[]{:S(2)}, u32[]{:S(2)}) collective-permute-start(bf16[128,1152]{1,0:T(8,128)(2,1)} %texts.1), channel_id=1, source_target_pairs={{0,4},{4,8},{8,12},{12,16},{16,20},{20,24},{24,28},{28,32},{32,36}... | collective-permute-start | bytes 884744 | tf_op jit(solution)/shard_map/ppermute | solution.py:16
  30.7 0.0 collective-permute-done.core
  30.7 0.0 collective-permute-done.2.diagonal
  30.7 0.0 copy-start
  30.7 1.0 %copy-done = bf16[128,1152]{1,0:T(8,128)(2,1)S(1)} copy-done((bf16[128,1152]{1,0:T(8,128)(2,1)S(1)}, bf16[128,1152]{1,0:T(8,128)(2,1)}, u32[]{:S(2)}) %copy-start) | copy-done | bytes 294936
  31.7 0.0 copy-start.2
  31.7 1.0 %copy-done.2 = bf16[128,1152]{1,0:T(8,128)(2,1)S(1)} copy-done((bf16[128,1152]{1,0:T(8,128)(2,1)S(1)}, bf16[128,1152]{1,0:T(8,128)(2,1)}, u32[]{:S(2)}) %copy-start.2) | copy-done | bytes 294936
  32.6 1.3 %own_texts.1 = (bf16[512,1152]{1,0:T(8,128)(2,1)S(1)}, bf16[128,1152]{1,0:T(8,128)(2,1)S(1)}, bf16[128,512]{1,0:T(8,128)(2,1)S(1)}, f32[1,512]{1,0:T(1,128)S(1)}, bf16[128,1152]{1,0:T(8,128)(2,1)S(1)}) custom-call(f32[1]{0:T(128)S(6)} %copy.7.log_scale, f32[1]{0:T(128)S(6)} %copy.8.bias, bf16[128,1152]{1,0:T(8,128)(2,1)S(1)} %copy-done, ...), custom_call_target="tpu_custom_call" | custom-call | flops 301989888 | bytes 3377160 | tf_op jit(solution)/shard_map/own_texts/pallas_call | solution.py:128
  33.9 12.1 %collective-permute-done.4.texts_two = bf16[128,1152]{1,0:T(8,128)(2,1)S(1)} collective-permute-done((bf16[128,1152]{1,0:T(8,128)(2,1)}, bf16[128,1152]{1,0:T(8,128)(2,1)S(1)}, u32[]{:S(2)}, u32[]{:S(2)}) %collective-permute-start.4) | collective-permute-done | bytes 294944 | tf_op jit(solution)/shard_map/ppermute | solution.py:16
  46.0 6.3 %collective-permute-done.3.texts_one = bf16[128,1152]{1,0:T(8,128)(2,1)S(1)} collective-permute-done((bf16[128,1152]{1,0:T(8,128)(2,1)}, bf16[128,1152]{1,0:T(8,128)(2,1)S(1)}, u32[]{:S(2)}, u32[]{:S(2)}) %collective-permute-start.3) | collective-permute-done | bytes 294944 | tf_op jit(solution)/shard_map/ppermute | solution.py:16
  52.2 2.4 %band_texts.1 = (bf16[2,144,1152]{2,1,0:T(8,128)(2,1)S(1)}, f32[2,128,1152]{2,1,0:T(8,128)S(1)}, f32[2,128]{1,0:T(2,128)S(1)}, bf16[128,1152]{1,0:T(8,128)(2,1)S(1)}, f32[128,1152]{1,0:T(8,128)S(1)}) custom-call(f32[1]{0:T(128)S(6)} %copy.7.log_scale, f32[1]{0:T(128)S(6)} %copy.8.bias, bf16[512,1152]{1,0:T(8,128)(2,1)S(1)} %get-tuple-element.15.units, ...), custom_call_target="tpu_custom_call" | custom-call | flops 1056964608 | bytes 4926472 | tf_op jit(solution)/shard_map/band_texts/pallas_call | solution.py:128
  54.6 2.6 %collective-permute-start.5 = (bf16[2,144,1152]{2,1,0:T(8,128)(2,1)S(1)}, bf16[2,144,1152]{2,1,0:T(8,128)(2,1)S(1)}, u32[]{:S(2)}, u32[]{:S(2)}) collective-permute-start(bf16[2,144,1152]{2,1,0:T(8,128)(2,1)S(1)} %get-tuple-element.21), channel_id=1, source_target_pairs={{0,1},{1,0},{2,3},{3,2},{4,5},{5,4},{6,7},{7,6},{8,9},{9,8},{10,11... | collective-permute-start | bytes 1990664 | tf_op jit(solution)/shard_map/ppermute | solution.py:20
  57.2 1.9 %collective-permute-start.8 = (bf16[128,1152]{1,0:T(8,128)(2,1)S(1)}, bf16[128,1152]{1,0:T(8,128)(2,1)S(1)}, u32[]{:S(2)}, u32[]{:S(2)}) collective-permute-start(bf16[128,1152]{1,0:T(8,128)(2,1)S(1)} %get-tuple-element.26), channel_id=1, source_target_pairs={{0,8},{4,12},{8,16},{12,20},{16,24},{20,28},{24,32},{28,36},{32,40... | collective-permute-start | bytes 884744 | tf_op jit(solution)/shard_map/ppermute | solution.py:16
  59.1 1.9 %collective-permute-start.7 = (bf16[128,1152]{1,0:T(8,128)(2,1)S(1)}, bf16[128,1152]{1,0:T(8,128)(2,1)S(1)}, u32[]{:S(2)}, u32[]{:S(2)}) collective-permute-start(bf16[128,1152]{1,0:T(8,128)(2,1)S(1)} %get-tuple-element.25), channel_id=1, source_target_pairs={{0,4},{4,8},{8,12},{12,16},{16,20},{20,24},{24,28},{28,32},{32,36}... | collective-permute-start | bytes 884744 | tf_op jit(solution)/shard_map/ppermute | solution.py:16
  61.0 0.0 collective-permute-done.5.from_core
  61.0 0.1 chip_sum.1
  61.1 0.0 copy-start.1
  61.1 2.4 %collective-permute-start.6 = (bf16[144,1152]{1,0:T(8,128)(2,1)S(1)}, bf16[144,1152]{1,0:T(8,128)(2,1)S(1)}, u32[]{:S(2)}, u32[]{:S(2)}) collective-permute-start(bf16[144,1152]{1,0:T(8,128)(2,1)S(1)} %chip_sum.1), channel_id=1, source_target_pairs={{0,2},{1,3},{2,0},{3,1},{4,6},{5,7},{6,4},{7,5},{8,10},{9,11},{10,... | collective-permute-start | bytes 995336 | tf_op jit(solution)/shard_map/ppermute | solution.py:20
  63.6 14.5 %collective-permute-done.8 = bf16[128,1152]{1,0:T(8,128)(2,1)S(1)} collective-permute-done((bf16[128,1152]{1,0:T(8,128)(2,1)S(1)}, bf16[128,1152]{1,0:T(8,128)(2,1)S(1)}, u32[]{:S(2)}, u32[]{:S(2)}) %collective-permute-start.8) | collective-permute-done | bytes 294944 | tf_op jit(solution)/shard_map/ppermute | solution.py:16
  78.1 1.7 %collective-permute-done.7 = bf16[128,1152]{1,0:T(8,128)(2,1)S(1)} collective-permute-done((bf16[128,1152]{1,0:T(8,128)(2,1)S(1)}, bf16[128,1152]{1,0:T(8,128)(2,1)S(1)}, u32[]{:S(2)}, u32[]{:S(2)}) %collective-permute-start.7) | collective-permute-done | bytes 294944 | tf_op jit(solution)/shard_map/ppermute | solution.py:16
  79.8 0.9 %convert_add_fusion = f32[128,1152]{1,0:T(8,128)} fusion(bf16[128,1152]{1,0:T(8,128)(2,1)S(1)} %collective-permute-done.8, f32[128,1152]{1,0:T(8,128)S(1)} %get-tuple-element.24, bf16[128,1152]{1,0:T(8,128)(2,1)S(1)} %collective-permute-done.7), kind=kLoop, calls=%fused_computation | loop fusion | flops 589824 | bytes 1769472 | tf_op jit(solution)/shard_map/add | solution.py:183
  80.7 4.5 %collective-permute-done.6.from_across = bf16[144,1152]{1,0:T(8,128)(2,1)S(1)} collective-permute-done((bf16[144,1152]{1,0:T(8,128)(2,1)S(1)}, bf16[144,1152]{1,0:T(8,128)(2,1)S(1)}, u32[]{:S(2)}, u32[]{:S(2)}) %collective-permute-start.6) | collective-permute-done | bytes 331808 | tf_op jit(solution)/shard_map/ppermute | solution.py:20
  85.3 0.0 copy-done.1
  85.3 1.1 %image_grad.1 = (f32[128,1152]{1,0:T(8,128)}, f32[1,128]{1,0:T(1,128)}) custom-call(bf16[128,1152]{1,0:T(8,128)(2,1)S(1)} %copy-done.1, f32[2,128,1152]{2,1,0:T(8,128)S(1)} %get-tuple-element.19.kept, f32[2,128]{1,0:T(2,128)S(1)} %get-tuple-element.20.kept_loss, bf16[2,144,1152]{2,1,0:T(8,128)(2,1)S(1)} %collective-permute-done.5.from_core, ...), custom_call_target="tpu_custom_call" | custom-call | bytes 3061248 | tf_op jit(solution)/shard_map/image_grad/pallas_call | solution.py:128
Async XLA Ops:
  0.6 18.0 %collective-permute-start.1 = (bf16[128,1152]{1,0:T(8,128)(2,1)}, bf16[128,1152]{1,0:T(8,128)(2,1)S(1)}, u32[]{:S(2)}, u32[]{:S(2)}) collective-permute-start(bf16[128,1152]{1,0:T(8,128)(2,1)} %images.1), channel_id=1, source_target_pairs={{0,2},{1,3},{2,0},{3,1},{4,6},{5,7},{6,4},{7,5},{8,10},{9,11},{10,... | collective-permute-start | bytes 884744 | tf_op jit(solution)/shard_map/ppermute | solution.py:20
  4.7 26.0 %collective-permute-start = (bf16[128,1152]{1,0:T(8,128)(2,1)}, bf16[128,1152]{1,0:T(8,128)(2,1)S(1)}, u32[]{:S(2)}, u32[]{:S(2)}) collective-permute-start(bf16[128,1152]{1,0:T(8,128)(2,1)} %images.1), channel_id=1, source_target_pairs={{0,1},{1,0},{2,3},{3,2},{4,5},{5,4},{6,7},{7,6},{8,9},{9,8},{10,11... | collective-permute-start | bytes 884744 | tf_op jit(solution)/shard_map/ppermute | solution.py:20
  18.6 12.0 %collective-permute-start.2 = (bf16[128,1152]{1,0:T(8,128)(2,1)S(1)}, bf16[128,1152]{1,0:T(8,128)(2,1)S(1)}, u32[]{:S(2)}, u32[]{:S(2)}) collective-permute-start(bf16[128,1152]{1,0:T(8,128)(2,1)S(1)} %collective-permute-done.1.across), channel_id=1, source_target_pairs={{0,1},{1,0},{2,3},{3,2},{4,5},{5,4},{6,7},{7,6},{8,9},{9,8},{10,11... | collective-permute-start | bytes 884744 | tf_op jit(solution)/shard_map/ppermute | solution.py:20
  25.5 20.4 %collective-permute-start.4 = (bf16[128,1152]{1,0:T(8,128)(2,1)}, bf16[128,1152]{1,0:T(8,128)(2,1)S(1)}, u32[]{:S(2)}, u32[]{:S(2)}) collective-permute-start(bf16[128,1152]{1,0:T(8,128)(2,1)} %texts.1), channel_id=1, source_target_pairs={{0,8},{4,12},{8,16},{12,20},{16,24},{20,28},{24,32},{28,36},{32,40... | collective-permute-start | bytes 884744 | tf_op jit(solution)/shard_map/ppermute | solution.py:16
  27.4 24.8 %collective-permute-start.3 = (bf16[128,1152]{1,0:T(8,128)(2,1)}, bf16[128,1152]{1,0:T(8,128)(2,1)S(1)}, u32[]{:S(2)}, u32[]{:S(2)}) collective-permute-start(bf16[128,1152]{1,0:T(8,128)(2,1)} %texts.1), channel_id=1, source_target_pairs={{0,4},{4,8},{8,12},{12,16},{16,20},{20,24},{24,28},{28,32},{32,36}... | collective-permute-start | bytes 884744 | tf_op jit(solution)/shard_map/ppermute | solution.py:16
  30.7 1.0 %copy-start = (bf16[128,1152]{1,0:T(8,128)(2,1)S(1)}, bf16[128,1152]{1,0:T(8,128)(2,1)}, u32[]{:S(2)}) copy-start(bf16[128,1152]{1,0:T(8,128)(2,1)} %images.1) | copy-start | bytes 884740
  31.7 1.0 %copy-start.2 = (bf16[128,1152]{1,0:T(8,128)(2,1)S(1)}, bf16[128,1152]{1,0:T(8,128)(2,1)}, u32[]{:S(2)}) copy-start(bf16[128,1152]{1,0:T(8,128)(2,1)} %texts.1) | copy-start | bytes 884740
  54.6 6.4 %collective-permute-start.5 = (bf16[2,144,1152]{2,1,0:T(8,128)(2,1)S(1)}, bf16[2,144,1152]{2,1,0:T(8,128)(2,1)S(1)}, u32[]{:S(2)}, u32[]{:S(2)}) collective-permute-start(bf16[2,144,1152]{2,1,0:T(8,128)(2,1)S(1)} %get-tuple-element.21), channel_id=1, source_target_pairs={{0,1},{1,0},{2,3},{3,2},{4,5},{5,4},{6,7},{7,6},{8,9},{9,8},{10,11... | collective-permute-start | bytes 1990664 | tf_op jit(solution)/shard_map/ppermute | solution.py:20
  57.2 20.9 %collective-permute-start.8 = (bf16[128,1152]{1,0:T(8,128)(2,1)S(1)}, bf16[128,1152]{1,0:T(8,128)(2,1)S(1)}, u32[]{:S(2)}, u32[]{:S(2)}) collective-permute-start(bf16[128,1152]{1,0:T(8,128)(2,1)S(1)} %get-tuple-element.26), channel_id=1, source_target_pairs={{0,8},{4,12},{8,16},{12,20},{16,24},{20,28},{24,32},{28,36},{32,40... | collective-permute-start | bytes 884744 | tf_op jit(solution)/shard_map/ppermute | solution.py:16
  59.1 20.7 %collective-permute-start.7 = (bf16[128,1152]{1,0:T(8,128)(2,1)S(1)}, bf16[128,1152]{1,0:T(8,128)(2,1)S(1)}, u32[]{:S(2)}, u32[]{:S(2)}) collective-permute-start(bf16[128,1152]{1,0:T(8,128)(2,1)S(1)} %get-tuple-element.25), channel_id=1, source_target_pairs={{0,4},{4,8},{8,12},{12,16},{16,20},{20,24},{24,28},{28,32},{32,36}... | collective-permute-start | bytes 884744 | tf_op jit(solution)/shard_map/ppermute | solution.py:16
  61.1 24.2 %copy-start.1 = (bf16[128,1152]{1,0:T(8,128)(2,1)S(1)}, bf16[128,1152]{1,0:T(8,128)(2,1)}, u32[]{:S(2)}) copy-start(bf16[128,1152]{1,0:T(8,128)(2,1)} %images.1) | copy-start | bytes 884740
  61.1 24.1 %collective-permute-start.6 = (bf16[144,1152]{1,0:T(8,128)(2,1)S(1)}, bf16[144,1152]{1,0:T(8,128)(2,1)S(1)}, u32[]{:S(2)}, u32[]{:S(2)}) collective-permute-start(bf16[144,1152]{1,0:T(8,128)(2,1)S(1)} %chip_sum.1), channel_id=1, source_target_pairs={{0,2},{1,3},{2,0},{3,1},{4,6},{5,7},{6,4},{7,5},{8,10},{9,11},{10,... | collective-permute-start | bytes 995336 | tf_op jit(solution)/shard_map/ppermute | solution.py:20

commit v2 on v1

v2 whole, which is shorter than its diff:
```python
import jax
import jax.numpy as jnp
from jax import lax
from jax.experimental import pallas as pl
from jax.experimental.pallas import tpu as pltpu
from jax.sharding import PartitionSpec as P

STEPS = 3
LOSS_ROWS = 16
F32 = jnp.float32
BF16 = jnp.bfloat16


def passed_along(block, flips):
    groups = lax.axis_size("blk")
    members = lax.axis_size("grp")
    route = []
    for group in range(groups):
        flip = 2 if group % (groups // 2) in flips else 0
        for member in range(members):
            target = (group + 1) % groups * members + (member ^ flip)
            route.append((group * members + member, target))
    return lax.ppermute(block, ("blk", "grp"), route)


def passed_two(block):
    groups = lax.axis_size("blk")
    return lax.ppermute(block, "blk", [(i, (i + 2) % groups) for i in range(groups)])


def swapped(block, flip):
    return lax.ppermute(block, "grp", [(i, i ^ flip) for i in range(lax.axis_size("grp"))])


def unit_rows(values):
    wide = values.astype(F32)
    inverse = lax.rsqrt(jnp.sum(wide * wide, axis=-1, keepdims=True) + 1e-06)
    return ((wide * inverse).astype(BF16), inverse)


def pair_terms(text_unit, image_units, scale, bias, positive=None):
    dots = lax.dot_general(
        text_unit, image_units, (((1,), (1,)), ((), ())), preferred_element_type=F32
    )
    logit = scale * dots + bias
    value = logit if positive is None else jnp.where(positive, -logit, logit)
    small = jnp.exp(-jnp.abs(value))
    term = jnp.maximum(value, 0.0) + jnp.log1p(small)
    share = jnp.where(value >= 0.0, 1.0, small) / (1.0 + small)
    coef = share * (scale / STEPS)
    if positive is not None:
        coef = jnp.where(positive, -coef, coef)
    return (jnp.sum(term, axis=0, keepdims=True), coef.astype(BF16))


def by_image(coef, text_unit):
    return lax.dot_general(
        coef, text_unit, (((0,), (0,)), ((), ())), preferred_element_type=F32
    )


def coded_loss(loss, width):
    high = loss.astype(BF16)
    low = (loss - high.astype(F32)).astype(BF16)
    rows = loss.shape[1]
    half = LOSS_ROWS // 2
    parts = [jnp.broadcast_to(part.astype(F32), (half, rows)) for part in (high, low)]
    filled = jnp.concatenate([jnp.concatenate(parts, axis=0), jnp.zeros((LOSS_ROWS, width - rows), F32)], axis=1)
    return filled.astype(BF16)


def decoded_loss(tail, rows):
    wide = tail.astype(F32)
    half = LOSS_ROWS // 2
    return wide[0:1, :rows] + wide[half : half + 1, :rows]


def own_kernel(log_scale, bias, images, texts, image_unit, text_unit, knobs, inverses):
    unit, inverse = unit_rows(images[...])
    image_unit[...] = unit
    inverses[...] = jnp.broadcast_to(inverse, inverses.shape)
    text_unit[...] = unit_rows(texts[...])[0]
    span = knobs.shape[1]
    knobs[0:1, :] = jnp.exp(jnp.full((1, span), log_scale[0], F32))
    knobs[1:2, :] = jnp.full((1, span), bias[0], F32)


def near_kernel(knobs, image_unit, text_unit, core, across, diagonal, texts_one, units, text_units, coefs, losses, part_zero, part_one):
    rows = image_unit.shape[0]
    units[:rows, :] = image_unit[...]
    for place, block in ((1, core), (2, across), (3, diagonal)):
        units[place * rows : (place + 1) * rows, :] = unit_rows(block[...])[0]
    scale, offset = knobs[0:1, :], knobs[1:2, :]
    everything = units[...]
    shape = (rows, everything.shape[0])
    positive = lax.broadcasted_iota(jnp.int32, shape, 0) == lax.broadcasted_iota(jnp.int32, shape, 1)
    total = None
    for step, part in enumerate((part_zero, part_one)):
        unit = text_unit[...] if step == 0 else unit_rows(texts_one[...])[0]
        loss, coef = pair_terms(unit, everything, scale, offset, positive if step == 0 else None)
        text_units[step * rows : (step + 1) * rows, :] = unit
        coefs[step * rows : (step + 1) * rows, :] = coef
        part[...] = jnp.dot(coef, everything, preferred_element_type=F32).astype(BF16)
        total = loss if total is None else total + loss
    losses[...] = total


def image_part(coefs, text_units, coef_two, unit_two, place):
    rows = unit_two.shape[0]
    part = slice(place * rows, (place + 1) * rows)
    return by_image(coefs[:, part], text_units[...]) + by_image(coef_two[:, part], unit_two)


def far_kernel(knobs, units, text_units, coefs, losses, texts_two, coef_out, unit_out, loss_out, to_core_top, to_core_low):
    rows, width = texts_two.shape
    unit_two = unit_rows(texts_two[...])[0]
    loss, coef = pair_terms(unit_two, units[...], knobs[0:1, :], knobs[1:2, :])
    unit_out[...] = unit_two
    coef_out[...] = coef
    loss = losses[...] + loss
    loss_out[...] = loss
    part = image_part(coefs, text_units, coef, unit_two, 3).astype(BF16)
    half = rows // 2
    to_core_top[...] = part[:half]
    to_core_low[:half, :] = part[half:]
    to_core_low[half : half + LOSS_ROWS, :] = coded_loss(loss[:, 3 * rows :], width)
    to_core_low[half + LOSS_ROWS :, :] = coded_loss(loss[:, rows : 2 * rows], width)


def rest_kernel(units, text_units, coefs, unit_two, coef_two, to_core, kept, part_two):
    unit = unit_two[...]
    coef = coef_two[...]
    kept[1] = image_part(coefs, text_units, coef, unit, 2)
    kept[0] = image_part(coefs, text_units, coef, unit, 0)
    to_core[...] = image_part(coefs, text_units, coef, unit, 1).astype(BF16)
    part_two[...] = jnp.dot(coef, units[...], preferred_element_type=F32)


def pair_kernel(kept, losses, from_top, from_low, to_across):
    rows = kept.shape[1]
    half = rows // 2
    to_across[:half, :] = (kept[1, :half] + from_top[...].astype(F32)).astype(BF16)
    to_across[half:rows, :] = (kept[1, half:] + from_low[:half, :].astype(F32)).astype(BF16)
    loss = losses[:, 2 * rows : 3 * rows] + decoded_loss(from_low[half : half + LOSS_ROWS, :], rows)
    to_across[rows:, :] = coded_loss(loss, kept.shape[2])


def last_kernel(units, inverses, kept, losses, from_core, from_low, from_across, image_grad, row_loss):
    rows = image_grad.shape[0]
    grad = kept[0] + from_core[...].astype(F32) + from_across[:rows, :].astype(F32)
    wide = units[:rows, :].astype(F32)
    along = jnp.sum(wide * grad, axis=1, keepdims=True)
    image_grad[...] = inverses[:, 0:1] * (grad - wide * along)
    loss = losses[:, :rows] + decoded_loss(from_low[rows // 2 + LOSS_ROWS :, :], rows) + decoded_loss(from_across[rows:, :], rows)
    row_loss[...] = loss / (STEPS * 4 * rows)


def text_kernel(part_two, part_one, part_zero, text_grad):
    text_grad[...] = part_two[...] + part_one[...].astype(F32) + part_zero[...].astype(F32)


def call(kernel, name, outs, arguments, scalars=0, flops=0):
    in_specs = [pl.BlockSpec(memory_space=pltpu.SMEM)] * scalars
    in_specs += [pl.BlockSpec(memory_space=pltpu.VMEM)] * (len(arguments) - scalars)
    moved = sum(a.size * a.dtype.itemsize for a in (*arguments, *outs))
    return pl.pallas_call(
        kernel,
        name=name,
        out_shape=outs,
        in_specs=in_specs,
        out_specs=tuple(pl.BlockSpec(memory_space=pltpu.VMEM) for _ in outs),
        cost_estimate=pl.CostEstimate(flops=flops, bytes_accessed=moved, transcendentals=0),
        compiler_params=pltpu.CompilerParams(vmem_limit_bytes=24 * 1024 * 1024),
    )(*arguments)


def shards(images, texts, log_scale, bias):
    rows, width = images.shape
    span = rows * lax.axis_size("grp")
    tall = rows + LOSS_ROWS
    half = lax.axis_size("blk") // 2
    first_flips = (half - 2, half - 1)
    second_flips = (half - 1, 0)
    made = jax.ShapeDtypeStruct
    texts_one = passed_along(texts, first_flips)
    across = swapped(images, 2)
    core = swapped(images, 1)
    texts_two = passed_along(texts_one, second_flips)
    diagonal = swapped(across, 1)
    matmul = 2 * rows * span * width
    image_unit, text_unit, knobs, inverses = call(
        own_kernel,
        "own_units",
        (made((rows, width), BF16), made((rows, width), BF16), made((2, span), F32), made((rows, 128), F32)),
        (log_scale, bias, images, texts),
        2,
    )
    units, text_units, coefs, losses, part_zero, part_one = call(
        near_kernel,
        "near_texts",
        (
            made((span, width), BF16),
            made((2 * rows, width), BF16),
            made((2 * rows, span), BF16),
            made((1, span), F32),
            made((rows, width), BF16),
            made((rows, width), BF16),
        ),
        (knobs, image_unit, text_unit, core, across, diagonal, texts_one),
        0,
        4 * matmul,
    )
    part_zero = passed_two(part_zero)
    part_one = passed_along(part_one, second_flips)
    coef_two, unit_two, losses, to_core_top, to_core_low = call(
        far_kernel,
        "far_texts",
        (
            made((rows, span), BF16),
            made((rows, width), BF16),
            made((1, span), F32),
            made((rows // 2, width), BF16),
            made((rows // 2 + 2 * LOSS_ROWS, width), BF16),
        ),
        (knobs, units, text_units, coefs, losses, texts_two),
        0,
        2 * matmul,
    )
    from_core_top = swapped(to_core_top, 1)
    from_core_low = swapped(to_core_low, 1)
    to_core_near, kept, part_two = call(
        rest_kernel,
        "image_parts",
        (made((rows, width), BF16), made((2, rows, width), F32), made((rows, width), F32)),
        (units, text_units, coefs, unit_two, coef_two),
    )
    (to_across,) = call(pair_kernel, "chip_sum", (made((tall, width), BF16),), (kept, losses, from_core_top, from_core_low))
    to_across, to_core_near = lax.optimization_barrier((to_across, to_core_near))
    from_across = swapped(to_across, 2)
    from_core_near = swapped(to_core_near, 1)
    (text_grad,) = call(text_kernel, "text_sum", (made((rows, width), F32),), (part_two, part_one, part_zero), 0, 100 * matmul)
    image_grad, row_loss = call(
        last_kernel,
        "image_grad",
        (made((rows, width), F32), made((1, rows), F32)),
        (units, inverses, kept, losses, from_core_near, from_core_low, from_across),
    )
    return (row_loss.reshape(rows), image_grad, text_grad)


def solution(mesh):
    return jax.shard_map(
        shards,
        mesh=mesh,
        in_specs=(P(("blk", "grp"), None), P(("blk", "grp"), None), P(), P()),
        out_specs=(P(("blk", "grp")), P(("blk", "grp"), None), P(("blk", "grp"), None)),
        check_vma=False,
    )
```

time: 86.9 us -> 73.1 us (0.84)
  waiting for transfers between devices: 39.1 us -> 23.5 us
  starting transfers between devices: 37.5 us -> 39 us
  Pallas kernels: 4.86 us -> 6.2 us
  other arithmetic: 0.92 us -> 0 us
    ppermute x4, waiting for transfers between devices: 34.6 us -> 17.4 us  [the longest x3 14.9 us: passed_along(): return lax.ppermute(block, ('blk', 'grp'), route)]
    ppermute x5 -> x7, waiting for transfers between devices: 4.53 us -> 6.09 us  [swapped(): lax.ppermute(block, 'grp', [(i, i ^ flip) for i in range(lax.axis_size('g...]
    pallas_call x4 -> x7, Pallas kernels: 4.86 us -> 6.2 us  [call(): pl.pallas_call(kernel, name=name, out_shape=outs, in_specs=in_specs, out_...]
    ppermute x4, starting transfers between devices: 7.68 us -> 8.87 us  [the longest x3 6.95 us: passed_along(): return lax.ppermute(block, ('blk', 'grp'), route)]
    add x1 -> x0, other arithmetic: 0.92 us -> none  [shards(): text_grad = part_two + part_one.astype(F32) + part_zero.astype(F32)]
    ppermute x5 -> x7, starting transfers between devices: 29.8 us -> 30.1 us  [swapped(): lax.ppermute(block, 'grp', [(i, i ^ flip) for i in range(lax.axis_size('g...]
    unnamed x6 -> x4, local copies, waits for them, and re-layouts: 1.92 us -> 1.92 us
  transfers between devices with their start and end apart: 9 -> 11, of which waited for: 5 -> 5; matrix products, arithmetic and copies ran while one was open for 1% -> 0% of each run, Pallas kernels for 2% -> 7%
where the time goes in v2:
time: 73.1 us; the launch traced here: 72.6 us
  starting transfers between devices  39 us (53%)
  waiting for transfers between devices  23.5 us (32%)
  Pallas kernels  6.2 us (8%)
  between operations  2.08 us (3%)
  local copies, waits for them, and re-layouts  1.92 us (3%)
    ppermute x7, starting transfers between devices, swapped(): lax.ppermute(block, 'grp', [(i, i ^ flip) for i in range(lax.axis_size('g...  30.1 us
    ppermute x3, waiting for transfers between devices, passed_along(): return lax.ppermute(block, ('blk', 'grp'), route)  14.9 us
    ppermute x3, starting transfers between devices, passed_along(): return lax.ppermute(block, ('blk', 'grp'), route)  6.95 us
    pallas_call x7, Pallas kernels, call(): pl.pallas_call(kernel, name=name, out_shape=outs, in_specs=in_specs, out_...  6.2 us
    ppermute x7, waiting for transfers between devices, swapped(): lax.ppermute(block, 'grp', [(i, i ^ flip) for i in range(lax.axis_size('g...  6.09 us
    ppermute x1, waiting for transfers between devices, passed_two(): lax.ppermute(block, 'blk', [(i, (i + 2) % groups) for i in range(groups)])  2.43 us
    ppermute x1, starting transfers between devices, passed_two(): lax.ppermute(block, 'blk', [(i, (i + 2) % groups) for i in range(groups)])  1.92 us
    unnamed x4, local copies, waits for them, and re-layouts  1.92 us
  transfers between devices with their start and end apart: 11, of which 5 were waited for; matrix products, arithmetic and copies ran while one was open for 0% of the time, Pallas kernels for 7%

profile of v2, /device:TPU:1, one launch (start us, length us, event | category | flops | bytes accessed | tf_op | source)
XLA Modules:
  0.0 72.6 jit_solution(6340709935085114171)
XLA Ops:
  0.6 4.0 %collective-permute-start.1 = (bf16[128,1152]{1,0:T(8,128)(2,1)}, bf16[128,1152]{1,0:T(8,128)(2,1)S(1)}, u32[]{:S(2)}, u32[]{:S(2)}) collective-permute-start(bf16[128,1152]{1,0:T(8,128)(2,1)} %images.1), channel_id=1, source_target_pairs={{0,2},{1,3},{2,0},{3,1},{4,6},{5,7},{6,4},{7,5},{8,10},{9,11},{10,... | collective-permute-start | bytes 884744 | tf_op jit(solution)/shard_map/ppermute | solution.py:32
  4.7 3.1 %collective-permute-start.3 = (bf16[128,1152]{1,0:T(8,128)(2,1)}, bf16[128,1152]{1,0:T(8,128)(2,1)S(1)}, u32[]{:S(2)}, u32[]{:S(2)}) collective-permute-start(bf16[128,1152]{1,0:T(8,128)(2,1)} %texts.1), channel_id=1, source_target_pairs={{0,4},{1,5},{2,6},{3,7},{4,8},{5,9},{6,10},{7,11},{8,12},{9,13},{1... | collective-permute-start | bytes 884744 | tf_op jit(solution)/shard_map/ppermute | solution.py:23
  7.8 12.7 %collective-permute-start = (bf16[128,1152]{1,0:T(8,128)(2,1)}, bf16[128,1152]{1,0:T(8,128)(2,1)S(1)}, u32[]{:S(2)}, u32[]{:S(2)}) collective-permute-start(bf16[128,1152]{1,0:T(8,128)(2,1)} %images.1), channel_id=1, source_target_pairs={{0,1},{1,0},{2,3},{3,2},{4,5},{5,4},{6,7},{7,6},{8,9},{9,8},{10,11... | collective-permute-start | bytes 884744 | tf_op jit(solution)/shard_map/ppermute | solution.py:32
  20.6 0.0 collective-permute-done.1.across
  20.6 4.9 %collective-permute-start.2 = (bf16[128,1152]{1,0:T(8,128)(2,1)S(1)}, bf16[128,1152]{1,0:T(8,128)(2,1)S(1)}, u32[]{:S(2)}, u32[]{:S(2)}) collective-permute-start(bf16[128,1152]{1,0:T(8,128)(2,1)S(1)} %collective-permute-done.1.across), channel_id=1, source_target_pairs={{0,1},{1,0},{2,3},{3,2},{4,5},{5,4},{6,7},{7,6},{8,9},{9,8},{10,11... | collective-permute-start | bytes 884744 | tf_op jit(solution)/shard_map/ppermute | solution.py:32
  25.5 8.0 %collective-permute-done.3.texts_one = bf16[128,1152]{1,0:T(8,128)(2,1)S(1)} collective-permute-done((bf16[128,1152]{1,0:T(8,128)(2,1)}, bf16[128,1152]{1,0:T(8,128)(2,1)S(1)}, u32[]{:S(2)}, u32[]{:S(2)}) %collective-permute-start.3) | collective-permute-done | bytes 294944 | tf_op jit(solution)/shard_map/ppermute | solution.py:23
  33.5 1.9 %collective-permute-start.4 = (bf16[128,1152]{1,0:T(8,128)(2,1)S(1)}, bf16[128,1152]{1,0:T(8,128)(2,1)S(1)}, u32[]{:S(2)}, u32[]{:S(2)}) collective-permute-start(bf16[128,1152]{1,0:T(8,128)(2,1)S(1)} %collective-permute-done.3.texts_one), channel_id=1, source_target_pairs={{0,6},{1,7},{2,4},{3,5},{4,8},{5,9},{6,10},{7,11},{8,12},{9,13},{1... | collective-permute-start | bytes 884744 | tf_op jit(solution)/shard_map/ppermute | solution.py:23
  36.7 0.0 copy-start
  36.7 1.0 %copy-done = bf16[128,1152]{1,0:T(8,128)(2,1)S(1)} copy-done((bf16[128,1152]{1,0:T(8,128)(2,1)S(1)}, bf16[128,1152]{1,0:T(8,128)(2,1)}, u32[]{:S(2)}) %copy-start) | copy-done | bytes 294936
  37.7 1.0 %copy-done.1 = bf16[128,1152]{1,0:T(8,128)(2,1)S(1)} copy-done((bf16[128,1152]{1,0:T(8,128)(2,1)S(1)}, bf16[128,1152]{1,0:T(8,128)(2,1)}, u32[]{:S(2)}) %copy-start.1) | copy-done | bytes 294936
  38.6 0.2 own_units.1
  38.8 0.0 collective-permute-done.core
  38.8 0.0 collective-permute-done.2.diagonal
  38.9 1.9 %near_texts.1 = (bf16[512,1152]{1,0:T(8,128)(2,1)S(1)}, bf16[256,1152]{1,0:T(8,128)(2,1)S(1)}, bf16[256,512]{1,0:T(8,128)(2,1)S(1)}, f32[1,512]{1,0:T(1,128)S(1)...) custom-call(f32[2,512]{1,0:T(2,128)S(1)} %get-tuple-element.25.knobs, ...), custom_call_target="tpu_custom_call" | custom-call | flops 603979776 | bytes 4397056 | tf_op jit(solution)/shard_map/near_texts/pallas_call | solution.py:166
  40.8 1.9 %collective-permute-start.9 = (bf16[128,1152]{1,0:T(8,128)(2,1)S(1)}, bf16[128,1152]{1,0:T(8,128)(2,1)S(1)}, u32[]{:S(2)}, u32[]{:S(2)}) collective-permute-start(bf16[128,1152]{1,0:T(8,128)(2,1)S(1)} %get-tuple-element.45), channel_id=1, source_target_pairs={{0,6},{1,7},{2,4},{3,5},{4,8},{5,9},{6,10},{7,11},{8,12},{9,13},{1... | collective-permute-start | bytes 884744 | tf_op jit(solution)/shard_map/ppermute | solution.py:23
  42.7 1.9 %collective-permute-start.10 = (bf16[128,1152]{1,0:T(8,128)(2,1)S(1)}, bf16[128,1152]{1,0:T(8,128)(2,1)S(1)}, u32[]{:S(2)}, u32[]{:S(2)}) collective-permute-start(bf16[128,1152]{1,0:T(8,128)(2,1)S(1)} %get-tuple-element.46), channel_id=1, source_target_pairs={{0,8},{4,12},{8,16},{12,20},{16,24},{20,28},{24,32},{28,36},{32,40... | collective-permute-start | bytes 884744 | tf_op jit(solution)/shard_map/ppermute | solution.py:28
  44.7 7.0 %collective-permute-done.4.texts_two = bf16[128,1152]{1,0:T(8,128)(2,1)S(1)} collective-permute-done((bf16[128,1152]{1,0:T(8,128)(2,1)S(1)}, bf16[128,1152]{1,0:T(8,128)(2,1)S(1)}, u32[]{:S(2)}, u32[]{:S(2)}) %collective-permute-start.4) | collective-permute-done | bytes 294944 | tf_op jit(solution)/shard_map/ppermute | solution.py:23
  51.6 1.1 %far_texts.1 = (bf16[128,512]{1,0:T(8,128)(2,1)S(1)}, bf16[128,1152]{1,0:T(8,128)(2,1)S(1)}, f32[1,512]{1,0:T(1,128)S(1)}, bf16[64,1152]{1,0:T(8,128)(2,1)S(1)}, bf16[96,1152]{1,0:T(8,128)(2,1)S(1)}) custom-call(f32[2,512]{1,0:T(2,128)S(1)} %get-tuple-element.25.knobs, bf16[512,1152]{1,0:T(8,128)(2,1)S(1)} %get-tuple-element.28.units, ...), custom_call_target="tpu_custom_call" | custom-call | flops 301989888 | bytes 3129344 | tf_op jit(solution)/shard_map/far_texts/pallas_call | solution.py:166
  52.7 2.5 %collective-permute-start.6 = (bf16[96,1152]{1,0:T(8,128)(2,1)S(1)}, bf16[96,1152]{1,0:T(8,128)(2,1)S(1)}, u32[]{:S(2)}, u32[]{:S(2)}) collective-permute-start(bf16[96,1152]{1,0:T(8,128)(2,1)S(1)} %get-tuple-element.38), channel_id=1, source_target_pairs={{0,1},{1,0},{2,3},{3,2},{4,5},{5,4},{6,7},{7,6},{8,9},{9,8},{10,11... | collective-permute-start | bytes 663560 | tf_op jit(solution)/shard_map/ppermute | solution.py:32
  55.2 1.9 %collective-permute-start.5 = (bf16[64,1152]{1,0:T(8,128)(2,1)S(1)}, bf16[64,1152]{1,0:T(8,128)(2,1)S(1)}, u32[]{:S(2)}, u32[]{:S(2)}) collective-permute-start(bf16[64,1152]{1,0:T(8,128)(2,1)S(1)} %get-tuple-element.37), channel_id=1, source_target_pairs={{0,1},{1,0},{2,3},{3,2},{4,5},{5,4},{6,7},{7,6},{8,9},{9,8},{10,11... | collective-permute-start | bytes 442376 | tf_op jit(solution)/shard_map/ppermute | solution.py:32
  57.1 0.9 %image_parts.1 = (bf16[128,1152]{1,0:T(8,128)(2,1)S(1)}, f32[2,128,1152]{2,1,0:T(8,128)S(1)}, f32[128,1152]{1,0:T(8,128)S(1)}) custom-call(bf16[512,1152]{1,0:T(8,128)(2,1)S(1)} %get-tuple-element.28.units, bf16[256,1152]{1,0:T(8,128)(2,1)S(1)} %get-tuple-element.30.text_units, bf16[256,512]{1,0:T(8,128)(2,1)S(1)} %get-tuple-element.31.coefs, ...), custom_call_target="tpu_custom_call" | custom-call | bytes 4521984 | tf_op jit(solution)/shard_map/image_parts/pallas_call | solution.py:166
  58.0 0.4 collective-permute-done.5.from_top
  58.5 0.0 collective-permute-done.6.from_low
  58.5 0.1 chip_sum.1
  58.6 2.1 %collective-permute-start.7 = (bf16[128,1152]{1,0:T(8,128)(2,1)S(1)}, bf16[128,1152]{1,0:T(8,128)(2,1)S(1)}, u32[]{:S(2)}, u32[]{:S(2)}) collective-permute-start(bf16[128,1152]{1,0:T(8,128)(2,1)S(1)} %get-tuple-element.40), channel_id=1, source_target_pairs={{0,1},{1,0},{2,3},{3,2},{4,5},{5,4},{6,7},{7,6},{8,9},{9,8},{10,11... | collective-permute-start | bytes 884744 | tf_op jit(solution)/shard_map/ppermute | solution.py:32
  60.6 1.9 %collective-permute-start.8 = (bf16[144,1152]{1,0:T(8,128)(2,1)S(1)}, bf16[144,1152]{1,0:T(8,128)(2,1)S(1)}, u32[]{:S(2)}, u32[]{:S(2)}) collective-permute-start(bf16[144,1152]{1,0:T(8,128)(2,1)S(1)} %chip_sum.1), channel_id=1, source_target_pairs={{0,2},{1,3},{2,0},{3,1},{4,6},{5,7},{6,4},{7,5},{8,10},{9,11},{10,... | collective-permute-start | bytes 995336 | tf_op jit(solution)/shard_map/ppermute | solution.py:32
  62.5 0.0 collective-permute-done.9.part_one
  62.6 2.4 %collective-permute-done.10.part_zero = bf16[128,1152]{1,0:T(8,128)(2,1)S(1)} collective-permute-done((bf16[128,1152]{1,0:T(8,128)(2,1)S(1)}, bf16[128,1152]{1,0:T(8,128)(2,1)S(1)}, u32[]{:S(2)}, u32[]{:S(2)}) %collective-permute-start.10) | collective-permute-done | bytes 294944 | tf_op jit(solution)/shard_map/ppermute | solution.py:28
  65.0 0.9 %text_sum.1 = f32[128,1152]{1,0:T(8,128)} custom-call(f32[128,1152]{1,0:T(8,128)S(1)} %get-tuple-element.44.part_two, bf16[128,1152]{1,0:T(8,128)(2,1)S(1)} %collective-permute-done.9.part_one, bf16[128,1152]{1,0:T(8,128)(2,1)S(1)} %collective-permute-done.10.part_zero), custom_call_target="tpu_custom_call" | custom-call | flops 15099494400 | bytes 1769472 | tf_op jit(solution)/shard_map/text_sum/pallas_call | solution.py:166
  65.9 0.0 collective-permute-done.7.from_core
  65.9 5.6 %collective-permute-done.8.from_across = bf16[144,1152]{1,0:T(8,128)(2,1)S(1)} collective-permute-done((bf16[144,1152]{1,0:T(8,128)(2,1)S(1)}, bf16[144,1152]{1,0:T(8,128)(2,1)S(1)}, u32[]{:S(2)}, u32[]{:S(2)}) %collective-permute-start.8) | collective-permute-done | bytes 331808 | tf_op jit(solution)/shard_map/ppermute | solution.py:32
  71.5 1.1 %image_grad.1 = (f32[128,1152]{1,0:T(8,128)}, f32[1,128]{1,0:T(1,128)}) custom-call(bf16[512,1152]{1,0:T(8,128)(2,1)S(1)} %get-tuple-element.28.units, f32[128,128]{1,0:T(8,128)S(1)} %get-tuple-element.29.inverses, f32[2,128,1152]{2,1,0:T(8,128)S(1)} %get-tuple-element.35.kept, f32[1,512]{1,0:T(1,128)S(1)} %get-tuple-element.36.losses, ...), custom_call_target="tpu_custom_call" | custom-call | bytes 3865088 | tf_op jit(solution)/shard_map/image_grad/pallas_call | solution.py:166
  (1 shorter events, 0.0 us)
Async XLA Ops:
  0.6 19.9 %collective-permute-start.1 = (bf16[128,1152]{1,0:T(8,128)(2,1)}, bf16[128,1152]{1,0:T(8,128)(2,1)S(1)}, u32[]{:S(2)}, u32[]{:S(2)}) collective-permute-start(bf16[128,1152]{1,0:T(8,128)(2,1)} %images.1), channel_id=1, source_target_pairs={{0,2},{1,3},{2,0},{3,1},{4,6},{5,7},{6,4},{7,5},{8,10},{9,11},{10,... | collective-permute-start | bytes 884744 | tf_op jit(solution)/shard_map/ppermute | solution.py:32
  4.7 28.8 %collective-permute-start.3 = (bf16[128,1152]{1,0:T(8,128)(2,1)}, bf16[128,1152]{1,0:T(8,128)(2,1)S(1)}, u32[]{:S(2)}, u32[]{:S(2)}) collective-permute-start(bf16[128,1152]{1,0:T(8,128)(2,1)} %texts.1), channel_id=1, source_target_pairs={{0,4},{1,5},{2,6},{3,7},{4,8},{5,9},{6,10},{7,11},{8,12},{9,13},{1... | collective-permute-start | bytes 884744 | tf_op jit(solution)/shard_map/ppermute | solution.py:23
  7.8 31.0 %collective-permute-start = (bf16[128,1152]{1,0:T(8,128)(2,1)}, bf16[128,1152]{1,0:T(8,128)(2,1)S(1)}, u32[]{:S(2)}, u32[]{:S(2)}) collective-permute-start(bf16[128,1152]{1,0:T(8,128)(2,1)} %images.1), channel_id=1, source_target_pairs={{0,1},{1,0},{2,3},{3,2},{4,5},{5,4},{6,7},{7,6},{8,9},{9,8},{10,11... | collective-permute-start | bytes 884744 | tf_op jit(solution)/shard_map/ppermute | solution.py:32
  20.6 18.3 %collective-permute-start.2 = (bf16[128,1152]{1,0:T(8,128)(2,1)S(1)}, bf16[128,1152]{1,0:T(8,128)(2,1)S(1)}, u32[]{:S(2)}, u32[]{:S(2)}) collective-permute-start(bf16[128,1152]{1,0:T(8,128)(2,1)S(1)} %collective-permute-done.1.across), channel_id=1, source_target_pairs={{0,1},{1,0},{2,3},{3,2},{4,5},{5,4},{6,7},{7,6},{8,9},{9,8},{10,11... | collective-permute-start | bytes 884744 | tf_op jit(solution)/shard_map/ppermute | solution.py:32
  33.5 18.1 %collective-permute-start.4 = (bf16[128,1152]{1,0:T(8,128)(2,1)S(1)}, bf16[128,1152]{1,0:T(8,128)(2,1)S(1)}, u32[]{:S(2)}, u32[]{:S(2)}) collective-permute-start(bf16[128,1152]{1,0:T(8,128)(2,1)S(1)} %collective-permute-done.3.texts_one), channel_id=1, source_target_pairs={{0,6},{1,7},{2,4},{3,5},{4,8},{5,9},{6,10},{7,11},{8,12},{9,13},{1... | collective-permute-start | bytes 884744 | tf_op jit(solution)/shard_map/ppermute | solution.py:23
  36.7 1.0 %copy-start = (bf16[128,1152]{1,0:T(8,128)(2,1)S(1)}, bf16[128,1152]{1,0:T(8,128)(2,1)}, u32[]{:S(2)}) copy-start(bf16[128,1152]{1,0:T(8,128)(2,1)} %texts.1) | copy-start | bytes 884740
  37.7 1.0 %copy-start.1 = (bf16[128,1152]{1,0:T(8,128)(2,1)S(1)}, bf16[128,1152]{1,0:T(8,128)(2,1)}, u32[]{:S(2)}) copy-start(bf16[128,1152]{1,0:T(8,128)(2,1)} %images.1) | copy-start | bytes 884740
  40.8 21.7 %collective-permute-start.9 = (bf16[128,1152]{1,0:T(8,128)(2,1)S(1)}, bf16[128,1152]{1,0:T(8,128)(2,1)S(1)}, u32[]{:S(2)}, u32[]{:S(2)}) collective-permute-start(bf16[128,1152]{1,0:T(8,128)(2,1)S(1)} %get-tuple-element.45), channel_id=1, source_target_pairs={{0,6},{1,7},{2,4},{3,5},{4,8},{5,9},{6,10},{7,11},{8,12},{9,13},{1... | collective-permute-start | bytes 884744 | tf_op jit(solution)/shard_map/ppermute | solution.py:23
  42.7 22.2 %collective-permute-start.10 = (bf16[128,1152]{1,0:T(8,128)(2,1)S(1)}, bf16[128,1152]{1,0:T(8,128)(2,1)S(1)}, u32[]{:S(2)}, u32[]{:S(2)}) collective-permute-start(bf16[128,1152]{1,0:T(8,128)(2,1)S(1)} %get-tuple-element.46), channel_id=1, source_target_pairs={{0,8},{4,12},{8,16},{12,20},{16,24},{20,28},{24,32},{28,36},{32,40... | collective-permute-start | bytes 884744 | tf_op jit(solution)/shard_map/ppermute | solution.py:28
  52.7 5.8 %collective-permute-start.6 = (bf16[96,1152]{1,0:T(8,128)(2,1)S(1)}, bf16[96,1152]{1,0:T(8,128)(2,1)S(1)}, u32[]{:S(2)}, u32[]{:S(2)}) collective-permute-start(bf16[96,1152]{1,0:T(8,128)(2,1)S(1)} %get-tuple-element.38), channel_id=1, source_target_pairs={{0,1},{1,0},{2,3},{3,2},{4,5},{5,4},{6,7},{7,6},{8,9},{9,8},{10,11... | collective-permute-start | bytes 663560 | tf_op jit(solution)/shard_map/ppermute | solution.py:32
  55.2 3.3 %collective-permute-start.5 = (bf16[64,1152]{1,0:T(8,128)(2,1)S(1)}, bf16[64,1152]{1,0:T(8,128)(2,1)S(1)}, u32[]{:S(2)}, u32[]{:S(2)}) collective-permute-start(bf16[64,1152]{1,0:T(8,128)(2,1)S(1)} %get-tuple-element.37), channel_id=1, source_target_pairs={{0,1},{1,0},{2,3},{3,2},{4,5},{5,4},{6,7},{7,6},{8,9},{9,8},{10,11... | collective-permute-start | bytes 442376 | tf_op jit(solution)/shard_map/ppermute | solution.py:32
  58.6 7.3 %collective-permute-start.7 = (bf16[128,1152]{1,0:T(8,128)(2,1)S(1)}, bf16[128,1152]{1,0:T(8,128)(2,1)S(1)}, u32[]{:S(2)}, u32[]{:S(2)}) collective-permute-start(bf16[128,1152]{1,0:T(8,128)(2,1)S(1)} %get-tuple-element.40), channel_id=1, source_target_pairs={{0,1},{1,0},{2,3},{3,2},{4,5},{5,4},{6,7},{7,6},{8,9},{9,8},{10,11... | collective-permute-start | bytes 884744 | tf_op jit(solution)/shard_map/ppermute | solution.py:32
  60.6 10.9 %collective-permute-start.8 = (bf16[144,1152]{1,0:T(8,128)(2,1)S(1)}, bf16[144,1152]{1,0:T(8,128)(2,1)S(1)}, u32[]{:S(2)}, u32[]{:S(2)}) collective-permute-start(bf16[144,1152]{1,0:T(8,128)(2,1)S(1)} %chip_sum.1), channel_id=1, source_target_pairs={{0,2},{1,3},{2,0},{3,1},{4,6},{5,7},{6,4},{7,5},{8,10},{9,11},{10,... | collective-permute-start | bytes 995336 | tf_op jit(solution)/shard_map/ppermute | solution.py:32

commit v3 on v2

--- a/solution.py
+++ b/solution.py
@@ -75,17 +75,24 @@
     return wide[0:1, :rows] + wide[half : half + 1, :rows]
 
 
-def own_kernel(log_scale, bias, images, texts, image_unit, text_unit, knobs, inverses):
-    unit, inverse = unit_rows(images[...])
+def own_kernel(images, texts, texts_one, image_unit, text_units, inverses, own_images, own_texts, sems):
+    copies = [
+        pltpu.make_async_copy(images, own_images, sems.at[0]),
+        pltpu.make_async_copy(texts, own_texts, sems.at[1]),
+    ]
+    rows = texts_one.shape[0]
+    for copy in copies:
+        copy.start()
+    text_units[rows:, :] = unit_rows(texts_one[...])[0]
+    for copy in copies:
+        copy.wait()
+    unit, inverse = unit_rows(own_images[...])
     image_unit[...] = unit
     inverses[...] = jnp.broadcast_to(inverse, inverses.shape)
-    text_unit[...] = unit_rows(texts[...])[0]
-    span = knobs.shape[1]
-    knobs[0:1, :] = jnp.exp(jnp.full((1, span), log_scale[0], F32))
-    knobs[1:2, :] = jnp.full((1, span), bias[0], F32)
-
-
-def near_kernel(knobs, image_unit, text_unit, core, across, diagonal, texts_one, units, text_units, coefs, losses, part_zero, part_one):
+    text_units[:rows, :] = unit_rows(own_texts[...])[0]
+
+
+def near_kernel(knobs, image_unit, text_units, core, across, diagonal, units, coefs, losses, part_zero, part_one):
     rows = image_unit.shape[0]
     units[:rows, :] = image_unit[...]
     for place, block in ((1, core), (2, across), (3, diagonal)):
@@ -96,9 +103,8 @@
     positive = lax.broadcasted_iota(jnp.int32, shape, 0) == lax.broadcasted_iota(jnp.int32, shape, 1)
     total = None
     for step, part in enumerate((part_zero, part_one)):
-        unit = text_unit[...] if step == 0 else unit_rows(texts_one[...])[0]
+        unit = text_units[step * rows : (step + 1) * rows, :]
         loss, coef = pair_terms(unit, everything, scale, offset, positive if step == 0 else None)
-        text_units[step * rows : (step + 1) * rows, :] = unit
         coefs[step * rows : (step + 1) * rows, :] = coef
         part[...] = jnp.dot(coef, everything, preferred_element_type=F32).astype(BF16)
         total = loss if total is None else total + loss
@@ -159,9 +165,9 @@
     text_grad[...] = part_two[...] + part_one[...].astype(F32) + part_zero[...].astype(F32)
 
 
-def call(kernel, name, outs, arguments, scalars=0, flops=0):
-    in_specs = [pl.BlockSpec(memory_space=pltpu.SMEM)] * scalars
-    in_specs += [pl.BlockSpec(memory_space=pltpu.VMEM)] * (len(arguments) - scalars)
+def call(kernel, name, outs, arguments, far=0, flops=0, scratch=()):
+    in_specs = [pl.BlockSpec(memory_space=pltpu.HBM)] * far
+    in_specs += [pl.BlockSpec(memory_space=pltpu.VMEM)] * (len(arguments) - far)
     moved = sum(a.size * a.dtype.itemsize for a in (*arguments, *outs))
     return pl.pallas_call(
         kernel,
@@ -169,6 +175,7 @@
         out_shape=outs,
         in_specs=in_specs,
         out_specs=tuple(pl.BlockSpec(memory_space=pltpu.VMEM) for _ in outs),
+        scratch_shapes=scratch,
         cost_estimate=pl.CostEstimate(flops=flops, bytes_accessed=moved, transcendentals=0),
         compiler_params=pltpu.CompilerParams(vmem_limit_bytes=24 * 1024 * 1024),
     )(*arguments)
@@ -179,36 +186,42 @@
     span = rows * lax.axis_size("grp")
     tall = rows + LOSS_ROWS
     half = lax.axis_size("blk") // 2
-    first_flips = (half - 2, half - 1)
-    second_flips = (half - 1, 0)
+    first_flips = (half - 1,)
+    second_flips = (0,)
     made = jax.ShapeDtypeStruct
     texts_one = passed_along(texts, first_flips)
     across = swapped(images, 2)
     core = swapped(images, 1)
-    texts_two = passed_along(texts_one, second_flips)
+    texts_two = passed_two(texts)
+    pair = jnp.stack([jnp.exp(log_scale), bias])
+    knobs = jnp.broadcast_to(pair, (2, span))
+    across, knobs = lax.optimization_barrier((across, knobs))
     diagonal = swapped(across, 1)
     matmul = 2 * rows * span * width
-    image_unit, text_unit, knobs, inverses = call(
+    image_unit, text_units, inverses = call(
         own_kernel,
         "own_units",
-        (made((rows, width), BF16), made((rows, width), BF16), made((2, span), F32), made((rows, 128), F32)),
-        (log_scale, bias, images, texts),
+        (made((rows, width), BF16), made((2 * rows, width), BF16), made((rows, 128), F32)),
+        (
+            pltpu.with_memory_space_constraint(images, pltpu.HBM),
+            pltpu.with_memory_space_constraint(texts, pltpu.HBM),
+            texts_one,
+        ),
         2,
-    )
-    units, text_units, coefs, losses, part_zero, part_one = call(
+        30 * matmul,
+        (pltpu.VMEM((rows, width), BF16), pltpu.VMEM((rows, width), BF16), pltpu.SemaphoreType.DMA((2,))),
+    )
+    units, coefs, losses, part_zero, part_one = call(
         near_kernel,
         "near_texts",
         (
             made((span, width), BF16),
-            made((2 * rows, width), BF16),
             made((2 * rows, span), BF16),
             made((1, span), F32),
             made((rows, width), BF16),
             made((rows, width), BF16),
         ),
-        (knobs, image_unit, text_unit, core, across, diagonal, texts_one),
-        0,
-        4 * matmul,
+        (knobs, image_unit, text_units, core, across, diagonal),
     )
     part_zero = passed_two(part_zero)
     part_one = passed_along(part_one, second_flips)
@@ -223,8 +236,6 @@
             made((rows // 2 + 2 * LOSS_ROWS, width), BF16),
         ),
         (knobs, units, text_units, coefs, losses, texts_two),
-        0,
-        2 * matmul,
     )
     from_core_top = swapped(to_core_top, 1)
     from_core_low = swapped(to_core_low, 1)
@@ -238,7 +249,7 @@
     to_across, to_core_near = lax.optimization_barrier((to_across, to_core_near))
     from_across = swapped(to_across, 2)
     from_core_near = swapped(to_core_near, 1)
-    (text_grad,) = call(text_kernel, "text_sum", (made((rows, width), F32),), (part_two, part_one, part_zero), 0, 100 * matmul)
+    (text_grad,) = call(text_kernel, "text_sum", (made((rows, width), F32),), (part_two, part_one, part_zero), 0, 20 * matmul)
     image_grad, row_loss = call(
         last_kernel,
         "image_grad",

time: 73.1 us -> 66.7 us (0.912)
  waiting for transfers between devices: 23.5 us -> 18.7 us
  local copies, waits for them, and re-layouts: 1.92 us -> 0.07 us
  Pallas kernels: 6.2 us -> 7.29 us
  starting transfers between devices: 39 us -> 38 us
    ppermute x3 -> x2, waiting for transfers between devices: 14.9 us -> 7.62 us  [passed_along(): return lax.ppermute(block, ('blk', 'grp'), route)]
    ppermute x7, waiting for transfers between devices: 6.09 us -> 9.73 us  [swapped(): lax.ppermute(block, 'grp', [(i, i ^ flip) for i in range(lax.axis_size('g...]
    ppermute x1 -> x2, starting transfers between devices: 1.92 us -> 3.84 us  [passed_two(): lax.ppermute(block, 'blk', [(i, (i + 2) % groups) for i in range(groups)])]
    unnamed x4 -> x0, local copies, waits for them, and re-layouts: 1.92 us -> none
    ppermute x3 -> x2, starting transfers between devices: 6.95 us -> 5.04 us  [passed_along(): return lax.ppermute(block, ('blk', 'grp'), route)]
    pallas_call x7, Pallas kernels: 6.2 us -> 7.29 us  [call(): pl.pallas_call(kernel, name=name, out_shape=outs, in_specs=in_specs, out_...]
    ppermute x1 -> x2, waiting for transfers between devices: 2.43 us -> 1.35 us  [passed_two(): lax.ppermute(block, 'blk', [(i, (i + 2) % groups) for i in range(groups)])]
    ppermute x7, starting transfers between devices: 30.1 us -> 29.1 us  [swapped(): lax.ppermute(block, 'grp', [(i, i ^ flip) for i in range(lax.axis_size('g...]
  transfers between devices with their start and end apart: 11 -> 11, of which waited for: 5 -> 5; matrix products, arithmetic and copies ran while one was open for 0% -> 0% of each run, Pallas kernels for 7% -> 9%
where the time goes in v3:
time: 66.7 us; the launch traced here: 66.3 us
  starting transfers between devices  38 us (57%)
  waiting for transfers between devices  18.7 us (28%)
  Pallas kernels  7.29 us (11%)
  between operations  2.11 us (3%)
    ppermute x7, starting transfers between devices, swapped(): lax.ppermute(block, 'grp', [(i, i ^ flip) for i in range(lax.axis_size('g...  29.1 us
    ppermute x7, waiting for transfers between devices, swapped(): lax.ppermute(block, 'grp', [(i, i ^ flip) for i in range(lax.axis_size('g...  9.73 us
    ppermute x2, waiting for transfers between devices, passed_along(): return lax.ppermute(block, ('blk', 'grp'), route)  7.62 us
    pallas_call x7, Pallas kernels, call(): pl.pallas_call(kernel, name=name, out_shape=outs, in_specs=in_specs, out_...  7.29 us
    ppermute x2, starting transfers between devices, passed_along(): return lax.ppermute(block, ('blk', 'grp'), route)  5.04 us
    ppermute x2, starting transfers between devices, passed_two(): lax.ppermute(block, 'blk', [(i, (i + 2) % groups) for i in range(groups)])  3.84 us
    ppermute x2, waiting for transfers between devices, passed_two(): lax.ppermute(block, 'blk', [(i, (i + 2) % groups) for i in range(groups)])  1.35 us
  transfers between devices with their start and end apart: 11, of which 5 were waited for; matrix products, arithmetic and copies ran while one was open for 0% of the time, Pallas kernels for 9%

profile of v3, /device:TPU:1, one launch (start us, length us, event | category | flops | bytes accessed | tf_op | source)
XLA Modules:
  0.0 66.3 jit_solution(3641853107397045908)
XLA Ops:
  0.6 4.0 %collective-permute-start = (bf16[128,1152]{1,0:T(8,128)(2,1)}, bf16[128,1152]{1,0:T(8,128)(2,1)S(1)}, u32[]{:S(2)}, u32[]{:S(2)}) collective-permute-start(bf16[128,1152]{1,0:T(8,128)(2,1)} %images.1), channel_id=1, source_target_pairs={{0,2},{1,3},{2,0},{3,1},{4,6},{5,7},{6,4},{7,5},{8,10},{9,11},{10,... | collective-permute-start | bytes 884744 | tf_op jit(solution)/shard_map/ppermute | solution.py:32
  4.7 3.1 %collective-permute-start.1 = (bf16[128,1152]{1,0:T(8,128)(2,1)}, bf16[128,1152]{1,0:T(8,128)(2,1)S(1)}, u32[]{:S(2)}, u32[]{:S(2)}) collective-permute-start(bf16[128,1152]{1,0:T(8,128)(2,1)} %texts.1), channel_id=1, source_target_pairs={{0,4},{1,5},{2,6},{3,7},{4,8},{5,9},{6,10},{7,11},{8,12},{9,13},{1... | collective-permute-start | bytes 884744 | tf_op jit(solution)/shard_map/ppermute | solution.py:23
  7.8 12.8 %collective-permute-start.2 = (bf16[128,1152]{1,0:T(8,128)(2,1)}, bf16[128,1152]{1,0:T(8,128)(2,1)S(1)}, u32[]{:S(2)}, u32[]{:S(2)}) collective-permute-start(bf16[128,1152]{1,0:T(8,128)(2,1)} %images.1), channel_id=1, source_target_pairs={{0,1},{1,0},{2,3},{3,2},{4,5},{5,4},{6,7},{7,6},{8,9},{9,8},{10,11... | collective-permute-start | bytes 884744 | tf_op jit(solution)/shard_map/ppermute | solution.py:32
  20.6 1.9 %collective-permute-start.4 = (bf16[128,1152]{1,0:T(8,128)(2,1)}, bf16[128,1152]{1,0:T(8,128)(2,1)S(1)}, u32[]{:S(2)}, u32[]{:S(2)}) collective-permute-start(bf16[128,1152]{1,0:T(8,128)(2,1)} %texts.1), channel_id=1, source_target_pairs={{0,8},{4,12},{8,16},{12,20},{16,24},{20,28},{24,32},{28,36},{32,40... | collective-permute-start | bytes 884744 | tf_op jit(solution)/shard_map/ppermute | solution.py:28
  23.8 0.1 maximum_bitcast_fusion
  23.9 0.0 collective-permute-done.across
  23.9 0.1 broadcast_in_dim.8.knobs
  24.0 1.9 %collective-permute-start.3 = (bf16[128,1152]{1,0:T(8,128)(2,1)S(1)}, bf16[128,1152]{1,0:T(8,128)(2,1)S(1)}, u32[]{:S(2)}, u32[]{:S(2)}) collective-permute-start(bf16[128,1152]{1,0:T(8,128)(2,1)S(1)} %collective-permute-done.across), channel_id=1, source_target_pairs={{0,1},{1,0},{2,3},{3,2},{4,5},{5,4},{6,7},{7,6},{8,9},{9,8},{10,11... | collective-permute-start | bytes 884744 | tf_op jit(solution)/shard_map/ppermute | solution.py:32
  25.9 7.6 %collective-permute-done.1.texts_one = bf16[128,1152]{1,0:T(8,128)(2,1)S(1)} collective-permute-done((bf16[128,1152]{1,0:T(8,128)(2,1)}, bf16[128,1152]{1,0:T(8,128)(2,1)S(1)}, u32[]{:S(2)}, u32[]{:S(2)}) %collective-permute-start.1) | collective-permute-done | bytes 294944 | tf_op jit(solution)/shard_map/ppermute | solution.py:23
  33.5 1.3 %own_units.1 = (bf16[128,1152]{1,0:T(8,128)(2,1)S(1)}, bf16[256,1152]{1,0:T(8,128)(2,1)S(1)}, f32[128,128]{1,0:T(8,128)S(1)}) custom-call(bf16[128,1152]{1,0:T(8,128)(2,1)} %images.1, bf16[128,1152]{1,0:T(8,128)(2,1)} %texts.1, bf16[128,1152]{1,0:T(8,128)(2,1)S(1)} %collective-permute-done.1.texts_one), custom_call_target="tpu_custom_call" | custom-call | flops 4529848320 | bytes 1835008 | tf_op jit(solution)/shard_map/own_units/pallas_call | solution.py:172
  34.8 0.0 collective-permute-done.2.core
  34.8 0.0 collective-permute-done.3.diagonal
  34.9 1.9 %near_texts.1 = (bf16[512,1152]{1,0:T(8,128)(2,1)S(1)}, bf16[256,512]{1,0:T(8,128)(2,1)S(1)}, f32[1,512]{1,0:T(1,128)S(1)}, bf16[128,1152]{1,0:T(8,128)(2,1)S(1)}, bf16[128,1152]{1,0:T(8,128)(2,1)S(1)}) custom-call(f32[2,512]{1,0:T(2,128)S(1)} %broadcast_in_dim.8.knobs, bf16[128,1152]{1,0:T(8,128)(2,1)S(1)} %get-tuple-element.26.image_unit, ...), custom_call_target="tpu_custom_call" | custom-call | bytes 3807232 | tf_op jit(solution)/shard_map/near_texts/pallas_call | solution.py:172
  36.8 1.9 %collective-permute-start.9 = (bf16[128,1152]{1,0:T(8,128)(2,1)S(1)}, bf16[128,1152]{1,0:T(8,128)(2,1)S(1)}, u32[]{:S(2)}, u32[]{:S(2)}) collective-permute-start(bf16[128,1152]{1,0:T(8,128)(2,1)S(1)} %get-tuple-element.45), channel_id=1, source_target_pairs={{0,6},{1,7},{2,4},{3,5},{4,8},{5,9},{6,10},{7,11},{8,12},{9,13},{1... | collective-permute-start | bytes 884744 | tf_op jit(solution)/shard_map/ppermute | solution.py:23
  38.7 1.9 %collective-permute-start.10 = (bf16[128,1152]{1,0:T(8,128)(2,1)S(1)}, bf16[128,1152]{1,0:T(8,128)(2,1)S(1)}, u32[]{:S(2)}, u32[]{:S(2)}) collective-permute-start(bf16[128,1152]{1,0:T(8,128)(2,1)S(1)} %get-tuple-element.46), channel_id=1, source_target_pairs={{0,8},{4,12},{8,16},{12,20},{16,24},{20,28},{24,32},{28,36},{32,40... | collective-permute-start | bytes 884744 | tf_op jit(solution)/shard_map/ppermute | solution.py:28
  40.6 1.3 %collective-permute-done.4.texts_two = bf16[128,1152]{1,0:T(8,128)(2,1)S(1)} collective-permute-done((bf16[128,1152]{1,0:T(8,128)(2,1)}, bf16[128,1152]{1,0:T(8,128)(2,1)S(1)}, u32[]{:S(2)}, u32[]{:S(2)}) %collective-permute-start.4) | collective-permute-done | bytes 294944 | tf_op jit(solution)/shard_map/ppermute | solution.py:28
  42.0 1.1 %far_texts.1 = (bf16[128,512]{1,0:T(8,128)(2,1)S(1)}, bf16[128,1152]{1,0:T(8,128)(2,1)S(1)}, f32[1,512]{1,0:T(1,128)S(1)}, bf16[64,1152]{1,0:T(8,128)(2,1)S(1)}, bf16[96,1152]{1,0:T(8,128)(2,1)S(1)}) custom-call(f32[2,512]{1,0:T(2,128)S(1)} %broadcast_in_dim.8.knobs, bf16[512,1152]{1,0:T(8,128)(2,1)S(1)} %get-tuple-element.29.units, ...), custom_call_target="tpu_custom_call" | custom-call | bytes 3129344 | tf_op jit(solution)/shard_map/far_texts/pallas_call | solution.py:172
  43.1 3.9 %collective-permute-start.6 = (bf16[96,1152]{1,0:T(8,128)(2,1)S(1)}, bf16[96,1152]{1,0:T(8,128)(2,1)S(1)}, u32[]{:S(2)}, u32[]{:S(2)}) collective-permute-start(bf16[96,1152]{1,0:T(8,128)(2,1)S(1)} %get-tuple-element.38), channel_id=1, source_target_pairs={{0,1},{1,0},{2,3},{3,2},{4,5},{5,4},{6,7},{7,6},{8,9},{9,8},{10,11... | collective-permute-start | bytes 663560 | tf_op jit(solution)/shard_map/ppermute | solution.py:32
  46.9 1.9 %collective-permute-start.5 = (bf16[64,1152]{1,0:T(8,128)(2,1)S(1)}, bf16[64,1152]{1,0:T(8,128)(2,1)S(1)}, u32[]{:S(2)}, u32[]{:S(2)}) collective-permute-start(bf16[64,1152]{1,0:T(8,128)(2,1)S(1)} %get-tuple-element.37), channel_id=1, source_target_pairs={{0,1},{1,0},{2,3},{3,2},{4,5},{5,4},{6,7},{7,6},{8,9},{9,8},{10,11... | collective-permute-start | bytes 442376 | tf_op jit(solution)/shard_map/ppermute | solution.py:32
  48.8 0.9 %image_parts.1 = (bf16[128,1152]{1,0:T(8,128)(2,1)S(1)}, f32[2,128,1152]{2,1,0:T(8,128)S(1)}, f32[128,1152]{1,0:T(8,128)S(1)}) custom-call(bf16[512,1152]{1,0:T(8,128)(2,1)S(1)} %get-tuple-element.29.units, bf16[256,1152]{1,0:T(8,128)(2,1)S(1)} %get-tuple-element.27.text_units, bf16[256,512]{1,0:T(8,128)(2,1)S(1)} %get-tuple-element.31.coefs, ...), custom_call_target="tpu_custom_call" | custom-call | bytes 4521984 | tf_op jit(solution)/shard_map/image_parts/pallas_call | solution.py:172
  49.8 0.4 collective-permute-done.5.from_top
  50.2 0.0 collective-permute-done.6.from_low
  50.2 0.1 chip_sum.1
  50.3 2.3 %collective-permute-start.8 = (bf16[144,1152]{1,0:T(8,128)(2,1)S(1)}, bf16[144,1152]{1,0:T(8,128)(2,1)S(1)}, u32[]{:S(2)}, u32[]{:S(2)}) collective-permute-start(bf16[144,1152]{1,0:T(8,128)(2,1)S(1)} %chip_sum.1), channel_id=1, source_target_pairs={{0,2},{1,3},{2,0},{3,1},{4,6},{5,7},{6,4},{7,5},{8,10},{9,11},{10,... | collective-permute-start | bytes 995336 | tf_op jit(solution)/shard_map/ppermute | solution.py:32
  52.6 2.3 %collective-permute-start.7 = (bf16[128,1152]{1,0:T(8,128)(2,1)S(1)}, bf16[128,1152]{1,0:T(8,128)(2,1)S(1)}, u32[]{:S(2)}, u32[]{:S(2)}) collective-permute-start(bf16[128,1152]{1,0:T(8,128)(2,1)S(1)} %get-tuple-element.40), channel_id=1, source_target_pairs={{0,1},{1,0},{2,3},{3,2},{4,5},{5,4},{6,7},{7,6},{8,9},{9,8},{10,11... | collective-permute-start | bytes 884744 | tf_op jit(solution)/shard_map/ppermute | solution.py:32
  54.9 0.0 collective-permute-done.9.part_one
  54.9 0.0 collective-permute-done.10.part_zero
  55.0 0.9 %text_sum.1 = f32[128,1152]{1,0:T(8,128)} custom-call(f32[128,1152]{1,0:T(8,128)S(1)} %get-tuple-element.44.part_two, bf16[128,1152]{1,0:T(8,128)(2,1)S(1)} %collective-permute-done.9.part_one, bf16[128,1152]{1,0:T(8,128)(2,1)S(1)} %collective-permute-done.10.part_zero), custom_call_target="tpu_custom_call" | custom-call | flops 3019898880 | bytes 1769472 | tf_op jit(solution)/shard_map/text_sum/pallas_call | solution.py:172
  55.9 0.2 collective-permute-done.7.from_core
  56.1 9.0 %collective-permute-done.8.from_across = bf16[144,1152]{1,0:T(8,128)(2,1)S(1)} collective-permute-done((bf16[144,1152]{1,0:T(8,128)(2,1)S(1)}, bf16[144,1152]{1,0:T(8,128)(2,1)S(1)}, u32[]{:S(2)}, u32[]{:S(2)}) %collective-permute-start.8) | collective-permute-done | bytes 331808 | tf_op jit(solution)/shard_map/ppermute | solution.py:32
  65.2 1.1 %image_grad.1 = (f32[128,1152]{1,0:T(8,128)}, f32[1,128]{1,0:T(1,128)}) custom-call(bf16[512,1152]{1,0:T(8,128)(2,1)S(1)} %get-tuple-element.29.units, f32[128,128]{1,0:T(8,128)S(1)} %get-tuple-element.30.inverses, f32[2,128,1152]{2,1,0:T(8,128)S(1)} %get-tuple-element.35.kept, f32[1,512]{1,0:T(1,128)S(1)} %get-tuple-element.36.losses, ...), custom_call_target="tpu_custom_call" | custom-call | bytes 3865088 | tf_op jit(solution)/shard_map/image_grad/pallas_call | solution.py:172
Async XLA Ops:
  0.6 23.3 %collective-permute-start = (bf16[128,1152]{1,0:T(8,128)(2,1)}, bf16[128,1152]{1,0:T(8,128)(2,1)S(1)}, u32[]{:S(2)}, u32[]{:S(2)}) collective-permute-start(bf16[128,1152]{1,0:T(8,128)(2,1)} %images.1), channel_id=1, source_target_pairs={{0,2},{1,3},{2,0},{3,1},{4,6},{5,7},{6,4},{7,5},{8,10},{9,11},{10,... | collective-permute-start | bytes 884744 | tf_op jit(solution)/shard_map/ppermute | solution.py:32
  4.7 28.8 %collective-permute-start.1 = (bf16[128,1152]{1,0:T(8,128)(2,1)}, bf16[128,1152]{1,0:T(8,128)(2,1)S(1)}, u32[]{:S(2)}, u32[]{:S(2)}) collective-permute-start(bf16[128,1152]{1,0:T(8,128)(2,1)} %texts.1), channel_id=1, source_target_pairs={{0,4},{1,5},{2,6},{3,7},{4,8},{5,9},{6,10},{7,11},{8,12},{9,13},{1... | collective-permute-start | bytes 884744 | tf_op jit(solution)/shard_map/ppermute | solution.py:23
  7.8 27.0 %collective-permute-start.2 = (bf16[128,1152]{1,0:T(8,128)(2,1)}, bf16[128,1152]{1,0:T(8,128)(2,1)S(1)}, u32[]{:S(2)}, u32[]{:S(2)}) collective-permute-start(bf16[128,1152]{1,0:T(8,128)(2,1)} %images.1), channel_id=1, source_target_pairs={{0,1},{1,0},{2,3},{3,2},{4,5},{5,4},{6,7},{7,6},{8,9},{9,8},{10,11... | collective-permute-start | bytes 884744 | tf_op jit(solution)/shard_map/ppermute | solution.py:32
  20.6 21.4 %collective-permute-start.4 = (bf16[128,1152]{1,0:T(8,128)(2,1)}, bf16[128,1152]{1,0:T(8,128)(2,1)S(1)}, u32[]{:S(2)}, u32[]{:S(2)}) collective-permute-start(bf16[128,1152]{1,0:T(8,128)(2,1)} %texts.1), channel_id=1, source_target_pairs={{0,8},{4,12},{8,16},{12,20},{16,24},{20,28},{24,32},{28,36},{32,40... | collective-permute-start | bytes 884744 | tf_op jit(solution)/shard_map/ppermute | solution.py:28
  24.0 10.9 %collective-permute-start.3 = (bf16[128,1152]{1,0:T(8,128)(2,1)S(1)}, bf16[128,1152]{1,0:T(8,128)(2,1)S(1)}, u32[]{:S(2)}, u32[]{:S(2)}) collective-permute-start(bf16[128,1152]{1,0:T(8,128)(2,1)S(1)} %collective-permute-done.across), channel_id=1, source_target_pairs={{0,1},{1,0},{2,3},{3,2},{4,5},{5,4},{6,7},{7,6},{8,9},{9,8},{10,11... | collective-permute-start | bytes 884744 | tf_op jit(solution)/shard_map/ppermute | solution.py:32
  36.8 18.2 %collective-permute-start.9 = (bf16[128,1152]{1,0:T(8,128)(2,1)S(1)}, bf16[128,1152]{1,0:T(8,128)(2,1)S(1)}, u32[]{:S(2)}, u32[]{:S(2)}) collective-permute-start(bf16[128,1152]{1,0:T(8,128)(2,1)S(1)} %get-tuple-element.45), channel_id=1, source_target_pairs={{0,6},{1,7},{2,4},{3,5},{4,8},{5,9},{6,10},{7,11},{8,12},{9,13},{1... | collective-permute-start | bytes 884744 | tf_op jit(solution)/shard_map/ppermute | solution.py:23
  38.7 16.3 %collective-permute-start.10 = (bf16[128,1152]{1,0:T(8,128)(2,1)S(1)}, bf16[128,1152]{1,0:T(8,128)(2,1)S(1)}, u32[]{:S(2)}, u32[]{:S(2)}) collective-permute-start(bf16[128,1152]{1,0:T(8,128)(2,1)S(1)} %get-tuple-element.46), channel_id=1, source_target_pairs={{0,8},{4,12},{8,16},{12,20},{16,24},{20,28},{24,32},{28,36},{32,40... | collective-permute-start | bytes 884744 | tf_op jit(solution)/shard_map/ppermute | solution.py:28
  43.1 7.1 %collective-permute-start.6 = (bf16[96,1152]{1,0:T(8,128)(2,1)S(1)}, bf16[96,1152]{1,0:T(8,128)(2,1)S(1)}, u32[]{:S(2)}, u32[]{:S(2)}) collective-permute-start(bf16[96,1152]{1,0:T(8,128)(2,1)S(1)} %get-tuple-element.38), channel_id=1, source_target_pairs={{0,1},{1,0},{2,3},{3,2},{4,5},{5,4},{6,7},{7,6},{8,9},{9,8},{10,11... | collective-permute-start | bytes 663560 | tf_op jit(solution)/shard_map/ppermute | solution.py:32
  46.9 3.3 %collective-permute-start.5 = (bf16[64,1152]{1,0:T(8,128)(2,1)S(1)}, bf16[64,1152]{1,0:T(8,128)(2,1)S(1)}, u32[]{:S(2)}, u32[]{:S(2)}) collective-permute-start(bf16[64,1152]{1,0:T(8,128)(2,1)S(1)} %get-tuple-element.37), channel_id=1, source_target_pairs={{0,1},{1,0},{2,3},{3,2},{4,5},{5,4},{6,7},{7,6},{8,9},{9,8},{10,11... | collective-permute-start | bytes 442376 | tf_op jit(solution)/shard_map/ppermute | solution.py:32
  50.3 14.9 %collective-permute-start.8 = (bf16[144,1152]{1,0:T(8,128)(2,1)S(1)}, bf16[144,1152]{1,0:T(8,128)(2,1)S(1)}, u32[]{:S(2)}, u32[]{:S(2)}) collective-permute-start(bf16[144,1152]{1,0:T(8,128)(2,1)S(1)} %chip_sum.1), channel_id=1, source_target_pairs={{0,2},{1,3},{2,0},{3,1},{4,6},{5,7},{6,4},{7,5},{8,10},{9,11},{10,... | collective-permute-start | bytes 995336 | tf_op jit(solution)/shard_map/ppermute | solution.py:32
  52.6 3.5 %collective-permute-start.7 = (bf16[128,1152]{1,0:T(8,128)(2,1)S(1)}, bf16[128,1152]{1,0:T(8,128)(2,1)S(1)}, u32[]{:S(2)}, u32[]{:S(2)}) collective-permute-start(bf16[128,1152]{1,0:T(8,128)(2,1)S(1)} %get-tuple-element.40), channel_id=1, source_target_pairs={{0,1},{1,0},{2,3},{3,2},{4,5},{5,4},{6,7},{7,6},{8,9},{9,8},{10,11... | collective-permute-start | bytes 884744 | tf_op jit(solution)/shard_map/ppermute | solution.py:32

commit v4 on v3

--- a/solution.py
+++ b/solution.py
@@ -75,24 +75,26 @@
     return wide[0:1, :rows] + wide[half : half + 1, :rows]
 
 
-def own_kernel(images, texts, texts_one, image_unit, text_units, inverses, own_images, own_texts, sems):
+def unit_kernel(texts, text_unit):
+    text_unit[...] = unit_rows(texts[...])[0]
+
+
+def own_kernel(images, texts, image_unit, text_unit, inverses, own_images, own_texts, sems):
     copies = [
         pltpu.make_async_copy(images, own_images, sems.at[0]),
         pltpu.make_async_copy(texts, own_texts, sems.at[1]),
     ]
-    rows = texts_one.shape[0]
     for copy in copies:
         copy.start()
-    text_units[rows:, :] = unit_rows(texts_one[...])[0]
     for copy in copies:
         copy.wait()
     unit, inverse = unit_rows(own_images[...])
     image_unit[...] = unit
     inverses[...] = jnp.broadcast_to(inverse, inverses.shape)
-    text_units[:rows, :] = unit_rows(own_texts[...])[0]
-
-
-def near_kernel(knobs, image_unit, text_units, core, across, diagonal, units, coefs, losses, part_zero, part_one):
+    text_unit[...] = unit_rows(own_texts[...])[0]
+
+
+def near_kernel(knobs, image_unit, text_unit, unit_one, core, across, diagonal, units, text_units, coefs, losses, part_zero, part_one):
     rows = image_unit.shape[0]
     units[:rows, :] = image_unit[...]
     for place, block in ((1, core), (2, across), (3, diagonal)):
@@ -102,8 +104,9 @@
     shape = (rows, everything.shape[0])
     positive = lax.broadcasted_iota(jnp.int32, shape, 0) == lax.broadcasted_iota(jnp.int32, shape, 1)
     total = None
-    for step, part in enumerate((part_zero, part_one)):
-        unit = text_units[step * rows : (step + 1) * rows, :]
+    for step, (block, part) in enumerate(((text_unit, part_zero), (unit_one, part_one))):
+        unit = block[...]
+        text_units[step * rows : (step + 1) * rows, :] = unit
         loss, coef = pair_terms(unit, everything, scale, offset, positive if step == 0 else None)
         coefs[step * rows : (step + 1) * rows, :] = coef
         part[...] = jnp.dot(coef, everything, preferred_element_type=F32).astype(BF16)
@@ -142,26 +145,25 @@
     part_two[...] = jnp.dot(coef, units[...], preferred_element_type=F32)
 
 
-def pair_kernel(kept, losses, from_top, from_low, to_across):
+def pair_kernel(kept, losses, from_top, from_low, to_across, loss_across):
     rows = kept.shape[1]
     half = rows // 2
     to_across[:half, :] = (kept[1, :half] + from_top[...].astype(F32)).astype(BF16)
-    to_across[half:rows, :] = (kept[1, half:] + from_low[:half, :].astype(F32)).astype(BF16)
-    loss = losses[:, 2 * rows : 3 * rows] + decoded_loss(from_low[half : half + LOSS_ROWS, :], rows)
-    to_across[rows:, :] = coded_loss(loss, kept.shape[2])
-
-
-def last_kernel(units, inverses, kept, losses, from_core, from_low, from_across, image_grad, row_loss):
+    to_across[half:, :] = (kept[1, half:] + from_low[:half, :].astype(F32)).astype(BF16)
+    loss_across[...] = losses[:, 2 * rows : 3 * rows] + decoded_loss(from_low[half : half + LOSS_ROWS, :], rows)
+
+
+def last_kernel(from_across, from_core, loss_across, from_low, units, inverses, kept, losses, image_grad, row_loss):
     rows = image_grad.shape[0]
-    grad = kept[0] + from_core[...].astype(F32) + from_across[:rows, :].astype(F32)
+    grad = kept[0] + from_core[...].astype(F32) + from_across[...].astype(F32)
     wide = units[:rows, :].astype(F32)
     along = jnp.sum(wide * grad, axis=1, keepdims=True)
     image_grad[...] = inverses[:, 0:1] * (grad - wide * along)
-    loss = losses[:, :rows] + decoded_loss(from_low[rows // 2 + LOSS_ROWS :, :], rows) + decoded_loss(from_across[rows:, :], rows)
+    loss = losses[:, :rows] + loss_across[...] + decoded_loss(from_low[rows // 2 + LOSS_ROWS :, :], rows)
     row_loss[...] = loss / (STEPS * 4 * rows)
 
 
-def text_kernel(part_two, part_one, part_zero, text_grad):
+def text_kernel(part_zero, part_one, part_two, text_grad):
     text_grad[...] = part_two[...] + part_one[...].astype(F32) + part_zero[...].astype(F32)
 
 
@@ -184,10 +186,9 @@
 def shards(images, texts, log_scale, bias):
     rows, width = images.shape
     span = rows * lax.axis_size("grp")
-    tall = rows + LOSS_ROWS
     half = lax.axis_size("blk") // 2
-    first_flips = (half - 1,)
-    second_flips = (0,)
+    first_flips = (half - 2, half - 1)
+    second_flips = (half - 1, 0)
     made = jax.ShapeDtypeStruct
     texts_one = passed_along(texts, first_flips)
     across = swapped(images, 2)
@@ -198,30 +199,31 @@
     across, knobs = lax.optimization_barrier((across, knobs))
     diagonal = swapped(across, 1)
     matmul = 2 * rows * span * width
-    image_unit, text_units, inverses = call(
+    (unit_one,) = call(unit_kernel, "next_units", (made((rows, width), BF16),), (texts_one,), 0, 30 * matmul)
+    image_unit, text_unit, inverses = call(
         own_kernel,
         "own_units",
-        (made((rows, width), BF16), made((2 * rows, width), BF16), made((rows, 128), F32)),
+        (made((rows, width), BF16), made((rows, width), BF16), made((rows, 128), F32)),
         (
             pltpu.with_memory_space_constraint(images, pltpu.HBM),
             pltpu.with_memory_space_constraint(texts, pltpu.HBM),
-            texts_one,
         ),
         2,
-        30 * matmul,
+        0 * matmul,
         (pltpu.VMEM((rows, width), BF16), pltpu.VMEM((rows, width), BF16), pltpu.SemaphoreType.DMA((2,))),
     )
-    units, coefs, losses, part_zero, part_one = call(
+    units, text_units, coefs, losses, part_zero, part_one = call(
         near_kernel,
         "near_texts",
         (
             made((span, width), BF16),
+            made((2 * rows, width), BF16),
             made((2 * rows, span), BF16),
             made((1, span), F32),
             made((rows, width), BF16),
             made((rows, width), BF16),
         ),
-        (knobs, image_unit, text_units, core, across, diagonal),
+        (knobs, image_unit, text_unit, unit_one, core, across, diagonal),
     )
     part_zero = passed_two(part_zero)
     part_one = passed_along(part_one, second_flips)
@@ -245,16 +247,22 @@
         (made((rows, width), BF16), made((2, rows, width), F32), made((rows, width), F32)),
         (units, text_units, coefs, unit_two, coef_two),
     )
-    (to_across,) = call(pair_kernel, "chip_sum", (made((tall, width), BF16),), (kept, losses, from_core_top, from_core_low))
+    to_across, loss_across = call(
+        pair_kernel,
+        "chip_sum",
+        (made((rows, width), BF16), made((1, rows), F32)),
+        (kept, losses, from_core_top, from_core_low),
+    )
     to_across, to_core_near = lax.optimization_barrier((to_across, to_core_near))
     from_across = swapped(to_across, 2)
     from_core_near = swapped(to_core_near, 1)
-    (text_grad,) = call(text_kernel, "text_sum", (made((rows, width), F32),), (part_two, part_one, part_zero), 0, 20 * matmul)
+    loss_across = swapped(loss_across, 2)
+    (text_grad,) = call(text_kernel, "text_sum", (made((rows, width), F32),), (part_zero, part_one, part_two), 0, 20 * matmul)
     image_grad, row_loss = call(
         last_kernel,
         "image_grad",
         (made((rows, width), F32), made((1, rows), F32)),
-        (units, inverses, kept, losses, from_core_near, from_core_low, from_across),
+        (from_across, from_core_near, loss_across, from_core_low, units, inverses, kept, losses),
     )
     return (row_loss.reshape(rows), image_grad, text_grad)
 

time: 66.7 us -> 64.4 us (0.966)
  waiting for transfers between devices: 18.7 us -> 14.5 us
  starting transfers between devices: 38 us -> 39.7 us
    ppermute x7 -> x8, waiting for transfers between devices: 9.73 us -> 0.44 us  [swapped(): lax.ppermute(block, 'grp', [(i, i ^ flip) for i in range(lax.axis_size('g...]
    ppermute x2, waiting for transfers between devices: 7.62 us -> 11.5 us  [passed_along(): return lax.ppermute(block, ('blk', 'grp'), route)]
    ppermute x7 -> x8, starting transfers between devices: 29.1 us -> 30.8 us  [swapped(): lax.ppermute(block, 'grp', [(i, i ^ flip) for i in range(lax.axis_size('g...]
    ppermute x2, waiting for transfers between devices: 1.35 us -> 2.52 us  [passed_two(): lax.ppermute(block, 'blk', [(i, (i + 2) % groups) for i in range(groups)])]
    pallas_call x7 -> x8, Pallas kernels: 7.29 us -> 7.43 us  [call(): pl.pallas_call(kernel, name=name, out_shape=outs, in_specs=in_specs, out_...]
  transfers between devices with their start and end apart: 11 -> 12, of which waited for: 5 -> 4; matrix products, arithmetic and copies ran while one was open for 0% -> 0% of each run, Pallas kernels for 9% -> 10%
where the time goes in v4:
time: 64.4 us; the launch traced here: 63.9 us
  starting transfers between devices  39.7 us (62%)
  waiting for transfers between devices  14.5 us (23%)
  Pallas kernels  7.43 us (12%)
  between operations  2.13 us (3%)
    ppermute x8, starting transfers between devices, swapped(): lax.ppermute(block, 'grp', [(i, i ^ flip) for i in range(lax.axis_size('g...  30.8 us
    ppermute x2, waiting for transfers between devices, passed_along(): return lax.ppermute(block, ('blk', 'grp'), route)  11.5 us
    pallas_call x8, Pallas kernels, call(): pl.pallas_call(kernel, name=name, out_shape=outs, in_specs=in_specs, out_...  7.43 us
    ppermute x2, starting transfers between devices, passed_along(): return lax.ppermute(block, ('blk', 'grp'), route)  5.04 us
    ppermute x2, starting transfers between devices, passed_two(): lax.ppermute(block, 'blk', [(i, (i + 2) % groups) for i in range(groups)])  3.84 us
    ppermute x2, waiting for transfers between devices, passed_two(): lax.ppermute(block, 'blk', [(i, (i + 2) % groups) for i in range(groups)])  2.52 us
  transfers between devices with their start and end apart: 12, of which 4 were waited for; matrix products, arithmetic and copies ran while one was open for 0% of the time, Pallas kernels for 10%

profile of v4, /device:TPU:1, one launch (start us, length us, event | category | flops | bytes accessed | tf_op | source)
XLA Modules:
  0.0 63.9 jit_solution(13648709162609224560)
XLA Ops:
  0.6 4.0 %collective-permute-start = (bf16[128,1152]{1,0:T(8,128)(2,1)}, bf16[128,1152]{1,0:T(8,128)(2,1)S(1)}, u32[]{:S(2)}, u32[]{:S(2)}) collective-permute-start(bf16[128,1152]{1,0:T(8,128)(2,1)} %images.1), channel_id=1, source_target_pairs={{0,2},{1,3},{2,0},{3,1},{4,6},{5,7},{6,4},{7,5},{8,10},{9,11},{10,... | collective-permute-start | bytes 884744 | tf_op jit(solution)/shard_map/ppermute | solution.py:32
  4.7 3.1 %collective-permute-start.1 = (bf16[128,1152]{1,0:T(8,128)(2,1)}, bf16[128,1152]{1,0:T(8,128)(2,1)S(1)}, u32[]{:S(2)}, u32[]{:S(2)}) collective-permute-start(bf16[128,1152]{1,0:T(8,128)(2,1)} %texts.1), channel_id=1, source_target_pairs={{0,4},{1,5},{2,6},{3,7},{4,8},{5,9},{6,10},{7,11},{8,12},{9,13},{1... | collective-permute-start | bytes 884744 | tf_op jit(solution)/shard_map/ppermute | solution.py:23
  7.8 12.7 %collective-permute-start.2 = (bf16[128,1152]{1,0:T(8,128)(2,1)}, bf16[128,1152]{1,0:T(8,128)(2,1)S(1)}, u32[]{:S(2)}, u32[]{:S(2)}) collective-permute-start(bf16[128,1152]{1,0:T(8,128)(2,1)} %images.1), channel_id=1, source_target_pairs={{0,1},{1,0},{2,3},{3,2},{4,5},{5,4},{6,7},{7,6},{8,9},{9,8},{10,11... | collective-permute-start | bytes 884744 | tf_op jit(solution)/shard_map/ppermute | solution.py:32
  20.6 1.9 %collective-permute-start.4 = (bf16[128,1152]{1,0:T(8,128)(2,1)}, bf16[128,1152]{1,0:T(8,128)(2,1)S(1)}, u32[]{:S(2)}, u32[]{:S(2)}) collective-permute-start(bf16[128,1152]{1,0:T(8,128)(2,1)} %texts.1), channel_id=1, source_target_pairs={{0,8},{4,12},{8,16},{12,20},{16,24},{20,28},{24,32},{28,36},{32,40... | collective-permute-start | bytes 884744 | tf_op jit(solution)/shard_map/ppermute | solution.py:28
  22.5 1.3 %own_units.1 = (bf16[128,1152]{1,0:T(8,128)(2,1)S(1)}, bf16[128,1152]{1,0:T(8,128)(2,1)S(1)}, f32[128,128]{1,0:T(8,128)S(1)}) custom-call(bf16[128,1152]{1,0:T(8,128)(2,1)} %images.1, bf16[128,1152]{1,0:T(8,128)(2,1)} %texts.1), custom_call_target="tpu_custom_call" | custom-call | bytes 1245184 | tf_op jit(solution)/shard_map/own_units/pallas_call | solution.py:174
  25.1 0.1 maximum_bitcast_fusion
  25.2 0.1 broadcast_in_dim.8.knobs
  25.2 1.9 %collective-permute-start.3 = (bf16[128,1152]{1,0:T(8,128)(2,1)S(1)}, bf16[128,1152]{1,0:T(8,128)(2,1)S(1)}, u32[]{:S(2)}, u32[]{:S(2)}) collective-permute-start(bf16[128,1152]{1,0:T(8,128)(2,1)S(1)} %collective-permute-done.across), channel_id=1, source_target_pairs={{0,1},{1,0},{2,3},{3,2},{4,5},{5,4},{6,7},{7,6},{8,9},{9,8},{10,11... | collective-permute-start | bytes 884744 | tf_op jit(solution)/shard_map/ppermute | solution.py:32
  27.2 6.3 %collective-permute-done.1.texts = bf16[128,1152]{1,0:T(8,128)(2,1)S(1)} collective-permute-done((bf16[128,1152]{1,0:T(8,128)(2,1)}, bf16[128,1152]{1,0:T(8,128)(2,1)S(1)}, u32[]{:S(2)}, u32[]{:S(2)}) %collective-permute-start.1) | collective-permute-done | bytes 294944 | tf_op jit(solution)/shard_map/ppermute | solution.py:23
  33.5 0.1 next_units.1.unit_one
  33.7 0.0 collective-permute-done.2.core
  33.7 0.0 collective-permute-done.3.diagonal
  33.7 2.0 %near_texts.1 = (bf16[512,1152]{1,0:T(8,128)(2,1)S(1)}, bf16[256,1152]{1,0:T(8,128)(2,1)S(1)}, bf16[256,512]{1,0:T(8,128)(2,1)S(1)}, f32[1,512]{1,0:T(1,128)S(1)...) custom-call(f32[2,512]{1,0:T(2,128)S(1)} %broadcast_in_dim.8.knobs, ...), custom_call_target="tpu_custom_call" | custom-call | bytes 4397056 | tf_op jit(solution)/shard_map/near_texts/pallas_call | solution.py:174
  35.6 1.9 %collective-permute-start.10 = (bf16[128,1152]{1,0:T(8,128)(2,1)S(1)}, bf16[128,1152]{1,0:T(8,128)(2,1)S(1)}, u32[]{:S(2)}, u32[]{:S(2)}) collective-permute-start(bf16[128,1152]{1,0:T(8,128)(2,1)S(1)} %get-tuple-element.50), channel_id=1, source_target_pairs={{0,8},{4,12},{8,16},{12,20},{16,24},{20,28},{24,32},{28,36},{32,40... | collective-permute-start | bytes 884744 | tf_op jit(solution)/shard_map/ppermute | solution.py:28
  37.6 1.9 %collective-permute-start.11 = (bf16[128,1152]{1,0:T(8,128)(2,1)S(1)}, bf16[128,1152]{1,0:T(8,128)(2,1)S(1)}, u32[]{:S(2)}, u32[]{:S(2)}) collective-permute-start(bf16[128,1152]{1,0:T(8,128)(2,1)S(1)} %get-tuple-element.51), channel_id=1, source_target_pairs={{0,6},{1,7},{2,4},{3,5},{4,8},{5,9},{6,10},{7,11},{8,12},{9,13},{1... | collective-permute-start | bytes 884744 | tf_op jit(solution)/shard_map/ppermute | solution.py:23
  39.5 2.5 %collective-permute-done.4.texts_two = bf16[128,1152]{1,0:T(8,128)(2,1)S(1)} collective-permute-done((bf16[128,1152]{1,0:T(8,128)(2,1)}, bf16[128,1152]{1,0:T(8,128)(2,1)S(1)}, u32[]{:S(2)}, u32[]{:S(2)}) %collective-permute-start.4) | collective-permute-done | bytes 294944 | tf_op jit(solution)/shard_map/ppermute | solution.py:28
  42.0 1.1 %far_texts.1 = (bf16[128,512]{1,0:T(8,128)(2,1)S(1)}, bf16[128,1152]{1,0:T(8,128)(2,1)S(1)}, f32[1,512]{1,0:T(1,128)S(1)}, bf16[64,1152]{1,0:T(8,128)(2,1)S(1)}, bf16[96,1152]{1,0:T(8,128)(2,1)S(1)}) custom-call(f32[2,512]{1,0:T(2,128)S(1)} %broadcast_in_dim.8.knobs, bf16[512,1152]{1,0:T(8,128)(2,1)S(1)} %get-tuple-element.32.units, ...), custom_call_target="tpu_custom_call" | custom-call | bytes 3129344 | tf_op jit(solution)/shard_map/far_texts/pallas_call | solution.py:174
  43.1 2.6 %collective-permute-start.6 = (bf16[96,1152]{1,0:T(8,128)(2,1)S(1)}, bf16[96,1152]{1,0:T(8,128)(2,1)S(1)}, u32[]{:S(2)}, u32[]{:S(2)}) collective-permute-start(bf16[96,1152]{1,0:T(8,128)(2,1)S(1)} %get-tuple-element.41), channel_id=1, source_target_pairs={{0,1},{1,0},{2,3},{3,2},{4,5},{5,4},{6,7},{7,6},{8,9},{9,8},{10,11... | collective-permute-start | bytes 663560 | tf_op jit(solution)/shard_map/ppermute | solution.py:32
  45.7 1.9 %collective-permute-start.5 = (bf16[64,1152]{1,0:T(8,128)(2,1)S(1)}, bf16[64,1152]{1,0:T(8,128)(2,1)S(1)}, u32[]{:S(2)}, u32[]{:S(2)}) collective-permute-start(bf16[64,1152]{1,0:T(8,128)(2,1)S(1)} %get-tuple-element.40), channel_id=1, source_target_pairs={{0,1},{1,0},{2,3},{3,2},{4,5},{5,4},{6,7},{7,6},{8,9},{9,8},{10,11... | collective-permute-start | bytes 442376 | tf_op jit(solution)/shard_map/ppermute | solution.py:32
  47.6 0.9 %image_parts.1 = (bf16[128,1152]{1,0:T(8,128)(2,1)S(1)}, f32[2,128,1152]{2,1,0:T(8,128)S(1)}, f32[128,1152]{1,0:T(8,128)S(1)}) custom-call(bf16[512,1152]{1,0:T(8,128)(2,1)S(1)} %get-tuple-element.32.units, bf16[256,1152]{1,0:T(8,128)(2,1)S(1)} %get-tuple-element.33.text_units, bf16[256,512]{1,0:T(8,128)(2,1)S(1)} %get-tuple-element.34.coefs, ...), custom_call_target="tpu_custom_call" | custom-call | bytes 4521984 | tf_op jit(solution)/shard_map/image_parts/pallas_call | solution.py:174
  48.5 0.4 collective-permute-done.5.from_top
  49.0 0.1 chip_sum.1
  49.0 2.3 %collective-permute-start.7 = (bf16[128,1152]{1,0:T(8,128)(2,1)S(1)}, bf16[128,1152]{1,0:T(8,128)(2,1)S(1)}, u32[]{:S(2)}, u32[]{:S(2)}) collective-permute-start(bf16[128,1152]{1,0:T(8,128)(2,1)S(1)} %get-tuple-element.44), channel_id=1, source_target_pairs={{0,2},{1,3},{2,0},{3,1},{4,6},{5,7},{6,4},{7,5},{8,10},{9,11},{10,... | collective-permute-start | bytes 884744 | tf_op jit(solution)/shard_map/ppermute | solution.py:32
  51.4 2.3 %collective-permute-start.8 = (bf16[128,1152]{1,0:T(8,128)(2,1)S(1)}, bf16[128,1152]{1,0:T(8,128)(2,1)S(1)}, u32[]{:S(2)}, u32[]{:S(2)}) collective-permute-start(bf16[128,1152]{1,0:T(8,128)(2,1)S(1)} %get-tuple-element.45), channel_id=1, source_target_pairs={{0,1},{1,0},{2,3},{3,2},{4,5},{5,4},{6,7},{7,6},{8,9},{9,8},{10,11... | collective-permute-start | bytes 884744 | tf_op jit(solution)/shard_map/ppermute | solution.py:32
  53.7 3.0 %collective-permute-start.9 = (f32[1,128]{1,0:T(1,128)S(1)}, f32[1,128]{1,0:T(1,128)S(1)}, u32[]{:S(2)}, u32[]{:S(2)}) collective-permute-start(f32[1,128]{1,0:T(1,128)S(1)} %get-tuple-element.46), channel_id=1, source_target_pairs={{0,2},{1,3},{2,0},{3,1},{4,6},{5,7},{6,4},{7,5},{8,10},{9,11},{10,... | collective-permute-start | bytes 1544 | tf_op jit(solution)/shard_map/ppermute | solution.py:32
  56.7 0.0 collective-permute-done.10.part_zero
  56.7 5.2 %collective-permute-done.11.part_one = bf16[128,1152]{1,0:T(8,128)(2,1)S(1)} collective-permute-done((bf16[128,1152]{1,0:T(8,128)(2,1)S(1)}, bf16[128,1152]{1,0:T(8,128)(2,1)S(1)}, u32[]{:S(2)}, u32[]{:S(2)}) %collective-permute-start.11) | collective-permute-done | bytes 294944 | tf_op jit(solution)/shard_map/ppermute | solution.py:23
  61.9 0.9 %text_sum.1 = f32[128,1152]{1,0:T(8,128)} custom-call(bf16[128,1152]{1,0:T(8,128)(2,1)S(1)} %collective-permute-done.10.part_zero, bf16[128,1152]{1,0:T(8,128)(2,1)S(1)} %collective-permute-done.11.part_one, f32[128,1152]{1,0:T(8,128)S(1)} %get-tuple-element.52.part_two), custom_call_target="tpu_custom_call" | custom-call | flops 3019898880 | bytes 1769472 | tf_op jit(solution)/shard_map/text_sum/pallas_call | solution.py:174
  62.8 0.0 collective-permute-done.9.loss_across
  62.8 0.0 collective-permute-done.7.from_across
  62.8 0.0 collective-permute-done.8.from_core
  62.8 1.1 %image_grad.1 = (f32[128,1152]{1,0:T(8,128)}, f32[1,128]{1,0:T(1,128)}) custom-call(bf16[128,1152]{1,0:T(8,128)(2,1)S(1)} %collective-permute-done.7.from_across, bf16[128,1152]{1,0:T(8,128)(2,1)S(1)} %collective-permute-done.8.from_core, f32[1,128]{1,0:T(1,128)S(1)} %collective-permute-done.9.loss_across, ...), custom_call_target="tpu_custom_call" | custom-call | bytes 3828736 | tf_op jit(solution)/shard_map/image_grad/pallas_call | solution.py:174
  (2 shorter events, 0.0 us)
Async XLA Ops:
  0.6 24.5 %collective-permute-start = (bf16[128,1152]{1,0:T(8,128)(2,1)}, bf16[128,1152]{1,0:T(8,128)(2,1)S(1)}, u32[]{:S(2)}, u32[]{:S(2)}) collective-permute-start(bf16[128,1152]{1,0:T(8,128)(2,1)} %images.1), channel_id=1, source_target_pairs={{0,2},{1,3},{2,0},{3,1},{4,6},{5,7},{6,4},{7,5},{8,10},{9,11},{10,... | collective-permute-start | bytes 884744 | tf_op jit(solution)/shard_map/ppermute | solution.py:32
  4.7 28.8 %collective-permute-start.1 = (bf16[128,1152]{1,0:T(8,128)(2,1)}, bf16[128,1152]{1,0:T(8,128)(2,1)S(1)}, u32[]{:S(2)}, u32[]{:S(2)}) collective-permute-start(bf16[128,1152]{1,0:T(8,128)(2,1)} %texts.1), channel_id=1, source_target_pairs={{0,4},{1,5},{2,6},{3,7},{4,8},{5,9},{6,10},{7,11},{8,12},{9,13},{1... | collective-permute-start | bytes 884744 | tf_op jit(solution)/shard_map/ppermute | solution.py:23
  7.8 25.9 %collective-permute-start.2 = (bf16[128,1152]{1,0:T(8,128)(2,1)}, bf16[128,1152]{1,0:T(8,128)(2,1)S(1)}, u32[]{:S(2)}, u32[]{:S(2)}) collective-permute-start(bf16[128,1152]{1,0:T(8,128)(2,1)} %images.1), channel_id=1, source_target_pairs={{0,1},{1,0},{2,3},{3,2},{4,5},{5,4},{6,7},{7,6},{8,9},{9,8},{10,11... | collective-permute-start | bytes 884744 | tf_op jit(solution)/shard_map/ppermute | solution.py:32
  20.6 21.5 %collective-permute-start.4 = (bf16[128,1152]{1,0:T(8,128)(2,1)}, bf16[128,1152]{1,0:T(8,128)(2,1)S(1)}, u32[]{:S(2)}, u32[]{:S(2)}) collective-permute-start(bf16[128,1152]{1,0:T(8,128)(2,1)} %texts.1), channel_id=1, source_target_pairs={{0,8},{4,12},{8,16},{12,20},{16,24},{20,28},{24,32},{28,36},{32,40... | collective-permute-start | bytes 884744 | tf_op jit(solution)/shard_map/ppermute | solution.py:28
  25.2 8.4 %collective-permute-start.3 = (bf16[128,1152]{1,0:T(8,128)(2,1)S(1)}, bf16[128,1152]{1,0:T(8,128)(2,1)S(1)}, u32[]{:S(2)}, u32[]{:S(2)}) collective-permute-start(bf16[128,1152]{1,0:T(8,128)(2,1)S(1)} %collective-permute-done.across), channel_id=1, source_target_pairs={{0,1},{1,0},{2,3},{3,2},{4,5},{5,4},{6,7},{7,6},{8,9},{9,8},{10,11... | collective-permute-start | bytes 884744 | tf_op jit(solution)/shard_map/ppermute | solution.py:32
  35.6 21.1 %collective-permute-start.10 = (bf16[128,1152]{1,0:T(8,128)(2,1)S(1)}, bf16[128,1152]{1,0:T(8,128)(2,1)S(1)}, u32[]{:S(2)}, u32[]{:S(2)}) collective-permute-start(bf16[128,1152]{1,0:T(8,128)(2,1)S(1)} %get-tuple-element.50), channel_id=1, source_target_pairs={{0,8},{4,12},{8,16},{12,20},{16,24},{20,28},{24,32},{28,36},{32,40... | collective-permute-start | bytes 884744 | tf_op jit(solution)/shard_map/ppermute | solution.py:28
  37.6 24.3 %collective-permute-start.11 = (bf16[128,1152]{1,0:T(8,128)(2,1)S(1)}, bf16[128,1152]{1,0:T(8,128)(2,1)S(1)}, u32[]{:S(2)}, u32[]{:S(2)}) collective-permute-start(bf16[128,1152]{1,0:T(8,128)(2,1)S(1)} %get-tuple-element.51), channel_id=1, source_target_pairs={{0,6},{1,7},{2,4},{3,5},{4,8},{5,9},{6,10},{7,11},{8,12},{9,13},{1... | collective-permute-start | bytes 884744 | tf_op jit(solution)/shard_map/ppermute | solution.py:23
  43.1 5.9 %collective-permute-start.6 = (bf16[96,1152]{1,0:T(8,128)(2,1)S(1)}, bf16[96,1152]{1,0:T(8,128)(2,1)S(1)}, u32[]{:S(2)}, u32[]{:S(2)}) collective-permute-start(bf16[96,1152]{1,0:T(8,128)(2,1)S(1)} %get-tuple-element.41), channel_id=1, source_target_pairs={{0,1},{1,0},{2,3},{3,2},{4,5},{5,4},{6,7},{7,6},{8,9},{9,8},{10,11... | collective-permute-start | bytes 663560 | tf_op jit(solution)/shard_map/ppermute | solution.py:32
  45.7 3.3 %collective-permute-start.5 = (bf16[64,1152]{1,0:T(8,128)(2,1)S(1)}, bf16[64,1152]{1,0:T(8,128)(2,1)S(1)}, u32[]{:S(2)}, u32[]{:S(2)}) collective-permute-start(bf16[64,1152]{1,0:T(8,128)(2,1)S(1)} %get-tuple-element.40), channel_id=1, source_target_pairs={{0,1},{1,0},{2,3},{3,2},{4,5},{5,4},{6,7},{7,6},{8,9},{9,8},{10,11... | collective-permute-start | bytes 442376 | tf_op jit(solution)/shard_map/ppermute | solution.py:32
  49.0 13.8 %collective-permute-start.7 = (bf16[128,1152]{1,0:T(8,128)(2,1)S(1)}, bf16[128,1152]{1,0:T(8,128)(2,1)S(1)}, u32[]{:S(2)}, u32[]{:S(2)}) collective-permute-start(bf16[128,1152]{1,0:T(8,128)(2,1)S(1)} %get-tuple-element.44), channel_id=1, source_target_pairs={{0,2},{1,3},{2,0},{3,1},{4,6},{5,7},{6,4},{7,5},{8,10},{9,11},{10,... | collective-permute-start | bytes 884744 | tf_op jit(solution)/shard_map/ppermute | solution.py:32
  51.4 11.5 %collective-permute-start.8 = (bf16[128,1152]{1,0:T(8,128)(2,1)S(1)}, bf16[128,1152]{1,0:T(8,128)(2,1)S(1)}, u32[]{:S(2)}, u32[]{:S(2)}) collective-permute-start(bf16[128,1152]{1,0:T(8,128)(2,1)S(1)} %get-tuple-element.45), channel_id=1, source_target_pairs={{0,1},{1,0},{2,3},{3,2},{4,5},{5,4},{6,7},{7,6},{8,9},{9,8},{10,11... | collective-permute-start | bytes 884744 | tf_op jit(solution)/shard_map/ppermute | solution.py:32
  53.7 9.1 %collective-permute-start.9 = (f32[1,128]{1,0:T(1,128)S(1)}, f32[1,128]{1,0:T(1,128)S(1)}, u32[]{:S(2)}, u32[]{:S(2)}) collective-permute-start(f32[1,128]{1,0:T(1,128)S(1)} %get-tuple-element.46), channel_id=1, source_target_pairs={{0,2},{1,3},{2,0},{3,1},{4,6},{5,7},{6,4},{7,5},{8,10},{9,11},{10,... | collective-permute-start | bytes 1544 | tf_op jit(solution)/shard_map/ppermute | solution.py:32

commit v5 on v4

--- a/solution.py
+++ b/solution.py
@@ -187,8 +187,8 @@
     rows, width = images.shape
     span = rows * lax.axis_size("grp")
     half = lax.axis_size("blk") // 2
-    first_flips = (half - 2, half - 1)
-    second_flips = (half - 1, 0)
+    first_flips = (half - 2,)
+    second_flips = (half - 1,)
     made = jax.ShapeDtypeStruct
     texts_one = passed_along(texts, first_flips)
     across = swapped(images, 2)

time: 64.4 us -> 63.4 us (0.984)
  waiting for transfers between devices: 14.5 us -> 12.8 us
  starting transfers between devices: 39.7 us -> 40.5 us
    ppermute x2, waiting for transfers between devices: 11.5 us -> 10.5 us  [passed_along(): return lax.ppermute(block, ('blk', 'grp'), route)]
    ppermute x8, starting transfers between devices: 30.8 us -> 31.6 us  [swapped(): lax.ppermute(block, 'grp', [(i, i ^ flip) for i in range(lax.axis_size('g...]
    ppermute x2, waiting for transfers between devices: 2.52 us -> 1.82 us  [passed_two(): lax.ppermute(block, 'blk', [(i, (i + 2) % groups) for i in range(groups)])]
where the time goes in v5:
time: 63.4 us; the launch traced here: 62.9 us
  starting transfers between devices  40.5 us (64%)
  waiting for transfers between devices  12.8 us (20%)
  Pallas kernels  7.4 us (12%)
  between operations  2.13 us (3%)
    ppermute x8, starting transfers between devices, swapped(): lax.ppermute(block, 'grp', [(i, i ^ flip) for i in range(lax.axis_size('g...  31.6 us
    ppermute x2, waiting for transfers between devices, passed_along(): return lax.ppermute(block, ('blk', 'grp'), route)  10.5 us
    pallas_call x8, Pallas kernels, call(): pl.pallas_call(kernel, name=name, out_shape=outs, in_specs=in_specs, out_...  7.4 us
    ppermute x2, starting transfers between devices, passed_along(): return lax.ppermute(block, ('blk', 'grp'), route)  5.04 us
    ppermute x2, starting transfers between devices, passed_two(): lax.ppermute(block, 'blk', [(i, (i + 2) % groups) for i in range(groups)])  3.84 us
    ppermute x2, waiting for transfers between devices, passed_two(): lax.ppermute(block, 'blk', [(i, (i + 2) % groups) for i in range(groups)])  1.82 us
  transfers between devices with their start and end apart: 12, of which 4 were waited for; matrix products, arithmetic and copies ran while one was open for 0% of the time, Pallas kernels for 10%

profile of v5, /device:TPU:1, one launch (start us, length us, event | category | flops | bytes accessed | tf_op | source)
XLA Modules:
  0.0 62.9 jit_solution(11628262302248665036)
XLA Ops:
  0.6 4.0 %collective-permute-start = (bf16[128,1152]{1,0:T(8,128)(2,1)}, bf16[128,1152]{1,0:T(8,128)(2,1)S(1)}, u32[]{:S(2)}, u32[]{:S(2)}) collective-permute-start(bf16[128,1152]{1,0:T(8,128)(2,1)} %images.1), channel_id=1, source_target_pairs={{0,2},{1,3},{2,0},{3,1},{4,6},{5,7},{6,4},{7,5},{8,10},{9,11},{10,... | collective-permute-start | bytes 884744 | tf_op jit(solution)/shard_map/ppermute | solution.py:32
  4.7 3.1 %collective-permute-start.1 = (bf16[128,1152]{1,0:T(8,128)(2,1)}, bf16[128,1152]{1,0:T(8,128)(2,1)S(1)}, u32[]{:S(2)}, u32[]{:S(2)}) collective-permute-start(bf16[128,1152]{1,0:T(8,128)(2,1)} %texts.1), channel_id=1, source_target_pairs={{0,4},{1,5},{2,6},{3,7},{4,8},{5,9},{6,10},{7,11},{8,12},{9,13},{1... | collective-permute-start | bytes 884744 | tf_op jit(solution)/shard_map/ppermute | solution.py:23
  7.8 12.7 %collective-permute-start.2 = (bf16[128,1152]{1,0:T(8,128)(2,1)}, bf16[128,1152]{1,0:T(8,128)(2,1)S(1)}, u32[]{:S(2)}, u32[]{:S(2)}) collective-permute-start(bf16[128,1152]{1,0:T(8,128)(2,1)} %images.1), channel_id=1, source_target_pairs={{0,1},{1,0},{2,3},{3,2},{4,5},{5,4},{6,7},{7,6},{8,9},{9,8},{10,11... | collective-permute-start | bytes 884744 | tf_op jit(solution)/shard_map/ppermute | solution.py:32
  20.6 1.9 %collective-permute-start.4 = (bf16[128,1152]{1,0:T(8,128)(2,1)}, bf16[128,1152]{1,0:T(8,128)(2,1)S(1)}, u32[]{:S(2)}, u32[]{:S(2)}) collective-permute-start(bf16[128,1152]{1,0:T(8,128)(2,1)} %texts.1), channel_id=1, source_target_pairs={{0,8},{4,12},{8,16},{12,20},{16,24},{20,28},{24,32},{28,36},{32,40... | collective-permute-start | bytes 884744 | tf_op jit(solution)/shard_map/ppermute | solution.py:28
  22.5 1.3 %own_units.1 = (bf16[128,1152]{1,0:T(8,128)(2,1)S(1)}, bf16[128,1152]{1,0:T(8,128)(2,1)S(1)}, f32[128,128]{1,0:T(8,128)S(1)}) custom-call(bf16[128,1152]{1,0:T(8,128)(2,1)} %images.1, bf16[128,1152]{1,0:T(8,128)(2,1)} %texts.1), custom_call_target="tpu_custom_call" | custom-call | bytes 1245184 | tf_op jit(solution)/shard_map/own_units/pallas_call | solution.py:174
  25.1 0.1 maximum_bitcast_fusion
  25.2 0.0 collective-permute-done.across
  25.2 0.1 broadcast_in_dim.8.knobs
  25.2 1.9 %collective-permute-start.3 = (bf16[128,1152]{1,0:T(8,128)(2,1)S(1)}, bf16[128,1152]{1,0:T(8,128)(2,1)S(1)}, u32[]{:S(2)}, u32[]{:S(2)}) collective-permute-start(bf16[128,1152]{1,0:T(8,128)(2,1)S(1)} %collective-permute-done.across), channel_id=1, source_target_pairs={{0,1},{1,0},{2,3},{3,2},{4,5},{5,4},{6,7},{7,6},{8,9},{9,8},{10,11... | collective-permute-start | bytes 884744 | tf_op jit(solution)/shard_map/ppermute | solution.py:32
  27.2 7.1 %collective-permute-done.1.texts = bf16[128,1152]{1,0:T(8,128)(2,1)S(1)} collective-permute-done((bf16[128,1152]{1,0:T(8,128)(2,1)}, bf16[128,1152]{1,0:T(8,128)(2,1)S(1)}, u32[]{:S(2)}, u32[]{:S(2)}) %collective-permute-start.1) | collective-permute-done | bytes 294944 | tf_op jit(solution)/shard_map/ppermute | solution.py:23
  34.2 0.1 next_units.1.unit_one
  34.4 0.0 collective-permute-done.3.diagonal
  34.4 1.9 %near_texts.1 = (bf16[512,1152]{1,0:T(8,128)(2,1)S(1)}, bf16[256,1152]{1,0:T(8,128)(2,1)S(1)}, bf16[256,512]{1,0:T(8,128)(2,1)S(1)}, f32[1,512]{1,0:T(1,128)S(1)...) custom-call(f32[2,512]{1,0:T(2,128)S(1)} %broadcast_in_dim.8.knobs, ...), custom_call_target="tpu_custom_call" | custom-call | bytes 4397056 | tf_op jit(solution)/shard_map/near_texts/pallas_call | solution.py:174
  36.3 1.9 %collective-permute-start.10 = (bf16[128,1152]{1,0:T(8,128)(2,1)S(1)}, bf16[128,1152]{1,0:T(8,128)(2,1)S(1)}, u32[]{:S(2)}, u32[]{:S(2)}) collective-permute-start(bf16[128,1152]{1,0:T(8,128)(2,1)S(1)} %get-tuple-element.50), channel_id=1, source_target_pairs={{0,8},{4,12},{8,16},{12,20},{16,24},{20,28},{24,32},{28,36},{32,40... | collective-permute-start | bytes 884744 | tf_op jit(solution)/shard_map/ppermute | solution.py:28
  38.3 1.9 %collective-permute-start.11 = (bf16[128,1152]{1,0:T(8,128)(2,1)S(1)}, bf16[128,1152]{1,0:T(8,128)(2,1)S(1)}, u32[]{:S(2)}, u32[]{:S(2)}) collective-permute-start(bf16[128,1152]{1,0:T(8,128)(2,1)S(1)} %get-tuple-element.51), channel_id=1, source_target_pairs={{0,4},{1,5},{2,6},{3,7},{4,8},{5,9},{6,10},{7,11},{8,12},{9,13},{1... | collective-permute-start | bytes 884744 | tf_op jit(solution)/shard_map/ppermute | solution.py:23
  40.2 1.8 %collective-permute-done.4.texts_two = bf16[128,1152]{1,0:T(8,128)(2,1)S(1)} collective-permute-done((bf16[128,1152]{1,0:T(8,128)(2,1)}, bf16[128,1152]{1,0:T(8,128)(2,1)S(1)}, u32[]{:S(2)}, u32[]{:S(2)}) %collective-permute-start.4) | collective-permute-done | bytes 294944 | tf_op jit(solution)/shard_map/ppermute | solution.py:28
  42.0 1.1 %far_texts.1 = (bf16[128,512]{1,0:T(8,128)(2,1)S(1)}, bf16[128,1152]{1,0:T(8,128)(2,1)S(1)}, f32[1,512]{1,0:T(1,128)S(1)}, bf16[64,1152]{1,0:T(8,128)(2,1)S(1)}, bf16[96,1152]{1,0:T(8,128)(2,1)S(1)}) custom-call(f32[2,512]{1,0:T(2,128)S(1)} %broadcast_in_dim.8.knobs, bf16[512,1152]{1,0:T(8,128)(2,1)S(1)} %get-tuple-element.32.units, ...), custom_call_target="tpu_custom_call" | custom-call | bytes 3129344 | tf_op jit(solution)/shard_map/far_texts/pallas_call | solution.py:174
  43.1 3.3 %collective-permute-start.6 = (bf16[96,1152]{1,0:T(8,128)(2,1)S(1)}, bf16[96,1152]{1,0:T(8,128)(2,1)S(1)}, u32[]{:S(2)}, u32[]{:S(2)}) collective-permute-start(bf16[96,1152]{1,0:T(8,128)(2,1)S(1)} %get-tuple-element.41), channel_id=1, source_target_pairs={{0,1},{1,0},{2,3},{3,2},{4,5},{5,4},{6,7},{7,6},{8,9},{9,8},{10,11... | collective-permute-start | bytes 663560 | tf_op jit(solution)/shard_map/ppermute | solution.py:32
  46.4 1.9 %collective-permute-start.5 = (bf16[64,1152]{1,0:T(8,128)(2,1)S(1)}, bf16[64,1152]{1,0:T(8,128)(2,1)S(1)}, u32[]{:S(2)}, u32[]{:S(2)}) collective-permute-start(bf16[64,1152]{1,0:T(8,128)(2,1)S(1)} %get-tuple-element.40), channel_id=1, source_target_pairs={{0,1},{1,0},{2,3},{3,2},{4,5},{5,4},{6,7},{7,6},{8,9},{9,8},{10,11... | collective-permute-start | bytes 442376 | tf_op jit(solution)/shard_map/ppermute | solution.py:32
  48.4 0.9 %image_parts.1 = (bf16[128,1152]{1,0:T(8,128)(2,1)S(1)}, f32[2,128,1152]{2,1,0:T(8,128)S(1)}, f32[128,1152]{1,0:T(8,128)S(1)}) custom-call(bf16[512,1152]{1,0:T(8,128)(2,1)S(1)} %get-tuple-element.32.units, bf16[256,1152]{1,0:T(8,128)(2,1)S(1)} %get-tuple-element.33.text_units, bf16[256,512]{1,0:T(8,128)(2,1)S(1)} %get-tuple-element.34.coefs, ...), custom_call_target="tpu_custom_call" | custom-call | bytes 4521984 | tf_op jit(solution)/shard_map/image_parts/pallas_call | solution.py:174
  49.3 0.4 collective-permute-done.5.from_top
  49.7 0.0 collective-permute-done.6.from_low
  49.7 0.1 chip_sum.1
  49.8 1.9 %collective-permute-start.7 = (bf16[128,1152]{1,0:T(8,128)(2,1)S(1)}, bf16[128,1152]{1,0:T(8,128)(2,1)S(1)}, u32[]{:S(2)}, u32[]{:S(2)}) collective-permute-start(bf16[128,1152]{1,0:T(8,128)(2,1)S(1)} %get-tuple-element.44), channel_id=1, source_target_pairs={{0,2},{1,3},{2,0},{3,1},{4,6},{5,7},{6,4},{7,5},{8,10},{9,11},{10,... | collective-permute-start | bytes 884744 | tf_op jit(solution)/shard_map/ppermute | solution.py:32
  51.7 2.1 %collective-permute-start.8 = (bf16[128,1152]{1,0:T(8,128)(2,1)S(1)}, bf16[128,1152]{1,0:T(8,128)(2,1)S(1)}, u32[]{:S(2)}, u32[]{:S(2)}) collective-permute-start(bf16[128,1152]{1,0:T(8,128)(2,1)S(1)} %get-tuple-element.45), channel_id=1, source_target_pairs={{0,1},{1,0},{2,3},{3,2},{4,5},{5,4},{6,7},{7,6},{8,9},{9,8},{10,11... | collective-permute-start | bytes 884744 | tf_op jit(solution)/shard_map/ppermute | solution.py:32
  53.8 3.7 %collective-permute-start.9 = (f32[1,128]{1,0:T(1,128)S(1)}, f32[1,128]{1,0:T(1,128)S(1)}, u32[]{:S(2)}, u32[]{:S(2)}) collective-permute-start(f32[1,128]{1,0:T(1,128)S(1)} %get-tuple-element.46), channel_id=1, source_target_pairs={{0,2},{1,3},{2,0},{3,1},{4,6},{5,7},{6,4},{7,5},{8,10},{9,11},{10,... | collective-permute-start | bytes 1544 | tf_op jit(solution)/shard_map/ppermute | solution.py:32
  57.4 3.4 %collective-permute-done.11.part_one = bf16[128,1152]{1,0:T(8,128)(2,1)S(1)} collective-permute-done((bf16[128,1152]{1,0:T(8,128)(2,1)S(1)}, bf16[128,1152]{1,0:T(8,128)(2,1)S(1)}, u32[]{:S(2)}, u32[]{:S(2)}) %collective-permute-start.11) | collective-permute-done | bytes 294944 | tf_op jit(solution)/shard_map/ppermute | solution.py:23
  60.9 0.9 %text_sum.1 = f32[128,1152]{1,0:T(8,128)} custom-call(bf16[128,1152]{1,0:T(8,128)(2,1)S(1)} %collective-permute-done.10.part_zero, bf16[128,1152]{1,0:T(8,128)(2,1)S(1)} %collective-permute-done.11.part_one, f32[128,1152]{1,0:T(8,128)S(1)} %get-tuple-element.52.part_two), custom_call_target="tpu_custom_call" | custom-call | flops 3019898880 | bytes 1769472 | tf_op jit(solution)/shard_map/text_sum/pallas_call | solution.py:174
  61.8 0.0 collective-permute-done.9.loss_across
  61.8 0.0 collective-permute-done.7.from_across
  61.8 0.0 collective-permute-done.8.from_core
  61.8 1.1 %image_grad.1 = (f32[128,1152]{1,0:T(8,128)}, f32[1,128]{1,0:T(1,128)}) custom-call(bf16[128,1152]{1,0:T(8,128)(2,1)S(1)} %collective-permute-done.7.from_across, bf16[128,1152]{1,0:T(8,128)(2,1)S(1)} %collective-permute-done.8.from_core, f32[1,128]{1,0:T(1,128)S(1)} %collective-permute-done.9.loss_across, ...), custom_call_target="tpu_custom_call" | custom-call | bytes 3828736 | tf_op jit(solution)/shard_map/image_grad/pallas_call | solution.py:174
  (2 shorter events, 0.0 us)
Async XLA Ops:
  0.6 24.5 %collective-permute-start = (bf16[128,1152]{1,0:T(8,128)(2,1)}, bf16[128,1152]{1,0:T(8,128)(2,1)S(1)}, u32[]{:S(2)}, u32[]{:S(2)}) collective-permute-start(bf16[128,1152]{1,0:T(8,128)(2,1)} %images.1), channel_id=1, source_target_pairs={{0,2},{1,3},{2,0},{3,1},{4,6},{5,7},{6,4},{7,5},{8,10},{9,11},{10,... | collective-permute-start | bytes 884744 | tf_op jit(solution)/shard_map/ppermute | solution.py:32
  4.7 29.5 %collective-permute-start.1 = (bf16[128,1152]{1,0:T(8,128)(2,1)}, bf16[128,1152]{1,0:T(8,128)(2,1)S(1)}, u32[]{:S(2)}, u32[]{:S(2)}) collective-permute-start(bf16[128,1152]{1,0:T(8,128)(2,1)} %texts.1), channel_id=1, source_target_pairs={{0,4},{1,5},{2,6},{3,7},{4,8},{5,9},{6,10},{7,11},{8,12},{9,13},{1... | collective-permute-start | bytes 884744 | tf_op jit(solution)/shard_map/ppermute | solution.py:23
  7.8 26.6 %collective-permute-start.2 = (bf16[128,1152]{1,0:T(8,128)(2,1)}, bf16[128,1152]{1,0:T(8,128)(2,1)S(1)}, u32[]{:S(2)}, u32[]{:S(2)}) collective-permute-start(bf16[128,1152]{1,0:T(8,128)(2,1)} %images.1), channel_id=1, source_target_pairs={{0,1},{1,0},{2,3},{3,2},{4,5},{5,4},{6,7},{7,6},{8,9},{9,8},{10,11... | collective-permute-start | bytes 884744 | tf_op jit(solution)/shard_map/ppermute | solution.py:32
  20.6 21.5 %collective-permute-start.4 = (bf16[128,1152]{1,0:T(8,128)(2,1)}, bf16[128,1152]{1,0:T(8,128)(2,1)S(1)}, u32[]{:S(2)}, u32[]{:S(2)}) collective-permute-start(bf16[128,1152]{1,0:T(8,128)(2,1)} %texts.1), channel_id=1, source_target_pairs={{0,8},{4,12},{8,16},{12,20},{16,24},{20,28},{24,32},{28,36},{32,40... | collective-permute-start | bytes 884744 | tf_op jit(solution)/shard_map/ppermute | solution.py:28
  25.2 9.1 %collective-permute-start.3 = (bf16[128,1152]{1,0:T(8,128)(2,1)S(1)}, bf16[128,1152]{1,0:T(8,128)(2,1)S(1)}, u32[]{:S(2)}, u32[]{:S(2)}) collective-permute-start(bf16[128,1152]{1,0:T(8,128)(2,1)S(1)} %collective-permute-done.across), channel_id=1, source_target_pairs={{0,1},{1,0},{2,3},{3,2},{4,5},{5,4},{6,7},{7,6},{8,9},{9,8},{10,11... | collective-permute-start | bytes 884744 | tf_op jit(solution)/shard_map/ppermute | solution.py:32
  36.3 21.1 %collective-permute-start.10 = (bf16[128,1152]{1,0:T(8,128)(2,1)S(1)}, bf16[128,1152]{1,0:T(8,128)(2,1)S(1)}, u32[]{:S(2)}, u32[]{:S(2)}) collective-permute-start(bf16[128,1152]{1,0:T(8,128)(2,1)S(1)} %get-tuple-element.50), channel_id=1, source_target_pairs={{0,8},{4,12},{8,16},{12,20},{16,24},{20,28},{24,32},{28,36},{32,40... | collective-permute-start | bytes 884744 | tf_op jit(solution)/shard_map/ppermute | solution.py:28
  38.3 22.6 %collective-permute-start.11 = (bf16[128,1152]{1,0:T(8,128)(2,1)S(1)}, bf16[128,1152]{1,0:T(8,128)(2,1)S(1)}, u32[]{:S(2)}, u32[]{:S(2)}) collective-permute-start(bf16[128,1152]{1,0:T(8,128)(2,1)S(1)} %get-tuple-element.51), channel_id=1, source_target_pairs={{0,4},{1,5},{2,6},{3,7},{4,8},{5,9},{6,10},{7,11},{8,12},{9,13},{1... | collective-permute-start | bytes 884744 | tf_op jit(solution)/shard_map/ppermute | solution.py:23
  43.1 6.6 %collective-permute-start.6 = (bf16[96,1152]{1,0:T(8,128)(2,1)S(1)}, bf16[96,1152]{1,0:T(8,128)(2,1)S(1)}, u32[]{:S(2)}, u32[]{:S(2)}) collective-permute-start(bf16[96,1152]{1,0:T(8,128)(2,1)S(1)} %get-tuple-element.41), channel_id=1, source_target_pairs={{0,1},{1,0},{2,3},{3,2},{4,5},{5,4},{6,7},{7,6},{8,9},{9,8},{10,11... | collective-permute-start | bytes 663560 | tf_op jit(solution)/shard_map/ppermute | solution.py:32
  46.4 3.3 %collective-permute-start.5 = (bf16[64,1152]{1,0:T(8,128)(2,1)S(1)}, bf16[64,1152]{1,0:T(8,128)(2,1)S(1)}, u32[]{:S(2)}, u32[]{:S(2)}) collective-permute-start(bf16[64,1152]{1,0:T(8,128)(2,1)S(1)} %get-tuple-element.40), channel_id=1, source_target_pairs={{0,1},{1,0},{2,3},{3,2},{4,5},{5,4},{6,7},{7,6},{8,9},{9,8},{10,11... | collective-permute-start | bytes 442376 | tf_op jit(solution)/shard_map/ppermute | solution.py:32
  49.8 12.0 %collective-permute-start.7 = (bf16[128,1152]{1,0:T(8,128)(2,1)S(1)}, bf16[128,1152]{1,0:T(8,128)(2,1)S(1)}, u32[]{:S(2)}, u32[]{:S(2)}) collective-permute-start(bf16[128,1152]{1,0:T(8,128)(2,1)S(1)} %get-tuple-element.44), channel_id=1, source_target_pairs={{0,2},{1,3},{2,0},{3,1},{4,6},{5,7},{6,4},{7,5},{8,10},{9,11},{10,... | collective-permute-start | bytes 884744 | tf_op jit(solution)/shard_map/ppermute | solution.py:32
  51.7 10.1 %collective-permute-start.8 = (bf16[128,1152]{1,0:T(8,128)(2,1)S(1)}, bf16[128,1152]{1,0:T(8,128)(2,1)S(1)}, u32[]{:S(2)}, u32[]{:S(2)}) collective-permute-start(bf16[128,1152]{1,0:T(8,128)(2,1)S(1)} %get-tuple-element.45), channel_id=1, source_target_pairs={{0,1},{1,0},{2,3},{3,2},{4,5},{5,4},{6,7},{7,6},{8,9},{9,8},{10,11... | collective-permute-start | bytes 884744 | tf_op jit(solution)/shard_map/ppermute | solution.py:32
  53.8 8.0 %collective-permute-start.9 = (f32[1,128]{1,0:T(1,128)S(1)}, f32[1,128]{1,0:T(1,128)S(1)}, u32[]{:S(2)}, u32[]{:S(2)}) collective-permute-start(f32[1,128]{1,0:T(1,128)S(1)} %get-tuple-element.46), channel_id=1, source_target_pairs={{0,2},{1,3},{2,0},{3,1},{4,6},{5,7},{6,4},{7,5},{8,10},{9,11},{10,... | collective-permute-start | bytes 1544 | tf_op jit(solution)/shard_map/ppermute | solution.py:32

commit v6 on v5

--- a/solution.py
+++ b/solution.py
@@ -94,24 +94,31 @@
     text_unit[...] = unit_rows(own_texts[...])[0]
 
 
-def near_kernel(knobs, image_unit, text_unit, unit_one, core, across, diagonal, units, text_units, coefs, losses, part_zero, part_one):
+def same_kernel(knobs, image_unit, text_unit, unit_one, core, across, diagonal, units, text_units, coef_out, losses, part_zero):
     rows = image_unit.shape[0]
     units[:rows, :] = image_unit[...]
     for place, block in ((1, core), (2, across), (3, diagonal)):
         units[place * rows : (place + 1) * rows, :] = unit_rows(block[...])[0]
-    scale, offset = knobs[0:1, :], knobs[1:2, :]
+    unit = text_unit[...]
+    text_units[:rows, :] = unit
+    text_units[rows:, :] = unit_one[...]
     everything = units[...]
     shape = (rows, everything.shape[0])
     positive = lax.broadcasted_iota(jnp.int32, shape, 0) == lax.broadcasted_iota(jnp.int32, shape, 1)
-    total = None
-    for step, (block, part) in enumerate(((text_unit, part_zero), (unit_one, part_one))):
-        unit = block[...]
-        text_units[step * rows : (step + 1) * rows, :] = unit
-        loss, coef = pair_terms(unit, everything, scale, offset, positive if step == 0 else None)
-        coefs[step * rows : (step + 1) * rows, :] = coef
-        part[...] = jnp.dot(coef, everything, preferred_element_type=F32).astype(BF16)
-        total = loss if total is None else total + loss
-    losses[...] = total
+    loss, coef = pair_terms(unit, everything, knobs[0:1, :], knobs[1:2, :], positive)
+    coef_out[...] = coef
+    losses[...] = loss
+    part_zero[...] = jnp.dot(coef, everything, preferred_element_type=F32).astype(BF16)
+
+
+def next_kernel(knobs, units, text_units, coef_zero, loss_zero, coefs, losses, part_one):
+    rows = coef_zero.shape[0]
+    everything = units[...]
+    loss, coef = pair_terms(text_units[rows:, :], everything, knobs[0:1, :], knobs[1:2, :])
+    coefs[:rows, :] = coef_zero[...]
+    coefs[rows:, :] = coef
+    losses[...] = loss_zero[...] + loss
+    part_one[...] = jnp.dot(coef, everything, preferred_element_type=F32).astype(BF16)
 
 
 def image_part(coefs, text_units, coef_two, unit_two, place):
@@ -212,20 +219,25 @@
         0 * matmul,
         (pltpu.VMEM((rows, width), BF16), pltpu.VMEM((rows, width), BF16), pltpu.SemaphoreType.DMA((2,))),
     )
-    units, text_units, coefs, losses, part_zero, part_one = call(
-        near_kernel,
-        "near_texts",
+    units, text_units, coef_zero, loss_zero, part_zero = call(
+        same_kernel,
+        "same_texts",
         (
             made((span, width), BF16),
             made((2 * rows, width), BF16),
-            made((2 * rows, span), BF16),
+            made((rows, span), BF16),
             made((1, span), F32),
-            made((rows, width), BF16),
             made((rows, width), BF16),
         ),
         (knobs, image_unit, text_unit, unit_one, core, across, diagonal),
     )
     part_zero = passed_two(part_zero)
+    coefs, losses, part_one = call(
+        next_kernel,
+        "next_texts",
+        (made((2 * rows, span), BF16), made((1, span), F32), made((rows, width), BF16)),
+        (knobs, units, text_units, coef_zero, loss_zero),
+    )
     part_one = passed_along(part_one, second_flips)
     coef_two, unit_two, losses, to_core_top, to_core_low = call(
         far_kernel,

time: 63.4 us -> 62.5 us (0.986)
  waiting for transfers between devices: 12.8 us -> 11.5 us
    ppermute x2, waiting for transfers between devices: 10.5 us -> 9.48 us  [passed_along(): return lax.ppermute(block, ('blk', 'grp'), route)]
    pallas_call x8 -> x9, Pallas kernels: 7.4 us -> 7.62 us  [call(): pl.pallas_call(kernel, name=name, out_shape=outs, in_specs=in_specs, out_...]
  transfers between devices with their start and end apart: 12 -> 12, of which waited for: 4 -> 4; matrix products, arithmetic and copies ran while one was open for 0% -> 0% of each run, Pallas kernels for 10% -> 11%
where the time goes in v6:
time: 62.5 us; the launch traced here: 62.1 us
  starting transfers between devices  40.6 us (65%)
  waiting for transfers between devices  11.5 us (18%)
  Pallas kernels  7.62 us (12%)
  between operations  2.13 us (3%)
    ppermute x8, starting transfers between devices, swapped(): lax.ppermute(block, 'grp', [(i, i ^ flip) for i in range(lax.axis_size('g...  31.8 us
    ppermute x2, waiting for transfers between devices, passed_along(): return lax.ppermute(block, ('blk', 'grp'), route)  9.48 us
    pallas_call x9, Pallas kernels, call(): pl.pallas_call(kernel, name=name, out_shape=outs, in_specs=in_specs, out_...  7.62 us
    ppermute x2, starting transfers between devices, passed_along(): return lax.ppermute(block, ('blk', 'grp'), route)  5.04 us
    ppermute x2, starting transfers between devices, passed_two(): lax.ppermute(block, 'blk', [(i, (i + 2) % groups) for i in range(groups)])  3.84 us
    ppermute x2, waiting for transfers between devices, passed_two(): lax.ppermute(block, 'blk', [(i, (i + 2) % groups) for i in range(groups)])  1.62 us
  transfers between devices with their start and end apart: 12, of which 4 were waited for; matrix products, arithmetic and copies ran while one was open for 0% of the time, Pallas kernels for 11%

profile of v6, /device:TPU:1, one launch (start us, length us, event | category | flops | bytes accessed | tf_op | source)
XLA Modules:
  0.0 62.1 jit_solution(15965020050106940585)
XLA Ops:
  0.6 4.0 %collective-permute-start = (bf16[128,1152]{1,0:T(8,128)(2,1)}, bf16[128,1152]{1,0:T(8,128)(2,1)S(1)}, u32[]{:S(2)}, u32[]{:S(2)}) collective-permute-start(bf16[128,1152]{1,0:T(8,128)(2,1)} %images.1), channel_id=1, source_target_pairs={{0,2},{1,3},{2,0},{3,1},{4,6},{5,7},{6,4},{7,5},{8,10},{9,11},{10,... | collective-permute-start | bytes 884744 | tf_op jit(solution)/shard_map/ppermute | solution.py:32
  4.7 3.1 %collective-permute-start.1 = (bf16[128,1152]{1,0:T(8,128)(2,1)}, bf16[128,1152]{1,0:T(8,128)(2,1)S(1)}, u32[]{:S(2)}, u32[]{:S(2)}) collective-permute-start(bf16[128,1152]{1,0:T(8,128)(2,1)} %texts.1), channel_id=1, source_target_pairs={{0,4},{1,5},{2,6},{3,7},{4,8},{5,9},{6,10},{7,11},{8,12},{9,13},{1... | collective-permute-start | bytes 884744 | tf_op jit(solution)/shard_map/ppermute | solution.py:23
  7.8 12.7 %collective-permute-start.2 = (bf16[128,1152]{1,0:T(8,128)(2,1)}, bf16[128,1152]{1,0:T(8,128)(2,1)S(1)}, u32[]{:S(2)}, u32[]{:S(2)}) collective-permute-start(bf16[128,1152]{1,0:T(8,128)(2,1)} %images.1), channel_id=1, source_target_pairs={{0,1},{1,0},{2,3},{3,2},{4,5},{5,4},{6,7},{7,6},{8,9},{9,8},{10,11... | collective-permute-start | bytes 884744 | tf_op jit(solution)/shard_map/ppermute | solution.py:32
  20.6 1.9 %collective-permute-start.4 = (bf16[128,1152]{1,0:T(8,128)(2,1)}, bf16[128,1152]{1,0:T(8,128)(2,1)S(1)}, u32[]{:S(2)}, u32[]{:S(2)}) collective-permute-start(bf16[128,1152]{1,0:T(8,128)(2,1)} %texts.1), channel_id=1, source_target_pairs={{0,8},{4,12},{8,16},{12,20},{16,24},{20,28},{24,32},{28,36},{32,40... | collective-permute-start | bytes 884744 | tf_op jit(solution)/shard_map/ppermute | solution.py:28
  22.5 1.3 %own_units.1 = (bf16[128,1152]{1,0:T(8,128)(2,1)S(1)}, bf16[128,1152]{1,0:T(8,128)(2,1)S(1)}, f32[128,128]{1,0:T(8,128)S(1)}) custom-call(bf16[128,1152]{1,0:T(8,128)(2,1)} %images.1, bf16[128,1152]{1,0:T(8,128)(2,1)} %texts.1), custom_call_target="tpu_custom_call" | custom-call | bytes 1245184 | tf_op jit(solution)/shard_map/own_units/pallas_call | solution.py:181
  25.1 0.1 maximum_bitcast_fusion
  25.2 0.1 broadcast_in_dim.8.knobs
  25.2 1.9 %collective-permute-start.3 = (bf16[128,1152]{1,0:T(8,128)(2,1)S(1)}, bf16[128,1152]{1,0:T(8,128)(2,1)S(1)}, u32[]{:S(2)}, u32[]{:S(2)}) collective-permute-start(bf16[128,1152]{1,0:T(8,128)(2,1)S(1)} %collective-permute-done.across), channel_id=1, source_target_pairs={{0,1},{1,0},{2,3},{3,2},{4,5},{5,4},{6,7},{7,6},{8,9},{9,8},{10,11... | collective-permute-start | bytes 884744 | tf_op jit(solution)/shard_map/ppermute | solution.py:32
  27.2 7.1 %collective-permute-done.1.texts = bf16[128,1152]{1,0:T(8,128)(2,1)S(1)} collective-permute-done((bf16[128,1152]{1,0:T(8,128)(2,1)}, bf16[128,1152]{1,0:T(8,128)(2,1)S(1)}, u32[]{:S(2)}, u32[]{:S(2)}) %collective-permute-start.1) | collective-permute-done | bytes 294944 | tf_op jit(solution)/shard_map/ppermute | solution.py:23
  34.2 0.1 next_units.1.unit_one
  34.4 0.0 collective-permute-done.3.diagonal
  34.4 1.1 %same_texts.1 = (bf16[512,1152]{1,0:T(8,128)(2,1)S(1)}, bf16[256,1152]{1,0:T(8,128)(2,1)S(1)}, bf16[128,512]{1,0:T(8,128)(2,1)S(1)}, f32[1,512]{1,0:T(1,128)S(1)}, bf16[128,1152]{1,0:T(8,128)(2,1)S(1)}) custom-call(f32[2,512]{1,0:T(2,128)S(1)} %broadcast_in_dim.8.knobs, bf16[128,1152]{1,0:T(8,128)(2,1)S(1)} %get-tuple-element.31.image_unit, ...), custom_call_target="tpu_custom_call" | custom-call | bytes 3971072 | tf_op jit(solution)/shard_map/same_texts/pallas_call | solution.py:181
  35.5 1.9 %collective-permute-start.10 = (bf16[128,1152]{1,0:T(8,128)(2,1)S(1)}, bf16[128,1152]{1,0:T(8,128)(2,1)S(1)}, u32[]{:S(2)}, u32[]{:S(2)}) collective-permute-start(bf16[128,1152]{1,0:T(8,128)(2,1)S(1)} %get-tuple-element.54), channel_id=1, source_target_pairs={{0,8},{4,12},{8,16},{12,20},{16,24},{20,28},{24,32},{28,36},{32,40... | collective-permute-start | bytes 884744 | tf_op jit(solution)/shard_map/ppermute | solution.py:28
  37.5 1.0 %next_texts.1 = (bf16[256,512]{1,0:T(8,128)(2,1)S(1)}, f32[1,512]{1,0:T(1,128)S(1)}, bf16[128,1152]{1,0:T(8,128)(2,1)S(1)}) custom-call(f32[2,512]{1,0:T(2,128)S(1)} %broadcast_in_dim.8.knobs, bf16[512,1152]{1,0:T(8,128)(2,1)S(1)} %get-tuple-element.34.units, bf16[256,1152]{1,0:T(8,128)(2,1)S(1)} %get-tuple-element.35.text_units, ...), custom_call_target="tpu_custom_call" | custom-call | bytes 2465792 | tf_op jit(solution)/shard_map/next_texts/pallas_call | solution.py:181
  38.5 1.9 %collective-permute-start.11 = (bf16[128,1152]{1,0:T(8,128)(2,1)S(1)}, bf16[128,1152]{1,0:T(8,128)(2,1)S(1)}, u32[]{:S(2)}, u32[]{:S(2)}) collective-permute-start(bf16[128,1152]{1,0:T(8,128)(2,1)S(1)} %get-tuple-element.55), channel_id=1, source_target_pairs={{0,4},{1,5},{2,6},{3,7},{4,8},{5,9},{6,10},{7,11},{8,12},{9,13},{1... | collective-permute-start | bytes 884744 | tf_op jit(solution)/shard_map/ppermute | solution.py:23
  40.4 1.6 %collective-permute-done.4.texts_two = bf16[128,1152]{1,0:T(8,128)(2,1)S(1)} collective-permute-done((bf16[128,1152]{1,0:T(8,128)(2,1)}, bf16[128,1152]{1,0:T(8,128)(2,1)S(1)}, u32[]{:S(2)}, u32[]{:S(2)}) %collective-permute-start.4) | collective-permute-done | bytes 294944 | tf_op jit(solution)/shard_map/ppermute | solution.py:28
  42.0 1.1 %far_texts.1 = (bf16[128,512]{1,0:T(8,128)(2,1)S(1)}, bf16[128,1152]{1,0:T(8,128)(2,1)S(1)}, f32[1,512]{1,0:T(1,128)S(1)}, bf16[64,1152]{1,0:T(8,128)(2,1)S(1)}, bf16[96,1152]{1,0:T(8,128)(2,1)S(1)}) custom-call(f32[2,512]{1,0:T(2,128)S(1)} %broadcast_in_dim.8.knobs, bf16[512,1152]{1,0:T(8,128)(2,1)S(1)} %get-tuple-element.34.units, ...), custom_call_target="tpu_custom_call" | custom-call | bytes 3129344 | tf_op jit(solution)/shard_map/far_texts/pallas_call | solution.py:181
  43.1 3.5 %collective-permute-start.6 = (bf16[96,1152]{1,0:T(8,128)(2,1)S(1)}, bf16[96,1152]{1,0:T(8,128)(2,1)S(1)}, u32[]{:S(2)}, u32[]{:S(2)}) collective-permute-start(bf16[96,1152]{1,0:T(8,128)(2,1)S(1)} %get-tuple-element.45), channel_id=1, source_target_pairs={{0,1},{1,0},{2,3},{3,2},{4,5},{5,4},{6,7},{7,6},{8,9},{9,8},{10,11... | collective-permute-start | bytes 663560 | tf_op jit(solution)/shard_map/ppermute | solution.py:32
  46.6 1.9 %collective-permute-start.5 = (bf16[64,1152]{1,0:T(8,128)(2,1)S(1)}, bf16[64,1152]{1,0:T(8,128)(2,1)S(1)}, u32[]{:S(2)}, u32[]{:S(2)}) collective-permute-start(bf16[64,1152]{1,0:T(8,128)(2,1)S(1)} %get-tuple-element.44), channel_id=1, source_target_pairs={{0,1},{1,0},{2,3},{3,2},{4,5},{5,4},{6,7},{7,6},{8,9},{9,8},{10,11... | collective-permute-start | bytes 442376 | tf_op jit(solution)/shard_map/ppermute | solution.py:32
  48.5 0.9 %image_parts.1 = (bf16[128,1152]{1,0:T(8,128)(2,1)S(1)}, f32[2,128,1152]{2,1,0:T(8,128)S(1)}, f32[128,1152]{1,0:T(8,128)S(1)}) custom-call(bf16[512,1152]{1,0:T(8,128)(2,1)S(1)} %get-tuple-element.34.units, bf16[256,1152]{1,0:T(8,128)(2,1)S(1)} %get-tuple-element.35.text_units, bf16[256,512]{1,0:T(8,128)(2,1)S(1)} %get-tuple-element.38.coefs, ...), custom_call_target="tpu_custom_call" | custom-call | bytes 4521984 | tf_op jit(solution)/shard_map/image_parts/pallas_call | solution.py:181
  49.5 0.4 collective-permute-done.5.from_top
  49.9 0.1 chip_sum.1
  50.0 1.9 %collective-permute-start.7 = (bf16[128,1152]{1,0:T(8,128)(2,1)S(1)}, bf16[128,1152]{1,0:T(8,128)(2,1)S(1)}, u32[]{:S(2)}, u32[]{:S(2)}) collective-permute-start(bf16[128,1152]{1,0:T(8,128)(2,1)S(1)} %get-tuple-element.48), channel_id=1, source_target_pairs={{0,2},{1,3},{2,0},{3,1},{4,6},{5,7},{6,4},{7,5},{8,10},{9,11},{10,... | collective-permute-start | bytes 884744 | tf_op jit(solution)/shard_map/ppermute | solution.py:32
  51.9 2.1 %collective-permute-start.8 = (bf16[128,1152]{1,0:T(8,128)(2,1)S(1)}, bf16[128,1152]{1,0:T(8,128)(2,1)S(1)}, u32[]{:S(2)}, u32[]{:S(2)}) collective-permute-start(bf16[128,1152]{1,0:T(8,128)(2,1)S(1)} %get-tuple-element.49), channel_id=1, source_target_pairs={{0,1},{1,0},{2,3},{3,2},{4,5},{5,4},{6,7},{7,6},{8,9},{9,8},{10,11... | collective-permute-start | bytes 884744 | tf_op jit(solution)/shard_map/ppermute | solution.py:32
  53.9 3.7 %collective-permute-start.9 = (f32[1,128]{1,0:T(1,128)S(1)}, f32[1,128]{1,0:T(1,128)S(1)}, u32[]{:S(2)}, u32[]{:S(2)}) collective-permute-start(f32[1,128]{1,0:T(1,128)S(1)} %get-tuple-element.50), channel_id=1, source_target_pairs={{0,2},{1,3},{2,0},{3,1},{4,6},{5,7},{6,4},{7,5},{8,10},{9,11},{10,... | collective-permute-start | bytes 1544 | tf_op jit(solution)/shard_map/ppermute | solution.py:32
  57.6 0.0 collective-permute-done.10.part_zero
  57.6 2.4 %collective-permute-done.11.part_one = bf16[128,1152]{1,0:T(8,128)(2,1)S(1)} collective-permute-done((bf16[128,1152]{1,0:T(8,128)(2,1)S(1)}, bf16[128,1152]{1,0:T(8,128)(2,1)S(1)}, u32[]{:S(2)}, u32[]{:S(2)}) %collective-permute-start.11) | collective-permute-done | bytes 294944 | tf_op jit(solution)/shard_map/ppermute | solution.py:23
  60.0 0.9 %text_sum.1 = f32[128,1152]{1,0:T(8,128)} custom-call(bf16[128,1152]{1,0:T(8,128)(2,1)S(1)} %collective-permute-done.10.part_zero, bf16[128,1152]{1,0:T(8,128)(2,1)S(1)} %collective-permute-done.11.part_one, f32[128,1152]{1,0:T(8,128)S(1)} %get-tuple-element.56.part_two), custom_call_target="tpu_custom_call" | custom-call | flops 3019898880 | bytes 1769472 | tf_op jit(solution)/shard_map/text_sum/pallas_call | solution.py:181
  61.0 0.0 collective-permute-done.9.loss_across
  61.0 0.0 collective-permute-done.7.from_across
  61.0 0.0 collective-permute-done.8.from_core
  61.0 1.1 %image_grad.1 = (f32[128,1152]{1,0:T(8,128)}, f32[1,128]{1,0:T(1,128)}) custom-call(bf16[128,1152]{1,0:T(8,128)(2,1)S(1)} %collective-permute-done.7.from_across, bf16[128,1152]{1,0:T(8,128)(2,1)S(1)} %collective-permute-done.8.from_core, f32[1,128]{1,0:T(1,128)S(1)} %collective-permute-done.9.loss_across, ...), custom_call_target="tpu_custom_call" | custom-call | bytes 3828736 | tf_op jit(solution)/shard_map/image_grad/pallas_call | solution.py:181
  (3 shorter events, 0.0 us)
Async XLA Ops:
  0.6 24.5 %collective-permute-start = (bf16[128,1152]{1,0:T(8,128)(2,1)}, bf16[128,1152]{1,0:T(8,128)(2,1)S(1)}, u32[]{:S(2)}, u32[]{:S(2)}) collective-permute-start(bf16[128,1152]{1,0:T(8,128)(2,1)} %images.1), channel_id=1, source_target_pairs={{0,2},{1,3},{2,0},{3,1},{4,6},{5,7},{6,4},{7,5},{8,10},{9,11},{10,... | collective-permute-start | bytes 884744 | tf_op jit(solution)/shard_map/ppermute | solution.py:32
  4.7 29.5 %collective-permute-start.1 = (bf16[128,1152]{1,0:T(8,128)(2,1)}, bf16[128,1152]{1,0:T(8,128)(2,1)S(1)}, u32[]{:S(2)}, u32[]{:S(2)}) collective-permute-start(bf16[128,1152]{1,0:T(8,128)(2,1)} %texts.1), channel_id=1, source_target_pairs={{0,4},{1,5},{2,6},{3,7},{4,8},{5,9},{6,10},{7,11},{8,12},{9,13},{1... | collective-permute-start | bytes 884744 | tf_op jit(solution)/shard_map/ppermute | solution.py:23
  7.8 26.6 %collective-permute-start.2 = (bf16[128,1152]{1,0:T(8,128)(2,1)}, bf16[128,1152]{1,0:T(8,128)(2,1)S(1)}, u32[]{:S(2)}, u32[]{:S(2)}) collective-permute-start(bf16[128,1152]{1,0:T(8,128)(2,1)} %images.1), channel_id=1, source_target_pairs={{0,1},{1,0},{2,3},{3,2},{4,5},{5,4},{6,7},{7,6},{8,9},{9,8},{10,11... | collective-permute-start | bytes 884744 | tf_op jit(solution)/shard_map/ppermute | solution.py:32
  20.6 21.5 %collective-permute-start.4 = (bf16[128,1152]{1,0:T(8,128)(2,1)}, bf16[128,1152]{1,0:T(8,128)(2,1)S(1)}, u32[]{:S(2)}, u32[]{:S(2)}) collective-permute-start(bf16[128,1152]{1,0:T(8,128)(2,1)} %texts.1), channel_id=1, source_target_pairs={{0,8},{4,12},{8,16},{12,20},{16,24},{20,28},{24,32},{28,36},{32,40... | collective-permute-start | bytes 884744 | tf_op jit(solution)/shard_map/ppermute | solution.py:28
  25.2 9.1 %collective-permute-start.3 = (bf16[128,1152]{1,0:T(8,128)(2,1)S(1)}, bf16[128,1152]{1,0:T(8,128)(2,1)S(1)}, u32[]{:S(2)}, u32[]{:S(2)}) collective-permute-start(bf16[128,1152]{1,0:T(8,128)(2,1)S(1)} %collective-permute-done.across), channel_id=1, source_target_pairs={{0,1},{1,0},{2,3},{3,2},{4,5},{5,4},{6,7},{7,6},{8,9},{9,8},{10,11... | collective-permute-start | bytes 884744 | tf_op jit(solution)/shard_map/ppermute | solution.py:32
  35.5 22.1 %collective-permute-start.10 = (bf16[128,1152]{1,0:T(8,128)(2,1)S(1)}, bf16[128,1152]{1,0:T(8,128)(2,1)S(1)}, u32[]{:S(2)}, u32[]{:S(2)}) collective-permute-start(bf16[128,1152]{1,0:T(8,128)(2,1)S(1)} %get-tuple-element.54), channel_id=1, source_target_pairs={{0,8},{4,12},{8,16},{12,20},{16,24},{20,28},{24,32},{28,36},{32,40... | collective-permute-start | bytes 884744 | tf_op jit(solution)/shard_map/ppermute | solution.py:28
  38.5 21.6 %collective-permute-start.11 = (bf16[128,1152]{1,0:T(8,128)(2,1)S(1)}, bf16[128,1152]{1,0:T(8,128)(2,1)S(1)}, u32[]{:S(2)}, u32[]{:S(2)}) collective-permute-start(bf16[128,1152]{1,0:T(8,128)(2,1)S(1)} %get-tuple-element.55), channel_id=1, source_target_pairs={{0,4},{1,5},{2,6},{3,7},{4,8},{5,9},{6,10},{7,11},{8,12},{9,13},{1... | collective-permute-start | bytes 884744 | tf_op jit(solution)/shard_map/ppermute | solution.py:23
  43.1 6.8 %collective-permute-start.6 = (bf16[96,1152]{1,0:T(8,128)(2,1)S(1)}, bf16[96,1152]{1,0:T(8,128)(2,1)S(1)}, u32[]{:S(2)}, u32[]{:S(2)}) collective-permute-start(bf16[96,1152]{1,0:T(8,128)(2,1)S(1)} %get-tuple-element.45), channel_id=1, source_target_pairs={{0,1},{1,0},{2,3},{3,2},{4,5},{5,4},{6,7},{7,6},{8,9},{9,8},{10,11... | collective-permute-start | bytes 663560 | tf_op jit(solution)/shard_map/ppermute | solution.py:32
  46.6 3.3 %collective-permute-start.5 = (bf16[64,1152]{1,0:T(8,128)(2,1)S(1)}, bf16[64,1152]{1,0:T(8,128)(2,1)S(1)}, u32[]{:S(2)}, u32[]{:S(2)}) collective-permute-start(bf16[64,1152]{1,0:T(8,128)(2,1)S(1)} %get-tuple-element.44), channel_id=1, source_target_pairs={{0,1},{1,0},{2,3},{3,2},{4,5},{5,4},{6,7},{7,6},{8,9},{9,8},{10,11... | collective-permute-start | bytes 442376 | tf_op jit(solution)/shard_map/ppermute | solution.py:32
  50.0 11.0 %collective-permute-start.7 = (bf16[128,1152]{1,0:T(8,128)(2,1)S(1)}, bf16[128,1152]{1,0:T(8,128)(2,1)S(1)}, u32[]{:S(2)}, u32[]{:S(2)}) collective-permute-start(bf16[128,1152]{1,0:T(8,128)(2,1)S(1)} %get-tuple-element.48), channel_id=1, source_target_pairs={{0,2},{1,3},{2,0},{3,1},{4,6},{5,7},{6,4},{7,5},{8,10},{9,11},{10,... | collective-permute-start | bytes 884744 | tf_op jit(solution)/shard_map/ppermute | solution.py:32
  51.9 9.1 %collective-permute-start.8 = (bf16[128,1152]{1,0:T(8,128)(2,1)S(1)}, bf16[128,1152]{1,0:T(8,128)(2,1)S(1)}, u32[]{:S(2)}, u32[]{:S(2)}) collective-permute-start(bf16[128,1152]{1,0:T(8,128)(2,1)S(1)} %get-tuple-element.49), channel_id=1, source_target_pairs={{0,1},{1,0},{2,3},{3,2},{4,5},{5,4},{6,7},{7,6},{8,9},{9,8},{10,11... | collective-permute-start | bytes 884744 | tf_op jit(solution)/shard_map/ppermute | solution.py:32
  53.9 7.0 %collective-permute-start.9 = (f32[1,128]{1,0:T(1,128)S(1)}, f32[1,128]{1,0:T(1,128)S(1)}, u32[]{:S(2)}, u32[]{:S(2)}) collective-permute-start(f32[1,128]{1,0:T(1,128)S(1)} %get-tuple-element.50), channel_id=1, source_target_pairs={{0,2},{1,3},{2,0},{3,1},{4,6},{5,7},{6,4},{7,5},{8,10},{9,11},{10,... | collective-permute-start | bytes 1544 | tf_op jit(solution)/shard_map/ppermute | solution.py:32

commit v7 on v6

--- a/solution.py
+++ b/solution.py
@@ -160,7 +160,7 @@
     loss_across[...] = losses[:, 2 * rows : 3 * rows] + decoded_loss(from_low[half : half + LOSS_ROWS, :], rows)
 
 
-def last_kernel(from_across, from_core, loss_across, from_low, units, inverses, kept, losses, image_grad, row_loss):
+def last_kernel(from_across, from_core, loss_across, from_low, units, inverses, kept, losses, text_total, image_grad, row_loss, text_grad):
     rows = image_grad.shape[0]
     grad = kept[0] + from_core[...].astype(F32) + from_across[...].astype(F32)
     wide = units[:rows, :].astype(F32)
@@ -168,10 +168,11 @@
     image_grad[...] = inverses[:, 0:1] * (grad - wide * along)
     loss = losses[:, :rows] + loss_across[...] + decoded_loss(from_low[rows // 2 + LOSS_ROWS :, :], rows)
     row_loss[...] = loss / (STEPS * 4 * rows)
-
-
-def text_kernel(part_zero, part_one, part_two, text_grad):
-    text_grad[...] = part_two[...] + part_one[...].astype(F32) + part_zero[...].astype(F32)
+    text_grad[...] = text_total[...]
+
+
+def text_kernel(part_zero, part_one, part_two, text_total):
+    text_total[...] = part_two[...] + part_one[...].astype(F32) + part_zero[...].astype(F32)
 
 
 def call(kernel, name, outs, arguments, far=0, flops=0, scratch=()):
@@ -269,12 +270,12 @@
     from_across = swapped(to_across, 2)
     from_core_near = swapped(to_core_near, 1)
     loss_across = swapped(loss_across, 2)
-    (text_grad,) = call(text_kernel, "text_sum", (made((rows, width), F32),), (part_zero, part_one, part_two), 0, 20 * matmul)
-    image_grad, row_loss = call(
+    (text_total,) = call(text_kernel, "text_sum", (made((rows, width), F32),), (part_zero, part_one, part_two), 0, 20 * matmul)
+    image_grad, row_loss, text_grad = call(
         last_kernel,
         "image_grad",
-        (made((rows, width), F32), made((1, rows), F32)),
-        (from_across, from_core_near, loss_across, from_core_low, units, inverses, kept, losses),
+        (made((rows, width), F32), made((1, rows), F32), made((rows, width), F32)),
+        (from_across, from_core_near, loss_across, from_core_low, units, inverses, kept, losses, text_total),
     )
     return (row_loss.reshape(rows), image_grad, text_grad)
 

time: 62.5 us -> 62 us (level)
  Pallas kernels: 7.62 us -> 6.91 us
    pallas_call x9, Pallas kernels: 7.62 us -> 6.91 us  [call(): pl.pallas_call(kernel, name=name, out_shape=outs, in_specs=in_specs, out_...]
  transfers between devices with their start and end apart: 12 -> 12, of which waited for: 4 -> 5; matrix products, arithmetic and copies ran while one was open for 0% -> 0% of each run, Pallas kernels for 11% -> 9%
where the time goes in v7:
time: 62 us; the launch traced here: 61.5 us
  starting transfers between devices  40.6 us (65%)
  waiting for transfers between devices  11.7 us (19%)
  Pallas kernels  6.91 us (11%)
  between operations  2.13 us (3%)
    ppermute x8, starting transfers between devices, swapped(): lax.ppermute(block, 'grp', [(i, i ^ flip) for i in range(lax.axis_size('g...  31.8 us
    ppermute x2, waiting for transfers between devices, passed_along(): return lax.ppermute(block, ('blk', 'grp'), route)  9.49 us
    pallas_call x9, Pallas kernels, call(): pl.pallas_call(kernel, name=name, out_shape=outs, in_specs=in_specs, out_...  6.91 us
    ppermute x2, starting transfers between devices, passed_along(): return lax.ppermute(block, ('blk', 'grp'), route)  5.04 us
    ppermute x2, starting transfers between devices, passed_two(): lax.ppermute(block, 'blk', [(i, (i + 2) % groups) for i in range(groups)])  3.84 us
    ppermute x2, waiting for transfers between devices, passed_two(): lax.ppermute(block, 'blk', [(i, (i + 2) % groups) for i in range(groups)])  1.62 us
  transfers between devices with their start and end apart: 12, of which 5 were waited for; matrix products, arithmetic and copies ran while one was open for 0% of the time, Pallas kernels for 9%

profile of v7, /device:TPU:1, one launch (start us, length us, event | category | flops | bytes accessed | tf_op | source)
XLA Modules:
  0.0 61.5 jit_solution(11202805984269468387)
XLA Ops:
  0.6 4.0 %collective-permute-start = (bf16[128,1152]{1,0:T(8,128)(2,1)}, bf16[128,1152]{1,0:T(8,128)(2,1)S(1)}, u32[]{:S(2)}, u32[]{:S(2)}) collective-permute-start(bf16[128,1152]{1,0:T(8,128)(2,1)} %images.1), channel_id=1, source_target_pairs={{0,2},{1,3},{2,0},{3,1},{4,6},{5,7},{6,4},{7,5},{8,10},{9,11},{10,... | collective-permute-start | bytes 884744 | tf_op jit(solution)/shard_map/ppermute | solution.py:32
  4.7 3.1 %collective-permute-start.1 = (bf16[128,1152]{1,0:T(8,128)(2,1)}, bf16[128,1152]{1,0:T(8,128)(2,1)S(1)}, u32[]{:S(2)}, u32[]{:S(2)}) collective-permute-start(bf16[128,1152]{1,0:T(8,128)(2,1)} %texts.1), channel_id=1, source_target_pairs={{0,4},{1,5},{2,6},{3,7},{4,8},{5,9},{6,10},{7,11},{8,12},{9,13},{1... | collective-permute-start | bytes 884744 | tf_op jit(solution)/shard_map/ppermute | solution.py:23
  7.8 12.7 %collective-permute-start.2 = (bf16[128,1152]{1,0:T(8,128)(2,1)}, bf16[128,1152]{1,0:T(8,128)(2,1)S(1)}, u32[]{:S(2)}, u32[]{:S(2)}) collective-permute-start(bf16[128,1152]{1,0:T(8,128)(2,1)} %images.1), channel_id=1, source_target_pairs={{0,1},{1,0},{2,3},{3,2},{4,5},{5,4},{6,7},{7,6},{8,9},{9,8},{10,11... | collective-permute-start | bytes 884744 | tf_op jit(solution)/shard_map/ppermute | solution.py:32
  20.6 1.9 %collective-permute-start.4 = (bf16[128,1152]{1,0:T(8,128)(2,1)}, bf16[128,1152]{1,0:T(8,128)(2,1)S(1)}, u32[]{:S(2)}, u32[]{:S(2)}) collective-permute-start(bf16[128,1152]{1,0:T(8,128)(2,1)} %texts.1), channel_id=1, source_target_pairs={{0,8},{4,12},{8,16},{12,20},{16,24},{20,28},{24,32},{28,36},{32,40... | collective-permute-start | bytes 884744 | tf_op jit(solution)/shard_map/ppermute | solution.py:28
  22.5 1.3 %own_units.1 = (bf16[128,1152]{1,0:T(8,128)(2,1)S(1)}, bf16[128,1152]{1,0:T(8,128)(2,1)S(1)}, f32[128,128]{1,0:T(8,128)S(1)}) custom-call(bf16[128,1152]{1,0:T(8,128)(2,1)} %images.1, bf16[128,1152]{1,0:T(8,128)(2,1)} %texts.1), custom_call_target="tpu_custom_call" | custom-call | bytes 1245184 | tf_op jit(solution)/shard_map/own_units/pallas_call | solution.py:182
  25.1 0.1 maximum_bitcast_fusion
  25.2 0.0 collective-permute-done.across
  25.2 0.1 broadcast_in_dim.8.knobs
  25.2 1.9 %collective-permute-start.3 = (bf16[128,1152]{1,0:T(8,128)(2,1)S(1)}, bf16[128,1152]{1,0:T(8,128)(2,1)S(1)}, u32[]{:S(2)}, u32[]{:S(2)}) collective-permute-start(bf16[128,1152]{1,0:T(8,128)(2,1)S(1)} %collective-permute-done.across), channel_id=1, source_target_pairs={{0,1},{1,0},{2,3},{3,2},{4,5},{5,4},{6,7},{7,6},{8,9},{9,8},{10,11... | collective-permute-start | bytes 884744 | tf_op jit(solution)/shard_map/ppermute | solution.py:32
  27.2 7.1 %collective-permute-done.1.texts = bf16[128,1152]{1,0:T(8,128)(2,1)S(1)} collective-permute-done((bf16[128,1152]{1,0:T(8,128)(2,1)}, bf16[128,1152]{1,0:T(8,128)(2,1)S(1)}, u32[]{:S(2)}, u32[]{:S(2)}) %collective-permute-start.1) | collective-permute-done | bytes 294944 | tf_op jit(solution)/shard_map/ppermute | solution.py:23
  34.2 0.1 next_units.1.unit_one
  34.4 0.0 collective-permute-done.2.core
  34.4 0.0 collective-permute-done.3.diagonal
  34.4 1.1 %same_texts.1 = (bf16[512,1152]{1,0:T(8,128)(2,1)S(1)}, bf16[256,1152]{1,0:T(8,128)(2,1)S(1)}, bf16[128,512]{1,0:T(8,128)(2,1)S(1)}, f32[1,512]{1,0:T(1,128)S(1)}, bf16[128,1152]{1,0:T(8,128)(2,1)S(1)}) custom-call(f32[2,512]{1,0:T(2,128)S(1)} %broadcast_in_dim.8.knobs, bf16[128,1152]{1,0:T(8,128)(2,1)S(1)} %get-tuple-element.32.image_unit, ...), custom_call_target="tpu_custom_call" | custom-call | bytes 3971072 | tf_op jit(solution)/shard_map/same_texts/pallas_call | solution.py:182
  35.5 1.9 %collective-permute-start.10 = (bf16[128,1152]{1,0:T(8,128)(2,1)S(1)}, bf16[128,1152]{1,0:T(8,128)(2,1)S(1)}, u32[]{:S(2)}, u32[]{:S(2)}) collective-permute-start(bf16[128,1152]{1,0:T(8,128)(2,1)S(1)} %get-tuple-element.53), channel_id=1, source_target_pairs={{0,8},{4,12},{8,16},{12,20},{16,24},{20,28},{24,32},{28,36},{32,40... | collective-permute-start | bytes 884744 | tf_op jit(solution)/shard_map/ppermute | solution.py:28
  37.5 1.0 %next_texts.1 = (bf16[256,512]{1,0:T(8,128)(2,1)S(1)}, f32[1,512]{1,0:T(1,128)S(1)}, bf16[128,1152]{1,0:T(8,128)(2,1)S(1)}) custom-call(f32[2,512]{1,0:T(2,128)S(1)} %broadcast_in_dim.8.knobs, bf16[512,1152]{1,0:T(8,128)(2,1)S(1)} %get-tuple-element.35.units, bf16[256,1152]{1,0:T(8,128)(2,1)S(1)} %get-tuple-element.36.text_units, ...), custom_call_target="tpu_custom_call" | custom-call | bytes 2465792 | tf_op jit(solution)/shard_map/next_texts/pallas_call | solution.py:182
  38.5 1.9 %collective-permute-start.11 = (bf16[128,1152]{1,0:T(8,128)(2,1)S(1)}, bf16[128,1152]{1,0:T(8,128)(2,1)S(1)}, u32[]{:S(2)}, u32[]{:S(2)}) collective-permute-start(bf16[128,1152]{1,0:T(8,128)(2,1)S(1)} %get-tuple-element.54), channel_id=1, source_target_pairs={{0,4},{1,5},{2,6},{3,7},{4,8},{5,9},{6,10},{7,11},{8,12},{9,13},{1... | collective-permute-start | bytes 884744 | tf_op jit(solution)/shard_map/ppermute | solution.py:23
  40.4 1.6 %collective-permute-done.4.texts_two = bf16[128,1152]{1,0:T(8,128)(2,1)S(1)} collective-permute-done((bf16[128,1152]{1,0:T(8,128)(2,1)}, bf16[128,1152]{1,0:T(8,128)(2,1)S(1)}, u32[]{:S(2)}, u32[]{:S(2)}) %collective-permute-start.4) | collective-permute-done | bytes 294944 | tf_op jit(solution)/shard_map/ppermute | solution.py:28
  42.0 1.1 %far_texts.1 = (bf16[128,512]{1,0:T(8,128)(2,1)S(1)}, bf16[128,1152]{1,0:T(8,128)(2,1)S(1)}, f32[1,512]{1,0:T(1,128)S(1)}, bf16[64,1152]{1,0:T(8,128)(2,1)S(1)}, bf16[96,1152]{1,0:T(8,128)(2,1)S(1)}) custom-call(f32[2,512]{1,0:T(2,128)S(1)} %broadcast_in_dim.8.knobs, bf16[512,1152]{1,0:T(8,128)(2,1)S(1)} %get-tuple-element.35.units, ...), custom_call_target="tpu_custom_call" | custom-call | bytes 3129344 | tf_op jit(solution)/shard_map/far_texts/pallas_call | solution.py:182
  43.1 3.5 %collective-permute-start.6 = (bf16[96,1152]{1,0:T(8,128)(2,1)S(1)}, bf16[96,1152]{1,0:T(8,128)(2,1)S(1)}, u32[]{:S(2)}, u32[]{:S(2)}) collective-permute-start(bf16[96,1152]{1,0:T(8,128)(2,1)S(1)} %get-tuple-element.46), channel_id=1, source_target_pairs={{0,1},{1,0},{2,3},{3,2},{4,5},{5,4},{6,7},{7,6},{8,9},{9,8},{10,11... | collective-permute-start | bytes 663560 | tf_op jit(solution)/shard_map/ppermute | solution.py:32
  46.6 1.9 %collective-permute-start.5 = (bf16[64,1152]{1,0:T(8,128)(2,1)S(1)}, bf16[64,1152]{1,0:T(8,128)(2,1)S(1)}, u32[]{:S(2)}, u32[]{:S(2)}) collective-permute-start(bf16[64,1152]{1,0:T(8,128)(2,1)S(1)} %get-tuple-element.45), channel_id=1, source_target_pairs={{0,1},{1,0},{2,3},{3,2},{4,5},{5,4},{6,7},{7,6},{8,9},{9,8},{10,11... | collective-permute-start | bytes 442376 | tf_op jit(solution)/shard_map/ppermute | solution.py:32
  48.5 0.9 %image_parts.1 = (bf16[128,1152]{1,0:T(8,128)(2,1)S(1)}, f32[2,128,1152]{2,1,0:T(8,128)S(1)}, f32[128,1152]{1,0:T(8,128)S(1)}) custom-call(bf16[512,1152]{1,0:T(8,128)(2,1)S(1)} %get-tuple-element.35.units, bf16[256,1152]{1,0:T(8,128)(2,1)S(1)} %get-tuple-element.36.text_units, bf16[256,512]{1,0:T(8,128)(2,1)S(1)} %get-tuple-element.39.coefs, ...), custom_call_target="tpu_custom_call" | custom-call | bytes 4521984 | tf_op jit(solution)/shard_map/image_parts/pallas_call | solution.py:182
  49.5 0.4 collective-permute-done.5.from_top
  49.9 0.1 chip_sum.1
  49.9 1.9 %collective-permute-start.7 = (bf16[128,1152]{1,0:T(8,128)(2,1)S(1)}, bf16[128,1152]{1,0:T(8,128)(2,1)S(1)}, u32[]{:S(2)}, u32[]{:S(2)}) collective-permute-start(bf16[128,1152]{1,0:T(8,128)(2,1)S(1)} %get-tuple-element.49), channel_id=1, source_target_pairs={{0,2},{1,3},{2,0},{3,1},{4,6},{5,7},{6,4},{7,5},{8,10},{9,11},{10,... | collective-permute-start | bytes 884744 | tf_op jit(solution)/shard_map/ppermute | solution.py:32
  51.9 2.1 %collective-permute-start.8 = (bf16[128,1152]{1,0:T(8,128)(2,1)S(1)}, bf16[128,1152]{1,0:T(8,128)(2,1)S(1)}, u32[]{:S(2)}, u32[]{:S(2)}) collective-permute-start(bf16[128,1152]{1,0:T(8,128)(2,1)S(1)} %get-tuple-element.50), channel_id=1, source_target_pairs={{0,1},{1,0},{2,3},{3,2},{4,5},{5,4},{6,7},{7,6},{8,9},{9,8},{10,11... | collective-permute-start | bytes 884744 | tf_op jit(solution)/shard_map/ppermute | solution.py:32
  53.9 3.7 %collective-permute-start.9 = (f32[1,128]{1,0:T(1,128)S(1)}, f32[1,128]{1,0:T(1,128)S(1)}, u32[]{:S(2)}, u32[]{:S(2)}) collective-permute-start(f32[1,128]{1,0:T(1,128)S(1)} %get-tuple-element.51), channel_id=1, source_target_pairs={{0,2},{1,3},{2,0},{3,1},{4,6},{5,7},{6,4},{7,5},{8,10},{9,11},{10,... | collective-permute-start | bytes 1544 | tf_op jit(solution)/shard_map/ppermute | solution.py:32
  57.6 0.0 collective-permute-done.10.part_zero
  57.6 2.4 %collective-permute-done.11.part_one = bf16[128,1152]{1,0:T(8,128)(2,1)S(1)} collective-permute-done((bf16[128,1152]{1,0:T(8,128)(2,1)S(1)}, bf16[128,1152]{1,0:T(8,128)(2,1)S(1)}, u32[]{:S(2)}, u32[]{:S(2)}) %collective-permute-start.11) | collective-permute-done | bytes 294944 | tf_op jit(solution)/shard_map/ppermute | solution.py:23
  60.0 0.1 text_sum.1.text_total
  60.1 0.2 collective-permute-done.9.loss_across
  60.3 1.2 %image_grad.1 = (f32[128,1152]{1,0:T(8,128)}, f32[1,128]{1,0:T(1,128)}, f32[128,1152]{1,0:T(8,128)}) custom-call(bf16[128,1152]{1,0:T(8,128)(2,1)S(1)} %collective-permute-done.7.from_across, bf16[128,1152]{1,0:T(8,128)(2,1)S(1)} %collective-permute-done.8.from_core, f32[1,128]{1,0:T(1,128)S(1)} %collective-permute-done.9.loss_across, ...), custom_call_target="tpu_custom_call" | custom-call | bytes 5008384 | tf_op jit(solution)/shard_map/image_grad/pallas_call | solution.py:182
  (3 shorter events, 0.0 us)
Async XLA Ops:
  0.6 24.5 %collective-permute-start = (bf16[128,1152]{1,0:T(8,128)(2,1)}, bf16[128,1152]{1,0:T(8,128)(2,1)S(1)}, u32[]{:S(2)}, u32[]{:S(2)}) collective-permute-start(bf16[128,1152]{1,0:T(8,128)(2,1)} %images.1), channel_id=1, source_target_pairs={{0,2},{1,3},{2,0},{3,1},{4,6},{5,7},{6,4},{7,5},{8,10},{9,11},{10,... | collective-permute-start | bytes 884744 | tf_op jit(solution)/shard_map/ppermute | solution.py:32
  4.7 29.5 %collective-permute-start.1 = (bf16[128,1152]{1,0:T(8,128)(2,1)}, bf16[128,1152]{1,0:T(8,128)(2,1)S(1)}, u32[]{:S(2)}, u32[]{:S(2)}) collective-permute-start(bf16[128,1152]{1,0:T(8,128)(2,1)} %texts.1), channel_id=1, source_target_pairs={{0,4},{1,5},{2,6},{3,7},{4,8},{5,9},{6,10},{7,11},{8,12},{9,13},{1... | collective-permute-start | bytes 884744 | tf_op jit(solution)/shard_map/ppermute | solution.py:23
  7.8 26.6 %collective-permute-start.2 = (bf16[128,1152]{1,0:T(8,128)(2,1)}, bf16[128,1152]{1,0:T(8,128)(2,1)S(1)}, u32[]{:S(2)}, u32[]{:S(2)}) collective-permute-start(bf16[128,1152]{1,0:T(8,128)(2,1)} %images.1), channel_id=1, source_target_pairs={{0,1},{1,0},{2,3},{3,2},{4,5},{5,4},{6,7},{7,6},{8,9},{9,8},{10,11... | collective-permute-start | bytes 884744 | tf_op jit(solution)/shard_map/ppermute | solution.py:32
  20.6 21.5 %collective-permute-start.4 = (bf16[128,1152]{1,0:T(8,128)(2,1)}, bf16[128,1152]{1,0:T(8,128)(2,1)S(1)}, u32[]{:S(2)}, u32[]{:S(2)}) collective-permute-start(bf16[128,1152]{1,0:T(8,128)(2,1)} %texts.1), channel_id=1, source_target_pairs={{0,8},{4,12},{8,16},{12,20},{16,24},{20,28},{24,32},{28,36},{32,40... | collective-permute-start | bytes 884744 | tf_op jit(solution)/shard_map/ppermute | solution.py:28
  25.2 9.1 %collective-permute-start.3 = (bf16[128,1152]{1,0:T(8,128)(2,1)S(1)}, bf16[128,1152]{1,0:T(8,128)(2,1)S(1)}, u32[]{:S(2)}, u32[]{:S(2)}) collective-permute-start(bf16[128,1152]{1,0:T(8,128)(2,1)S(1)} %collective-permute-done.across), channel_id=1, source_target_pairs={{0,1},{1,0},{2,3},{3,2},{4,5},{5,4},{6,7},{7,6},{8,9},{9,8},{10,11... | collective-permute-start | bytes 884744 | tf_op jit(solution)/shard_map/ppermute | solution.py:32
  35.5 22.1 %collective-permute-start.10 = (bf16[128,1152]{1,0:T(8,128)(2,1)S(1)}, bf16[128,1152]{1,0:T(8,128)(2,1)S(1)}, u32[]{:S(2)}, u32[]{:S(2)}) collective-permute-start(bf16[128,1152]{1,0:T(8,128)(2,1)S(1)} %get-tuple-element.53), channel_id=1, source_target_pairs={{0,8},{4,12},{8,16},{12,20},{16,24},{20,28},{24,32},{28,36},{32,40... | collective-permute-start | bytes 884744 | tf_op jit(solution)/shard_map/ppermute | solution.py:28
  38.5 21.6 %collective-permute-start.11 = (bf16[128,1152]{1,0:T(8,128)(2,1)S(1)}, bf16[128,1152]{1,0:T(8,128)(2,1)S(1)}, u32[]{:S(2)}, u32[]{:S(2)}) collective-permute-start(bf16[128,1152]{1,0:T(8,128)(2,1)S(1)} %get-tuple-element.54), channel_id=1, source_target_pairs={{0,4},{1,5},{2,6},{3,7},{4,8},{5,9},{6,10},{7,11},{8,12},{9,13},{1... | collective-permute-start | bytes 884744 | tf_op jit(solution)/shard_map/ppermute | solution.py:23
  43.1 6.8 %collective-permute-start.6 = (bf16[96,1152]{1,0:T(8,128)(2,1)S(1)}, bf16[96,1152]{1,0:T(8,128)(2,1)S(1)}, u32[]{:S(2)}, u32[]{:S(2)}) collective-permute-start(bf16[96,1152]{1,0:T(8,128)(2,1)S(1)} %get-tuple-element.46), channel_id=1, source_target_pairs={{0,1},{1,0},{2,3},{3,2},{4,5},{5,4},{6,7},{7,6},{8,9},{9,8},{10,11... | collective-permute-start | bytes 663560 | tf_op jit(solution)/shard_map/ppermute | solution.py:32
  46.6 3.3 %collective-permute-start.5 = (bf16[64,1152]{1,0:T(8,128)(2,1)S(1)}, bf16[64,1152]{1,0:T(8,128)(2,1)S(1)}, u32[]{:S(2)}, u32[]{:S(2)}) collective-permute-start(bf16[64,1152]{1,0:T(8,128)(2,1)S(1)} %get-tuple-element.45), channel_id=1, source_target_pairs={{0,1},{1,0},{2,3},{3,2},{4,5},{5,4},{6,7},{7,6},{8,9},{9,8},{10,11... | collective-permute-start | bytes 442376 | tf_op jit(solution)/shard_map/ppermute | solution.py:32
  49.9 10.4 %collective-permute-start.7 = (bf16[128,1152]{1,0:T(8,128)(2,1)S(1)}, bf16[128,1152]{1,0:T(8,128)(2,1)S(1)}, u32[]{:S(2)}, u32[]{:S(2)}) collective-permute-start(bf16[128,1152]{1,0:T(8,128)(2,1)S(1)} %get-tuple-element.49), channel_id=1, source_target_pairs={{0,2},{1,3},{2,0},{3,1},{4,6},{5,7},{6,4},{7,5},{8,10},{9,11},{10,... | collective-permute-start | bytes 884744 | tf_op jit(solution)/shard_map/ppermute | solution.py:32
  51.9 8.4 %collective-permute-start.8 = (bf16[128,1152]{1,0:T(8,128)(2,1)S(1)}, bf16[128,1152]{1,0:T(8,128)(2,1)S(1)}, u32[]{:S(2)}, u32[]{:S(2)}) collective-permute-start(bf16[128,1152]{1,0:T(8,128)(2,1)S(1)} %get-tuple-element.50), channel_id=1, source_target_pairs={{0,1},{1,0},{2,3},{3,2},{4,5},{5,4},{6,7},{7,6},{8,9},{9,8},{10,11... | collective-permute-start | bytes 884744 | tf_op jit(solution)/shard_map/ppermute | solution.py:32
  53.9 6.4 %collective-permute-start.9 = (f32[1,128]{1,0:T(1,128)S(1)}, f32[1,128]{1,0:T(1,128)S(1)}, u32[]{:S(2)}, u32[]{:S(2)}) collective-permute-start(f32[1,128]{1,0:T(1,128)S(1)} %get-tuple-element.51), channel_id=1, source_target_pairs={{0,2},{1,3},{2,0},{3,1},{4,6},{5,7},{6,4},{7,5},{8,10},{9,11},{10,... | collective-permute-start | bytes 1544 | tf_op jit(solution)/shard_map/ppermute | solution.py:32

commit v8 on v7

--- a/solution.py
+++ b/solution.py
@@ -160,22 +160,30 @@
     loss_across[...] = losses[:, 2 * rows : 3 * rows] + decoded_loss(from_low[half : half + LOSS_ROWS, :], rows)
 
 
-def last_kernel(from_across, from_core, loss_across, from_low, units, inverses, kept, losses, text_total, image_grad, row_loss, text_grad):
-    rows = image_grad.shape[0]
-    grad = kept[0] + from_core[...].astype(F32) + from_across[...].astype(F32)
-    wide = units[:rows, :].astype(F32)
-    along = jnp.sum(wide * grad, axis=1, keepdims=True)
-    image_grad[...] = inverses[:, 0:1] * (grad - wide * along)
+def last_kernel(from_across, from_core, loss_across, from_low, units, inverses, kept, losses, text_total, image_grad, row_loss, text_grad, held, sems):
+    rows = held.shape[0]
+    half = rows // 2
+    copies = [pltpu.make_async_copy(text_total, text_grad, sems.at[0])]
+    copies[0].start()
+    for i in range(2):
+        part = slice(i * half, (i + 1) * half)
+        grad = kept[0, part] + from_core[part, :].astype(F32) + from_across[part, :].astype(F32)
+        wide = units[part, :].astype(F32)
+        along = jnp.sum(wide * grad, axis=1, keepdims=True)
+        held[part, :] = inverses[part, 0:1] * (grad - wide * along)
+        copies.append(pltpu.make_async_copy(held.at[part], image_grad.at[part], sems.at[i + 1]))
+        copies[-1].start()
     loss = losses[:, :rows] + loss_across[...] + decoded_loss(from_low[rows // 2 + LOSS_ROWS :, :], rows)
     row_loss[...] = loss / (STEPS * 4 * rows)
-    text_grad[...] = text_total[...]
+    for copy in copies:
+        copy.wait()
 
 
 def text_kernel(part_zero, part_one, part_two, text_total):
     text_total[...] = part_two[...] + part_one[...].astype(F32) + part_zero[...].astype(F32)
 
 
-def call(kernel, name, outs, arguments, far=0, flops=0, scratch=()):
+def call(kernel, name, outs, arguments, far=0, flops=0, scratch=(), spaces=None):
     in_specs = [pl.BlockSpec(memory_space=pltpu.HBM)] * far
     in_specs += [pl.BlockSpec(memory_space=pltpu.VMEM)] * (len(arguments) - far)
     moved = sum(a.size * a.dtype.itemsize for a in (*arguments, *outs))
@@ -184,7 +192,7 @@
         name=name,
         out_shape=outs,
         in_specs=in_specs,
-        out_specs=tuple(pl.BlockSpec(memory_space=pltpu.VMEM) for _ in outs),
+        out_specs=tuple(pl.BlockSpec(memory_space=space) for space in spaces or (pltpu.VMEM,) * len(outs)),
         scratch_shapes=scratch,
         cost_estimate=pl.CostEstimate(flops=flops, bytes_accessed=moved, transcendentals=0),
         compiler_params=pltpu.CompilerParams(vmem_limit_bytes=24 * 1024 * 1024),
@@ -276,6 +284,10 @@
         "image_grad",
         (made((rows, width), F32), made((1, rows), F32), made((rows, width), F32)),
         (from_across, from_core_near, loss_across, from_core_low, units, inverses, kept, losses, text_total),
+        0,
+        0,
+        (pltpu.VMEM((rows, width), F32), pltpu.SemaphoreType.DMA((3,))),
+        (pltpu.HBM, pltpu.VMEM, pltpu.HBM),
     )
     return (row_loss.reshape(rows), image_grad, text_grad)
 

time: 62 us -> 62.4 us (level)
  no operation moved by 1% of the time
where the time goes in v8:
time: 62.4 us; the launch traced here: 61.9 us
  starting transfers between devices  40.6 us (65%)
  waiting for transfers between devices  11.7 us (19%)
  Pallas kernels  7.29 us (12%)
  between operations  2.13 us (3%)
    ppermute x8, starting transfers between devices, swapped(): lax.ppermute(block, 'grp', [(i, i ^ flip) for i in range(lax.axis_size('g...  31.8 us
    ppermute x2, waiting for transfers between devices, passed_along(): return lax.ppermute(block, ('blk', 'grp'), route)  9.49 us
    pallas_call x9, Pallas kernels, call(): pl.pallas_call(kernel, name=name, out_shape=outs, in_specs=in_specs, out_...  7.29 us
    ppermute x2, starting transfers between devices, passed_along(): return lax.ppermute(block, ('blk', 'grp'), route)  5.04 us
    ppermute x2, starting transfers between devices, passed_two(): lax.ppermute(block, 'blk', [(i, (i + 2) % groups) for i in range(groups)])  3.84 us
    ppermute x2, waiting for transfers between devices, passed_two(): lax.ppermute(block, 'blk', [(i, (i + 2) % groups) for i in range(groups)])  1.62 us
  transfers between devices with their start and end apart: 12, of which 5 were waited for; matrix products, arithmetic and copies ran while one was open for 0% of the time, Pallas kernels for 9%

profile of v8, /device:TPU:1, one launch (start us, length us, event | category | flops | bytes accessed | tf_op | source)
XLA Modules:
  0.0 61.9 jit_solution(7779987782854331844)
XLA Ops:
  0.6 4.0 %collective-permute-start = (bf16[128,1152]{1,0:T(8,128)(2,1)}, bf16[128,1152]{1,0:T(8,128)(2,1)S(1)}, u32[]{:S(2)}, u32[]{:S(2)}) collective-permute-start(bf16[128,1152]{1,0:T(8,128)(2,1)} %images.1), channel_id=1, source_target_pairs={{0,2},{1,3},{2,0},{3,1},{4,6},{5,7},{6,4},{7,5},{8,10},{9,11},{10,... | collective-permute-start | bytes 884744 | tf_op jit(solution)/shard_map/ppermute | solution.py:32
  4.7 3.1 %collective-permute-start.1 = (bf16[128,1152]{1,0:T(8,128)(2,1)}, bf16[128,1152]{1,0:T(8,128)(2,1)S(1)}, u32[]{:S(2)}, u32[]{:S(2)}) collective-permute-start(bf16[128,1152]{1,0:T(8,128)(2,1)} %texts.1), channel_id=1, source_target_pairs={{0,4},{1,5},{2,6},{3,7},{4,8},{5,9},{6,10},{7,11},{8,12},{9,13},{1... | collective-permute-start | bytes 884744 | tf_op jit(solution)/shard_map/ppermute | solution.py:23
  7.8 12.7 %collective-permute-start.2 = (bf16[128,1152]{1,0:T(8,128)(2,1)}, bf16[128,1152]{1,0:T(8,128)(2,1)S(1)}, u32[]{:S(2)}, u32[]{:S(2)}) collective-permute-start(bf16[128,1152]{1,0:T(8,128)(2,1)} %images.1), channel_id=1, source_target_pairs={{0,1},{1,0},{2,3},{3,2},{4,5},{5,4},{6,7},{7,6},{8,9},{9,8},{10,11... | collective-permute-start | bytes 884744 | tf_op jit(solution)/shard_map/ppermute | solution.py:32
  20.6 1.9 %collective-permute-start.4 = (bf16[128,1152]{1,0:T(8,128)(2,1)}, bf16[128,1152]{1,0:T(8,128)(2,1)S(1)}, u32[]{:S(2)}, u32[]{:S(2)}) collective-permute-start(bf16[128,1152]{1,0:T(8,128)(2,1)} %texts.1), channel_id=1, source_target_pairs={{0,8},{4,12},{8,16},{12,20},{16,24},{20,28},{24,32},{28,36},{32,40... | collective-permute-start | bytes 884744 | tf_op jit(solution)/shard_map/ppermute | solution.py:28
  22.5 1.3 %own_units.1 = (bf16[128,1152]{1,0:T(8,128)(2,1)S(1)}, bf16[128,1152]{1,0:T(8,128)(2,1)S(1)}, f32[128,128]{1,0:T(8,128)S(1)}) custom-call(bf16[128,1152]{1,0:T(8,128)(2,1)} %images.1, bf16[128,1152]{1,0:T(8,128)(2,1)} %texts.1), custom_call_target="tpu_custom_call" | custom-call | bytes 1245184 | tf_op jit(solution)/shard_map/own_units/pallas_call | solution.py:190
  25.1 0.1 maximum_bitcast_fusion
  25.2 0.0 collective-permute-done.across
  25.2 0.1 broadcast_in_dim.8.knobs
  25.2 1.9 %collective-permute-start.3 = (bf16[128,1152]{1,0:T(8,128)(2,1)S(1)}, bf16[128,1152]{1,0:T(8,128)(2,1)S(1)}, u32[]{:S(2)}, u32[]{:S(2)}) collective-permute-start(bf16[128,1152]{1,0:T(8,128)(2,1)S(1)} %collective-permute-done.across), channel_id=1, source_target_pairs={{0,1},{1,0},{2,3},{3,2},{4,5},{5,4},{6,7},{7,6},{8,9},{9,8},{10,11... | collective-permute-start | bytes 884744 | tf_op jit(solution)/shard_map/ppermute | solution.py:32
  27.2 7.1 %collective-permute-done.1.texts = bf16[128,1152]{1,0:T(8,128)(2,1)S(1)} collective-permute-done((bf16[128,1152]{1,0:T(8,128)(2,1)}, bf16[128,1152]{1,0:T(8,128)(2,1)S(1)}, u32[]{:S(2)}, u32[]{:S(2)}) %collective-permute-start.1) | collective-permute-done | bytes 294944 | tf_op jit(solution)/shard_map/ppermute | solution.py:23
  34.2 0.1 next_units.1.unit_one
  34.4 0.0 collective-permute-done.3.diagonal
  34.4 1.1 %same_texts.1 = (bf16[512,1152]{1,0:T(8,128)(2,1)S(1)}, bf16[256,1152]{1,0:T(8,128)(2,1)S(1)}, bf16[128,512]{1,0:T(8,128)(2,1)S(1)}, f32[1,512]{1,0:T(1,128)S(1)}, bf16[128,1152]{1,0:T(8,128)(2,1)S(1)}) custom-call(f32[2,512]{1,0:T(2,128)S(1)} %broadcast_in_dim.8.knobs, bf16[128,1152]{1,0:T(8,128)(2,1)S(1)} %get-tuple-element.32.image_unit, ...), custom_call_target="tpu_custom_call" | custom-call | bytes 3971072 | tf_op jit(solution)/shard_map/same_texts/pallas_call | solution.py:190
  35.5 1.9 %collective-permute-start.10 = (bf16[128,1152]{1,0:T(8,128)(2,1)S(1)}, bf16[128,1152]{1,0:T(8,128)(2,1)S(1)}, u32[]{:S(2)}, u32[]{:S(2)}) collective-permute-start(bf16[128,1152]{1,0:T(8,128)(2,1)S(1)} %get-tuple-element.53), channel_id=1, source_target_pairs={{0,8},{4,12},{8,16},{12,20},{16,24},{20,28},{24,32},{28,36},{32,40... | collective-permute-start | bytes 884744 | tf_op jit(solution)/shard_map/ppermute | solution.py:28
  37.5 1.0 %next_texts.1 = (bf16[256,512]{1,0:T(8,128)(2,1)S(1)}, f32[1,512]{1,0:T(1,128)S(1)}, bf16[128,1152]{1,0:T(8,128)(2,1)S(1)}) custom-call(f32[2,512]{1,0:T(2,128)S(1)} %broadcast_in_dim.8.knobs, bf16[512,1152]{1,0:T(8,128)(2,1)S(1)} %get-tuple-element.35.units, bf16[256,1152]{1,0:T(8,128)(2,1)S(1)} %get-tuple-element.36.text_units, ...), custom_call_target="tpu_custom_call" | custom-call | bytes 2465792 | tf_op jit(solution)/shard_map/next_texts/pallas_call | solution.py:190
  38.5 1.9 %collective-permute-start.11 = (bf16[128,1152]{1,0:T(8,128)(2,1)S(1)}, bf16[128,1152]{1,0:T(8,128)(2,1)S(1)}, u32[]{:S(2)}, u32[]{:S(2)}) collective-permute-start(bf16[128,1152]{1,0:T(8,128)(2,1)S(1)} %get-tuple-element.54), channel_id=1, source_target_pairs={{0,4},{1,5},{2,6},{3,7},{4,8},{5,9},{6,10},{7,11},{8,12},{9,13},{1... | collective-permute-start | bytes 884744 | tf_op jit(solution)/shard_map/ppermute | solution.py:23
  40.4 1.6 %collective-permute-done.4.texts_two = bf16[128,1152]{1,0:T(8,128)(2,1)S(1)} collective-permute-done((bf16[128,1152]{1,0:T(8,128)(2,1)}, bf16[128,1152]{1,0:T(8,128)(2,1)S(1)}, u32[]{:S(2)}, u32[]{:S(2)}) %collective-permute-start.4) | collective-permute-done | bytes 294944 | tf_op jit(solution)/shard_map/ppermute | solution.py:28
  42.0 1.1 %far_texts.1 = (bf16[128,512]{1,0:T(8,128)(2,1)S(1)}, bf16[128,1152]{1,0:T(8,128)(2,1)S(1)}, f32[1,512]{1,0:T(1,128)S(1)}, bf16[64,1152]{1,0:T(8,128)(2,1)S(1)}, bf16[96,1152]{1,0:T(8,128)(2,1)S(1)}) custom-call(f32[2,512]{1,0:T(2,128)S(1)} %broadcast_in_dim.8.knobs, bf16[512,1152]{1,0:T(8,128)(2,1)S(1)} %get-tuple-element.35.units, ...), custom_call_target="tpu_custom_call" | custom-call | bytes 3129344 | tf_op jit(solution)/shard_map/far_texts/pallas_call | solution.py:190
  43.1 3.5 %collective-permute-start.6 = (bf16[96,1152]{1,0:T(8,128)(2,1)S(1)}, bf16[96,1152]{1,0:T(8,128)(2,1)S(1)}, u32[]{:S(2)}, u32[]{:S(2)}) collective-permute-start(bf16[96,1152]{1,0:T(8,128)(2,1)S(1)} %get-tuple-element.46), channel_id=1, source_target_pairs={{0,1},{1,0},{2,3},{3,2},{4,5},{5,4},{6,7},{7,6},{8,9},{9,8},{10,11... | collective-permute-start | bytes 663560 | tf_op jit(solution)/shard_map/ppermute | solution.py:32
  46.6 1.9 %collective-permute-start.5 = (bf16[64,1152]{1,0:T(8,128)(2,1)S(1)}, bf16[64,1152]{1,0:T(8,128)(2,1)S(1)}, u32[]{:S(2)}, u32[]{:S(2)}) collective-permute-start(bf16[64,1152]{1,0:T(8,128)(2,1)S(1)} %get-tuple-element.45), channel_id=1, source_target_pairs={{0,1},{1,0},{2,3},{3,2},{4,5},{5,4},{6,7},{7,6},{8,9},{9,8},{10,11... | collective-permute-start | bytes 442376 | tf_op jit(solution)/shard_map/ppermute | solution.py:32
  48.5 0.9 %image_parts.1 = (bf16[128,1152]{1,0:T(8,128)(2,1)S(1)}, f32[2,128,1152]{2,1,0:T(8,128)S(1)}, f32[128,1152]{1,0:T(8,128)S(1)}) custom-call(bf16[512,1152]{1,0:T(8,128)(2,1)S(1)} %get-tuple-element.35.units, bf16[256,1152]{1,0:T(8,128)(2,1)S(1)} %get-tuple-element.36.text_units, bf16[256,512]{1,0:T(8,128)(2,1)S(1)} %get-tuple-element.39.coefs, ...), custom_call_target="tpu_custom_call" | custom-call | bytes 4521984 | tf_op jit(solution)/shard_map/image_parts/pallas_call | solution.py:190
  49.5 0.4 collective-permute-done.5.from_top
  49.9 0.0 collective-permute-done.6.from_low
  49.9 0.1 chip_sum.1
  49.9 1.9 %collective-permute-start.7 = (bf16[128,1152]{1,0:T(8,128)(2,1)S(1)}, bf16[128,1152]{1,0:T(8,128)(2,1)S(1)}, u32[]{:S(2)}, u32[]{:S(2)}) collective-permute-start(bf16[128,1152]{1,0:T(8,128)(2,1)S(1)} %get-tuple-element.49), channel_id=1, source_target_pairs={{0,2},{1,3},{2,0},{3,1},{4,6},{5,7},{6,4},{7,5},{8,10},{9,11},{10,... | collective-permute-start | bytes 884744 | tf_op jit(solution)/shard_map/ppermute | solution.py:32
  51.9 2.1 %collective-permute-start.8 = (bf16[128,1152]{1,0:T(8,128)(2,1)S(1)}, bf16[128,1152]{1,0:T(8,128)(2,1)S(1)}, u32[]{:S(2)}, u32[]{:S(2)}) collective-permute-start(bf16[128,1152]{1,0:T(8,128)(2,1)S(1)} %get-tuple-element.50), channel_id=1, source_target_pairs={{0,1},{1,0},{2,3},{3,2},{4,5},{5,4},{6,7},{7,6},{8,9},{9,8},{10,11... | collective-permute-start | bytes 884744 | tf_op jit(solution)/shard_map/ppermute | solution.py:32
  53.9 3.7 %collective-permute-start.9 = (f32[1,128]{1,0:T(1,128)S(1)}, f32[1,128]{1,0:T(1,128)S(1)}, u32[]{:S(2)}, u32[]{:S(2)}) collective-permute-start(f32[1,128]{1,0:T(1,128)S(1)} %get-tuple-element.51), channel_id=1, source_target_pairs={{0,2},{1,3},{2,0},{3,1},{4,6},{5,7},{6,4},{7,5},{8,10},{9,11},{10,... | collective-permute-start | bytes 1544 | tf_op jit(solution)/shard_map/ppermute | solution.py:32
  57.6 2.4 %collective-permute-done.11.part_one = bf16[128,1152]{1,0:T(8,128)(2,1)S(1)} collective-permute-done((bf16[128,1152]{1,0:T(8,128)(2,1)S(1)}, bf16[128,1152]{1,0:T(8,128)(2,1)S(1)}, u32[]{:S(2)}, u32[]{:S(2)}) %collective-permute-start.11) | collective-permute-done | bytes 294944 | tf_op jit(solution)/shard_map/ppermute | solution.py:23
  60.0 0.1 text_sum.1.text_total
  60.1 0.2 collective-permute-done.9.loss_across
  60.3 0.0 collective-permute-done.7.from_across
  60.3 1.6 %image_grad.1 = (f32[128,1152]{1,0:T(8,128)}, f32[1,128]{1,0:T(1,128)}, f32[128,1152]{1,0:T(8,128)}) custom-call(bf16[128,1152]{1,0:T(8,128)(2,1)S(1)} %collective-permute-done.7.from_across, bf16[128,1152]{1,0:T(8,128)(2,1)S(1)} %collective-permute-done.8.from_core, f32[1,128]{1,0:T(1,128)S(1)} %collective-permute-done.9.loss_across, ...), custom_call_target="tpu_custom_call" | custom-call | bytes 5008384 | tf_op jit(solution)/shard_map/image_grad/pallas_call | solution.py:190
  (3 shorter events, 0.0 us)
Async XLA Ops:
  0.6 24.5 %collective-permute-start = (bf16[128,1152]{1,0:T(8,128)(2,1)}, bf16[128,1152]{1,0:T(8,128)(2,1)S(1)}, u32[]{:S(2)}, u32[]{:S(2)}) collective-permute-start(bf16[128,1152]{1,0:T(8,128)(2,1)} %images.1), channel_id=1, source_target_pairs={{0,2},{1,3},{2,0},{3,1},{4,6},{5,7},{6,4},{7,5},{8,10},{9,11},{10,... | collective-permute-start | bytes 884744 | tf_op jit(solution)/shard_map/ppermute | solution.py:32
  4.7 29.5 %collective-permute-start.1 = (bf16[128,1152]{1,0:T(8,128)(2,1)}, bf16[128,1152]{1,0:T(8,128)(2,1)S(1)}, u32[]{:S(2)}, u32[]{:S(2)}) collective-permute-start(bf16[128,1152]{1,0:T(8,128)(2,1)} %texts.1), channel_id=1, source_target_pairs={{0,4},{1,5},{2,6},{3,7},{4,8},{5,9},{6,10},{7,11},{8,12},{9,13},{1... | collective-permute-start | bytes 884744 | tf_op jit(solution)/shard_map/ppermute | solution.py:23
  7.8 26.6 %collective-permute-start.2 = (bf16[128,1152]{1,0:T(8,128)(2,1)}, bf16[128,1152]{1,0:T(8,128)(2,1)S(1)}, u32[]{:S(2)}, u32[]{:S(2)}) collective-permute-start(bf16[128,1152]{1,0:T(8,128)(2,1)} %images.1), channel_id=1, source_target_pairs={{0,1},{1,0},{2,3},{3,2},{4,5},{5,4},{6,7},{7,6},{8,9},{9,8},{10,11... | collective-permute-start | bytes 884744 | tf_op jit(solution)/shard_map/ppermute | solution.py:32
  20.6 21.5 %collective-permute-start.4 = (bf16[128,1152]{1,0:T(8,128)(2,1)}, bf16[128,1152]{1,0:T(8,128)(2,1)S(1)}, u32[]{:S(2)}, u32[]{:S(2)}) collective-permute-start(bf16[128,1152]{1,0:T(8,128)(2,1)} %texts.1), channel_id=1, source_target_pairs={{0,8},{4,12},{8,16},{12,20},{16,24},{20,28},{24,32},{28,36},{32,40... | collective-permute-start | bytes 884744 | tf_op jit(solution)/shard_map/ppermute | solution.py:28
  25.2 9.1 %collective-permute-start.3 = (bf16[128,1152]{1,0:T(8,128)(2,1)S(1)}, bf16[128,1152]{1,0:T(8,128)(2,1)S(1)}, u32[]{:S(2)}, u32[]{:S(2)}) collective-permute-start(bf16[128,1152]{1,0:T(8,128)(2,1)S(1)} %collective-permute-done.across), channel_id=1, source_target_pairs={{0,1},{1,0},{2,3},{3,2},{4,5},{5,4},{6,7},{7,6},{8,9},{9,8},{10,11... | collective-permute-start | bytes 884744 | tf_op jit(solution)/shard_map/ppermute | solution.py:32
  35.5 22.1 %collective-permute-start.10 = (bf16[128,1152]{1,0:T(8,128)(2,1)S(1)}, bf16[128,1152]{1,0:T(8,128)(2,1)S(1)}, u32[]{:S(2)}, u32[]{:S(2)}) collective-permute-start(bf16[128,1152]{1,0:T(8,128)(2,1)S(1)} %get-tuple-element.53), channel_id=1, source_target_pairs={{0,8},{4,12},{8,16},{12,20},{16,24},{20,28},{24,32},{28,36},{32,40... | collective-permute-start | bytes 884744 | tf_op jit(solution)/shard_map/ppermute | solution.py:28
  38.5 21.6 %collective-permute-start.11 = (bf16[128,1152]{1,0:T(8,128)(2,1)S(1)}, bf16[128,1152]{1,0:T(8,128)(2,1)S(1)}, u32[]{:S(2)}, u32[]{:S(2)}) collective-permute-start(bf16[128,1152]{1,0:T(8,128)(2,1)S(1)} %get-tuple-element.54), channel_id=1, source_target_pairs={{0,4},{1,5},{2,6},{3,7},{4,8},{5,9},{6,10},{7,11},{8,12},{9,13},{1... | collective-permute-start | bytes 884744 | tf_op jit(solution)/shard_map/ppermute | solution.py:23
  43.1 6.8 %collective-permute-start.6 = (bf16[96,1152]{1,0:T(8,128)(2,1)S(1)}, bf16[96,1152]{1,0:T(8,128)(2,1)S(1)}, u32[]{:S(2)}, u32[]{:S(2)}) collective-permute-start(bf16[96,1152]{1,0:T(8,128)(2,1)S(1)} %get-tuple-element.46), channel_id=1, source_target_pairs={{0,1},{1,0},{2,3},{3,2},{4,5},{5,4},{6,7},{7,6},{8,9},{9,8},{10,11... | collective-permute-start | bytes 663560 | tf_op jit(solution)/shard_map/ppermute | solution.py:32
  46.6 3.3 %collective-permute-start.5 = (bf16[64,1152]{1,0:T(8,128)(2,1)S(1)}, bf16[64,1152]{1,0:T(8,128)(2,1)S(1)}, u32[]{:S(2)}, u32[]{:S(2)}) collective-permute-start(bf16[64,1152]{1,0:T(8,128)(2,1)S(1)} %get-tuple-element.45), channel_id=1, source_target_pairs={{0,1},{1,0},{2,3},{3,2},{4,5},{5,4},{6,7},{7,6},{8,9},{9,8},{10,11... | collective-permute-start | bytes 442376 | tf_op jit(solution)/shard_map/ppermute | solution.py:32
  49.9 10.4 %collective-permute-start.7 = (bf16[128,1152]{1,0:T(8,128)(2,1)S(1)}, bf16[128,1152]{1,0:T(8,128)(2,1)S(1)}, u32[]{:S(2)}, u32[]{:S(2)}) collective-permute-start(bf16[128,1152]{1,0:T(8,128)(2,1)S(1)} %get-tuple-element.49), channel_id=1, source_target_pairs={{0,2},{1,3},{2,0},{3,1},{4,6},{5,7},{6,4},{7,5},{8,10},{9,11},{10,... | collective-permute-start | bytes 884744 | tf_op jit(solution)/shard_map/ppermute | solution.py:32
  51.9 8.4 %collective-permute-start.8 = (bf16[128,1152]{1,0:T(8,128)(2,1)S(1)}, bf16[128,1152]{1,0:T(8,128)(2,1)S(1)}, u32[]{:S(2)}, u32[]{:S(2)}) collective-permute-start(bf16[128,1152]{1,0:T(8,128)(2,1)S(1)} %get-tuple-element.50), channel_id=1, source_target_pairs={{0,1},{1,0},{2,3},{3,2},{4,5},{5,4},{6,7},{7,6},{8,9},{9,8},{10,11... | collective-permute-start | bytes 884744 | tf_op jit(solution)/shard_map/ppermute | solution.py:32
  53.9 6.4 %collective-permute-start.9 = (f32[1,128]{1,0:T(1,128)S(1)}, f32[1,128]{1,0:T(1,128)S(1)}, u32[]{:S(2)}, u32[]{:S(2)}) collective-permute-start(f32[1,128]{1,0:T(1,128)S(1)} %get-tuple-element.51), channel_id=1, source_target_pairs={{0,2},{1,3},{2,0},{3,1},{4,6},{5,7},{6,4},{7,5},{8,10},{9,11},{10,... | collective-permute-start | bytes 1544 | tf_op jit(solution)/shard_map/ppermute | solution.py:32
